TPU v7x, 32 devices: a whole 2x2x4 slice. The times are simulated.
32 devices in a mesh: seq: 8 (over z, y), head: 4 (over x, core).
Axes of the slice: x: 2, y: 2, z: 4, core: 2. Of those that a mesh axis runs over, the one named last changes fastest.
Arguments:
- tokens: bfloat16 [8192, 2048], P('seq'), may hold values from -26 to 26, as said below
- w_query: bfloat16 [2048, 2048], P(None, 'head'), as said below
- w_key: bfloat16 [2048, 2048], P(None, 'head'), as said below
- w_value: bfloat16 [2048, 2048], P(None, 'head'), may hold values from -0.125 to 0.125
- w_out: bfloat16 [2048, 2048], P('head'), may hold values from -0.125 to 0.125
- window_blocks: int32 [64, 3], P('seq'), may hold values from 0 to 63, as said below
- random_blocks: int32 [64, 4], replicated, may hold values from 0 to 63, as said below
- summary_blocks: int32 [64, 2], P('seq'), may hold values from 0 to 3
- seg_start: int32 [512], replicated, may hold values from 0 to 8191, as said below
- seg_end: int32 [512], replicated, may hold values from 1 to 8192, as said below
Outputs:
- mixed: bfloat16 [8192, 2048], P('seq', 'head')
Inputs may be any that keep to these rules, and one draw needn't show every extreme that they name: `tokens`: finite activations. `w_query`: a projection scaled by its fan-in. `w_key`: a projection scaled by its fan-in. `window_blocks`: row i names block i first, then two other blocks at most 2 blocks away from i. `random_blocks`: in the rows of one index of seq (aligned runs of 8 rows), the blocks held by any one index of seq are named at most 6 times, and those of some index exactly 6 times. `seg_start`: each segment holds 1 to 512 tokens, segment 0 exactly 512; segment s lies within the tokens of one index of seq, namely index (s // 64 + 4) mod 8. seg_end is greater than seg_start and at most seg_start + 512.
All inputs are finite; a program needn't handle non-finite values.
Results may differ from a plain program's by a relative error of at most 0.0095.
Values may be sent and summed in bfloat16 or wider, within the bound.
No kernel may reach another device: no remote copies, remote signals or barrier semaphores. Data moves between devices by JAX's collectives and lax.ppermute only.
A program may use at most 192 MiB of HBM per device.

v0:
```python
import jax
import jax.numpy as jnp
from jax import lax
from jax.sharding import PartitionSpec as P

HD = 128
BLK = 128
WIN = 3
R = 4
FIXL = 2


def with_halo(block, sides, width):
    for axis, dim in sides:
        count = lax.axis_size(axis)
        forward = [(i, i + 1) for i in range(count - 1)]
        backward = [(target, source) for source, target in forward]
        low = lax.ppermute(
            lax.slice_in_dim(block, block.shape[dim] - width, None, axis=dim), axis, forward
        )
        high = lax.ppermute(lax.slice_in_dim(block, 0, width, axis=dim), axis, backward)
        block = jnp.concatenate([low, block, high], axis=dim)
    return block


def project(tokens, weight):
    return jnp.dot(tokens, weight, preferred_element_type=jnp.float32).astype(jnp.bfloat16)


def rank_refs(random_blocks, devices, block_count):
    ref_lists = random_blocks.reshape(devices, -1)
    owners = ref_lists // block_count
    within = ref_lists - owners * block_count
    ref_count = ref_lists.shape[1]
    same_owner = (owners[:, :, None] == owners[:, None, :]).astype(jnp.int32)
    earlier = (
        lax.iota(jnp.int32, ref_count)[None, :] < lax.iota(jnp.int32, ref_count)[:, None]
    ).astype(jnp.int32)
    ranking = jnp.sum(same_owner * earlier[None, :, :], axis=2)
    return (owners, within, ranking)


def per_device(
    tokens,
    w_query,
    w_key,
    w_value,
    w_out,
    window_blocks,
    random_blocks,
    summary_blocks,
    seg_start,
    seg_end,
):
    tok_rows = tokens.shape[0]
    columns = w_query.shape[1]
    head_count = columns // HD
    block_count = tok_rows // BLK
    devices = lax.axis_size("seq")
    my_index = lax.axis_index("seq")
    ref_count = block_count * R
    slot_count = max(2, (3 * ref_count + 2 * devices - 1) // (2 * devices))
    queries = project(tokens, w_query)
    key_rows = project(tokens, w_key)
    values = project(tokens, w_value)
    key_value = jnp.stack([key_rows, values], axis=1)
    blocks = key_value.reshape(block_count, BLK, 2, columns)
    position = my_index * tok_rows + lax.iota(jnp.int32, tok_rows)
    member = (
        (position[None, :] >= seg_start[:, None]) & (position[None, :] < seg_end[:, None])
    ).astype(jnp.bfloat16)
    partial_sums = jnp.dot(
        member, key_value.reshape(tok_rows, 2 * columns), preferred_element_type=jnp.float32
    )
    counts = (seg_end - seg_start).astype(jnp.float32)
    whole_sums = lax.psum(partial_sums, "seq")
    means = (whole_sums / counts[:, None]).astype(jnp.bfloat16)
    summary = means.reshape(-1, BLK, 2, columns)
    owners, within, ranking = rank_refs(random_blocks, devices, block_count)
    slot_ids = lax.iota(jnp.int32, slot_count)
    chosen = (
        (owners == my_index)[:, :, None] & (ranking[:, :, None] == slot_ids[None, None, :])
    ).astype(jnp.int32)
    send_index = jnp.sum(chosen * within[:, :, None], axis=1)
    outgoing = blocks[send_index]
    mine_owner = lax.dynamic_index_in_dim(owners, my_index, 0, keepdims=False)
    mine_rank = lax.dynamic_index_in_dim(ranking, my_index, 0, keepdims=False)
    arrived = lax.all_to_all(outgoing, "seq", split_axis=0, concat_axis=0, tiled=True)
    padded = with_halo(key_value, (("seq", 0),), 2 * BLK)
    nearby = padded.reshape(block_count + 4, BLK, 2, columns)
    fetched = arrived.reshape(devices * slot_count, BLK, 2, columns)
    random_index = (mine_owner * slot_count + mine_rank).reshape(block_count, R)
    window_index = window_blocks - my_index * block_count + 2
    group_size = min(4, block_count)
    group_count = block_count // group_size
    score_scale = HD ** (-0.5)

    def attend(inputs):
        block_queries, window_ids, random_ids, summary_ids = inputs
        gathered = jnp.concatenate(
            [nearby[window_ids], fetched[random_ids], summary[summary_ids]], axis=1
        )
        key_count = gathered.shape[1] * BLK
        gathered = gathered.reshape(group_size, key_count, 2, head_count, HD)
        scores = (
            jnp.einsum(
                "gqhd,gkhd->ghqk",
                block_queries,
                gathered[:, :, 0],
                preferred_element_type=jnp.float32,
            )
            * score_scale
        )
        row_peak = jnp.max(scores, axis=-1, keepdims=True)
        weights = jnp.exp(scores - row_peak)
        row_total = jnp.sum(weights, axis=-1)
        mixed = jnp.einsum(
            "ghqk,gkhd->gqhd",
            weights.astype(jnp.bfloat16),
            gathered[:, :, 1],
            preferred_element_type=jnp.float32,
        )
        mixed = mixed / jnp.transpose(row_total, (0, 2, 1))[..., None]
        return mixed.astype(jnp.bfloat16)

    attended = lax.map(
        attend,
        (
            queries.reshape(group_count, group_size, BLK, head_count, HD),
            window_index.reshape(group_count, group_size, WIN),
            random_index.reshape(group_count, group_size, R),
            summary_blocks.reshape(group_count, group_size, FIXL),
        ),
    )
    attended = attended.reshape(tok_rows, columns)
    partial_value = jnp.dot(attended, w_out, preferred_element_type=jnp.float32)
    return lax.psum_scatter(
        partial_value.astype(jnp.bfloat16), "head", scatter_dimension=1, tiled=True
    )


def solution(mesh):
    placed = (
        P("seq", None),
        P(None, "head"),
        P(None, "head"),
        P(None, "head"),
        P("head", None),
        P("seq", None),
        P(),
        P("seq", None),
        P(),
        P(),
    )
    return jax.shard_map(
        per_device, mesh=mesh, in_specs=placed, out_specs=P("seq", "head"), check_vma=False
    )
```

profile of v0, /device:TPU:0, one launch (start us, length us, event | category | flops | bytes accessed | tf_op | source)
XLA Modules:
  0.0 655.3 jit_solution(8665046302727600465)
XLA Ops:
  19.7 7.8 %gather_fusion.3 = bf16[48,128,2,512]{3,1,2,0:T(8,128)(2,1)} fusion(bf16[8,128,2,512]{3,1,0,2:T(8,128)(2,1)} %pad_maximum_fusion.3, s32[1024]{0:T(1024)S(1)} %pad_clamp_fusion.3), kind=kCustom, calls=%fused_computation.3 | custom fusion | bytes 25166016 | tf_op jit(solution)/shard_map/gather | solution.py:85
  27.6 23.6 %copy.41 = bf16[8,6,128,2,512]{4,3,2,1,0:T(2,128)(2,1)} copy(bf16[8,6,128,2,512]{4,2,3,1,0:T(8,128)(2,1)} %bitcast.104) | data formatting | bytes 25165824 | tf_op jit(solution)/shard_map/gather | solution.py:85
  51.2 7.3 %all-to-all-start = ((bf16[8,6,128,2,512]{4,3,2,1,0:T(2,128)(2,1)}), bf16[8,6,128,2,512]{4,3,2,1,0:T(2,128)(2,1)}, u32[]{:S(2)}, u32[]{:S(2)}) async-start(bf16[8,6,128,2,512]{4,3,2,1,0:T(2,128)(2,1)} %copy.41), calls=%async_computation | async-start | bytes 25165824 | tf_op jit(solution)/shard_map/all_to_all | solution.py:88
  78.0 6.2 convolution_convert_fusion.1
  86.6 92.0 %collective-permute-done = bf16[256,2,512]{2,0,1:T(8,128)(2,1)} collective-permute-done((bf16[256,2,512]{2,0,1:T(8,128)(2,1)}, bf16[256,2,512]{2,0,1:T(8,128)(2,1)}, u32[]{:S(2)}, u32[]{:S(2)}) %collective-permute-start) | collective-permute-done | bytes 524320 | tf_op jit(solution)/shard_map/ppermute | solution.py:18
  185.1 214.7 %all-reduce.2.cloned.1.call-done = f32[512,1024]{1,0:T(8,128)} async-done(((f32[512,1024]{1,0:T(8,128)}), f32[512,1024]{1,0:T(8,128)}) %all-reduce.2.cloned.1.call-update) | async-done | bytes 2097168 | tf_op jit(solution)/shard_map/psum | solution.py:76
  404.6 195.0 %while.10 = (s32[]{:T(128)}, bf16[2,4,128,4,128]{4,3,2,1,0:T(4,128)(2,1)}, s32[2,4,3]{1,0,2:T(2,128)S(1)}, bf16[12,128,2,512]{3,2,1,0:T(2,128)(2,1)}, s32[2,4,4]...) while((s32[]{:T(128)}, ...), condition=%wide.region_6.7_spmd, body=%wide.region_3.6_spmd.sunk | while | flops 1236794496 | bytes 204527360 | solution.py:126
  404.9 14.5 %gather_fusion.1 = bf16[16,128,2,512]{3,2,1,0:T(2,128)(2,1)} fusion(bf16[48,128,2,512]{3,2,1,0:T(2,128)(2,1)} %get-tuple-element.194, s32[1024]{0:T(1024)S(1)} %pad_clamp_fusion.8), kind=kCustom, calls=%fused_computation.1.clone.1 | custom fusion | bytes 8388672 | tf_op jit(solution)/shard_map/while/body/eval_jaxpr/gather | solution.py:101
  424.7 9.7 %gather_fusion.2 = bf16[12,128,2,512]{3,2,1,0:T(2,128)(2,1)} fusion(bf16[12,128,2,512]{3,2,1,0:T(2,128)(2,1)} %get-tuple-element.192, s32[1024]{0:T(1024)S(1)} %pad_clamp_fusion.9), kind=kCustom, calls=%fused_computation.clone.1 | custom fusion | bytes 6291504 | tf_op jit(solution)/shard_map/while/body/eval_jaxpr/gather | solution.py:101
  438.9 5.7 gather_fusion
  447.4 6.3 pad_maximum_fusion.5
  453.7 13.9 %reshape.311 = bf16[4,1152,2,4,128]{4,3,1,2,0:T(4,128)(2,1)} reshape(bf16[4,9,128,2,512]{4,2,1,3,0:T(8,128)(2,1)} %pad_maximum_fusion.5) | data formatting | bytes 18874368 | tf_op jit(solution)/shard_map/while/body/eval_jaxpr/reshape | solution.py:104
  467.6 8.8 %fusion.54 = (bf16[4,1152,1,4,128]{4,3,1,2,0:T(4,128)(2,1)}, bf16[4,1152,1,4,128]{4,3,1,2,0:T(4,128)(2,1)S(1)}) fusion(bf16[4,1152,2,4,128]{4,3,1,2,0:T(4,128)(2,1)} %reshape.311), kind=kLoop, calls=%fused_computation.73.clone.1 | loop fusion | bytes 18874368 | tf_op jit(solution)/shard_map/while/body/eval_jaxpr/slice | solution.py:120
  481.9 8.2 %copy.82 = bf16[4,1152,1,4,128]{1,4,3,0,2:T(8,128)(2,1)} copy(bf16[4,1152,1,4,128]{4,3,1,2,0:T(4,128)(2,1)} %get-tuple-element.168) | data formatting | bytes 9437184 | tf_op jit(solution)/shard_map/while
  490.2 7.9 %fusion.56 = bf16[1,4,128,4,128]{2,4,3,1,0:T(8,128)(2,1)} fusion(f32[4,4,128,1152]{3,2,1,0:T(8,128)} %copy-done.1, f32[4,4,128]{2,1,0:T(4,128)S(1)} %get-tuple-element.167, bf16[4,1152,1,4,128]{1,4,3,0,2:T(8,128)(2,1)} %copy.82, f32[4,128,4]{1,2,0:T(4,128)S(1)} %bitcast.115), kind=kOutput, calls=%fused_computation.17.clone.1 | convolution fusion | flops 611581952 | bytes 14696448 | tf_op jit(solution)/shard_map/while/body/eval_jaxpr/ghqk,gkhd->gqhd/dot_general | solution.py:117
  502.3 14.5 %gather_fusion.1 = bf16[16,128,2,512]{3,2,1,0:T(2,128)(2,1)} fusion(bf16[48,128,2,512]{3,2,1,0:T(2,128)(2,1)} %get-tuple-element.194, s32[1024]{0:T(1024)S(1)} %pad_clamp_fusion.8), kind=kCustom, calls=%fused_computation.1.clone.1 | custom fusion | bytes 8388672 | tf_op jit(solution)/shard_map/while/body/eval_jaxpr/gather | solution.py:101
  522.1 9.8 %gather_fusion.2 = bf16[12,128,2,512]{3,2,1,0:T(2,128)(2,1)} fusion(bf16[12,128,2,512]{3,2,1,0:T(2,128)(2,1)} %get-tuple-element.192, s32[1024]{0:T(1024)S(1)} %pad_clamp_fusion.9), kind=kCustom, calls=%fused_computation.clone.1 | custom fusion | bytes 6291504 | tf_op jit(solution)/shard_map/while/body/eval_jaxpr/gather | solution.py:101
  536.3 5.8 gather_fusion
  544.8 6.3 pad_maximum_fusion.5
  551.1 13.9 %reshape.311 = bf16[4,1152,2,4,128]{4,3,1,2,0:T(4,128)(2,1)} reshape(bf16[4,9,128,2,512]{4,2,1,3,0:T(8,128)(2,1)} %pad_maximum_fusion.5) | data formatting | bytes 18874368 | tf_op jit(solution)/shard_map/while/body/eval_jaxpr/reshape | solution.py:104
  565.1 8.8 %fusion.54 = (bf16[4,1152,1,4,128]{4,3,1,2,0:T(4,128)(2,1)}, bf16[4,1152,1,4,128]{4,3,1,2,0:T(4,128)(2,1)S(1)}) fusion(bf16[4,1152,2,4,128]{4,3,1,2,0:T(4,128)(2,1)} %reshape.311), kind=kLoop, calls=%fused_computation.73.clone.1 | loop fusion | bytes 18874368 | tf_op jit(solution)/shard_map/while/body/eval_jaxpr/slice | solution.py:120
  579.3 8.2 %copy.82 = bf16[4,1152,1,4,128]{1,4,3,0,2:T(8,128)(2,1)} copy(bf16[4,1152,1,4,128]{4,3,1,2,0:T(4,128)(2,1)} %get-tuple-element.168) | data formatting | bytes 9437184 | tf_op jit(solution)/shard_map/while
  587.6 7.9 %fusion.56 = bf16[1,4,128,4,128]{2,4,3,1,0:T(8,128)(2,1)} fusion(f32[4,4,128,1152]{3,2,1,0:T(8,128)} %copy-done.1, f32[4,4,128]{2,1,0:T(4,128)S(1)} %get-tuple-element.167, bf16[4,1152,1,4,128]{1,4,3,0,2:T(8,128)(2,1)} %copy.82, f32[4,128,4]{1,2,0:T(4,128)S(1)} %bitcast.115), kind=kOutput, calls=%fused_computation.17.clone.1 | convolution fusion | flops 611581952 | bytes 14696448 | tf_op jit(solution)/shard_map/while/body/eval_jaxpr/ghqk,gkhd->gqhd/dot_general | solution.py:117
  605.2 43.3 %reduce-scatter.2.cloned.1.call-done = bf16[1024,512]{1,0:T(8,128)(2,1)} async-done(((bf16[1024,2048]{1,0:T(8,128)(2,1)}), bf16[1024,512]{1,0:T(8,128)(2,1)}) %reduce-scatter.2.cloned.1.call-update) | async-done | bytes 1048592 | tf_op jit(solution)/shard_map/reduce_scatter | solution.py:137
  (106 shorter events, 96.0 us)
Async XLA Ops:
  6.5 593.1 %copy-start = (bf16[512,2048]{1,0:T(8,128)(2,1)S(1)}, bf16[512,2048]{1,0:T(8,128)(2,1)}, u32[]{:S(2)}) copy-start(bf16[512,2048]{1,0:T(8,128)(2,1)} %param.16) | copy-start | bytes 6291460
  7.6 5.4 copy-start.8
  7.6 5.4 copy-start.9
  51.2 353.4 %all-to-all-start = ((bf16[8,6,128,2,512]{4,3,2,1,0:T(2,128)(2,1)}), bf16[8,6,128,2,512]{4,3,2,1,0:T(2,128)(2,1)}, u32[]{:S(2)}, u32[]{:S(2)}) async-start(bf16[8,6,128,2,512]{4,3,2,1,0:T(2,128)(2,1)} %copy.41), calls=%async_computation | async-start | bytes 25165824 | tf_op jit(solution)/shard_map/all_to_all | solution.py:88
  58.5 341.4 %all-reduce.2.cloned.1.call-start = ((), (), s32[]{:S(2)}) async-start(), calls=%async_computation.2 | async-start | bytes 4194304 | tf_op jit(solution)/shard_map/psum | solution.py:76
  58.6 6.7 %copy-start.4 = (s32[512]{0:T(512)S(1)}, s32[512]{0:T(512)}, u32[]{:S(2)}) copy-start(s32[512]{0:T(512)} %param.21) | copy-start | bytes 6148
  58.6 6.7 %copy-start.5 = (s32[512]{0:T(512)S(1)}, s32[512]{0:T(512)}, u32[]{:S(2)}) copy-start(s32[512]{0:T(512)} %param.20) | copy-start | bytes 6148
  69.5 578.9 %reduce-scatter.2.cloned.1.call-start = ((), (), s32[]{:S(2)}) async-start(), calls=%async_computation.3 | async-start | bytes 5242880 | tf_op jit(solution)/shard_map/reduce_scatter | solution.py:137
  71.7 106.9 %collective-permute-start = (bf16[256,2,512]{2,0,1:T(8,128)(2,1)}, bf16[256,2,512]{2,0,1:T(8,128)(2,1)}, u32[]{:S(2)}, u32[]{:S(2)}) collective-permute-start(bf16[256,2,512]{2,0,1:T(8,128)(2,1)} %get-tuple-element.102), channel_id=1, source_target_pairs={{0,4},{4,8},{8,12},{12,16},{16,20},{20,24},{24,28},{1,5},{5,9},{9,... | collective-permute-start | bytes 1572872 | tf_op jit(solution)/shard_map/ppermute | solution.py:18
  76.4 7.9 %copy-start.6 = (s32[8,3]{0,1:T(4,128)S(1)}, s32[8,3]{0,1:T(4,128)}, u32[]{:S(2)}) copy-start(s32[8,3]{0,1:T(4,128)} %param.17) | copy-start | bytes 292
  76.4 10.1 %copy-start.7 = (s32[8,2]{0,1:T(2,128)S(1)}, s32[8,2]{0,1:T(2,128)}, u32[]{:S(2)}) copy-start(s32[8,2]{0,1:T(2,128)} %param.19) | copy-start | bytes 196
  76.4 102.2 %collective-permute-start.1 = (bf16[256,2,512]{2,0,1:T(8,128)(2,1)}, bf16[256,2,512]{2,0,1:T(8,128)(2,1)}, u32[]{:S(2)}, u32[]{:S(2)}) collective-permute-start(bf16[256,2,512]{2,0,1:T(8,128)(2,1)} %get-tuple-element.103), channel_id=1, source_target_pairs={{4,0},{8,4},{12,8},{16,12},{20,16},{24,20},{28,24},{5,1},{9,5},{13... | collective-permute-start | bytes 1572872 | tf_op jit(solution)/shard_map/ppermute | solution.py:21
  444.6 2.8 copy-start.2
  467.6 8.9 %copy-start.3 = (bf16[2,4,128,4,128]{4,3,2,1,0:T(4,128)(2,1)S(1)}, bf16[2,4,128,4,128]{4,3,2,1,0:T(4,128)(2,1)}, u32[]{:S(2)}) copy-start(bf16[2,4,128,4,128]{4,3,2,1,0:T(4,128)(2,1)} %get-tuple-element.197) | copy-start | bytes 3145732 | tf_op jit(solution)/shard_map/while
  478.4 3.6 copy-start.1
  542.0 2.8 copy-start.2
  565.1 8.9 %copy-start.3 = (bf16[2,4,128,4,128]{4,3,2,1,0:T(4,128)(2,1)S(1)}, bf16[2,4,128,4,128]{4,3,2,1,0:T(4,128)(2,1)}, u32[]{:S(2)}) copy-start(bf16[2,4,128,4,128]{4,3,2,1,0:T(4,128)(2,1)} %get-tuple-element.197) | copy-start | bytes 3145732 | tf_op jit(solution)/shard_map/while
  575.8 3.6 copy-start.1
Sparse Core Ops, SparseCore 0:
  69.6 330.1 all-reduce.1
  605.3 43.1 reduce-scatter.1
where the time goes:
time: 658 us; the launch traced here: 655 us
  waiting for transfers between devices  350 us (53%)
  local copies, waits for them, and re-layouts  205 us (31%)
  matrix products  43.8 us (7%)
  other arithmetic  29.3 us (4%)
  starting transfers between devices  13.7 us (2%)
  between operations  13.5 us (2%)
    psum x1, waiting for transfers between devices, per_device(): whole_sums = lax.psum(partial_sums, 'seq')  215 us
    ppermute x1, waiting for transfers between devices, with_halo(): lax.ppermute(lax.slice_in_dim(block, block.shape[dim] - width, None, axis...  92 us
    reduce_scatter x1, waiting for transfers between devices, per_device(): lax.psum_scatter(partial_value.astype(jnp.bfloat16), 'head', scatter_dime...  43.3 us
    gather x4, local copies, waits for them, and re-layouts, attend(): fetched[random_ids]  39.2 us
    gather x2, local copies, waits for them, and re-layouts, per_device(): outgoing = blocks[send_index]  31.4 us
    gather x4, local copies, waits for them, and re-layouts, attend(): nearby[window_ids]  27.9 us
    reshape x2, local copies, waits for them, and re-layouts, attend(): gathered = gathered.reshape(group_size, key_count, 2, head_count, HD)  27.8 us
    while x14, local copies, waits for them, and re-layouts  20.9 us
  transfers between devices with their start and end apart: 5, of which 3 were waited for; matrix products, arithmetic and copies ran while one was open for 5% of the time, Pallas kernels for 0%

commit v1 on v0

v1 whole, which is shorter than its diff:
```python
import functools

import jax
import jax.numpy as jnp
import numpy as np
from jax import lax
from jax.experimental import pallas as pl
from jax.experimental.pallas import tpu as pltpu
from jax.sharding import PartitionSpec as P

HD = 128
BLK = 128
MIB = 1 << 20


def ring_order(devices):
    half = devices // 2
    return [2 * i for i in range(half)] + [2 * i + 1 for i in reversed(range(half))]


def kv_kernel(tokens_ref, wk_ref, wv_ref, start_ref, end_ref, out_ref):
    tok_rows = tokens_ref.shape[0]
    share = start_ref.shape[0]
    weight = jnp.concatenate([wk_ref[...], wv_ref[...]], axis=1)
    kv = jnp.dot(tokens_ref[...], weight, preferred_element_type=jnp.float32).astype(jnp.bfloat16)
    out_ref[:tok_rows, :] = kv
    position = lax.broadcasted_iota(jnp.int32, (share, tok_rows), 1)
    start = start_ref[...]
    end = end_ref[...]
    member = ((position >= start) & (position < end)).astype(jnp.float32).astype(jnp.bfloat16)
    sums = jnp.dot(member, kv, preferred_element_type=jnp.float32)
    counts = (end - start).astype(jnp.float32)
    out_ref[tok_rows:, :] = (sums / counts).astype(jnp.bfloat16)


def project_kv(tokens, w_key, w_value, start, end, head):
    tok_rows, width = tokens.shape
    share = start.shape[0]
    return pl.pallas_call(
        kv_kernel,
        grid=(1,),
        in_specs=[
            pl.BlockSpec((tok_rows, width), lambda i: (0, 0)),
            pl.BlockSpec((width, HD), lambda i: (0, head)),
            pl.BlockSpec((width, HD), lambda i: (0, head)),
            pl.BlockSpec((share, 1), lambda i: (0, 0)),
            pl.BlockSpec((share, 1), lambda i: (0, 0)),
        ],
        out_specs=pl.BlockSpec((tok_rows + share, 2 * HD), lambda i: (0, 0)),
        out_shape=jax.ShapeDtypeStruct((tok_rows + share, 2 * HD), jnp.bfloat16),
        compiler_params=pltpu.CompilerParams(vmem_limit_bytes=40 * MIB),
        cost_estimate=pl.CostEstimate(
            flops=2 * tok_rows * width * 2 * HD, bytes_accessed=6 * MIB, transcendentals=0
        ),
        name="project_kv",
    )(tokens, w_key, w_value, start, end)


def attend_kernel(devices, table_ref, owner_ref, q_ref, *refs):
    buffers = refs[: devices + 1]
    out_ref, kv, summary, sems = refs[devices + 1 :]
    tok_rows = q_ref.shape[0]
    half = tok_rows // 2
    share = summary.shape[0] // devices
    copies = []

    def copy(source, target):
        done = pltpu.make_async_copy(source, target, sems.at[len(copies)])
        done.start()
        copies.append(done)

    for at, buffer in enumerate(buffers):
        owner = owner_ref[min(at, devices - 1)]
        first = half if at == devices else 0
        rows = tok_rows if at < devices - 1 else half
        base = pl.multiple_of(owner * tok_rows + first, BLK)
        copy(buffer.at[pl.ds(0, rows)], kv.at[pl.ds(base, rows)])
        if at != devices - 1:
            segment = lax.rem(owner + devices // 2, devices)
            base = pl.multiple_of(segment * share, 16)
            copy(buffer.at[pl.ds(rows, share)], summary.at[pl.ds(base, share)])
    for done in copies:
        done.wait()
    factor = HD**-0.5 * float(np.log2(np.e))
    slots = table_ref.shape[1]

    def one_block(block, carry):
        parts = []
        for slot in range(slots):
            base = pl.multiple_of(table_ref[block, slot] * BLK, BLK)
            source = kv if slot < slots - 2 else summary
            parts.append(source[pl.ds(base, BLK), :])
        gathered = jnp.concatenate(parts, axis=0)
        rows = pl.ds(pl.multiple_of(block * BLK, BLK), BLK)
        scores = lax.dot_general(
            q_ref[rows, :],
            gathered[:, :HD],
            (((1,), (1,)), ((), ())),
            preferred_element_type=jnp.float32,
        )
        peak = jnp.max(scores, axis=1, keepdims=True)
        weights = jnp.exp2((scores - peak) * factor)
        total = jnp.sum(weights, axis=1, keepdims=True)
        mixed = jnp.dot(
            weights.astype(jnp.bfloat16), gathered[:, HD:], preferred_element_type=jnp.float32
        )
        out_ref[rows, :] = (mixed / total).astype(jnp.bfloat16)
        return carry

    lax.fori_loop(0, tok_rows // BLK, one_block, 0)


def attend(table, owner_ids, queries, buffers, head, devices, share):
    tok_rows = queries.shape[0]
    any_spec = pl.BlockSpec(memory_space=pl.ANY)
    smem = pl.BlockSpec(memory_space=pltpu.SMEM)
    return pl.pallas_call(
        functools.partial(attend_kernel, devices),
        grid=(1,),
        in_specs=[smem, smem, pl.BlockSpec((tok_rows, HD), lambda i: (0, head))]
        + [any_spec] * len(buffers),
        out_specs=pl.BlockSpec((tok_rows, HD), lambda i: (0, 0)),
        out_shape=jax.ShapeDtypeStruct((tok_rows, HD), jnp.bfloat16),
        scratch_shapes=[
            pltpu.VMEM((devices * tok_rows, 2 * HD), jnp.bfloat16),
            pltpu.VMEM((devices * share, 2 * HD), jnp.bfloat16),
            pltpu.SemaphoreType.DMA((2 * devices + 1,)),
        ],
        compiler_params=pltpu.CompilerParams(vmem_limit_bytes=48 * MIB),
        cost_estimate=pl.CostEstimate(
            flops=4 * tok_rows * 1152 * HD,
            bytes_accessed=devices * tok_rows * 4 * HD,
            transcendentals=tok_rows * 1152,
        ),
        name="attend",
    )(table, owner_ids, queries, *buffers)


def out_kernel(pieces, *refs):
    w_ref, out_ref = refs[pieces:]
    rows = jnp.concatenate([ref[...] for ref in refs[:pieces]], axis=1)
    out_ref[...] = jnp.dot(rows, w_ref[...], preferred_element_type=jnp.float32).astype(
        jnp.bfloat16
    )


def project_out(pieces, weight):
    tok_rows = pieces[0].shape[0]
    width, columns = weight.shape
    tile = 256
    return pl.pallas_call(
        functools.partial(out_kernel, len(pieces)),
        grid=(tok_rows // tile,),
        in_specs=[pl.BlockSpec((tile, HD), lambda i: (i, 0))] * len(pieces)
        + [pl.BlockSpec((width, columns), lambda i: (0, 0))],
        out_specs=pl.BlockSpec((tile, columns), lambda i: (i, 0)),
        out_shape=jax.ShapeDtypeStruct((tok_rows, columns), jnp.bfloat16),
        compiler_params=pltpu.CompilerParams(vmem_limit_bytes=40 * MIB),
        cost_estimate=pl.CostEstimate(
            flops=2 * tok_rows * width * columns, bytes_accessed=7 * MIB, transcendentals=0
        ),
        name="project_out",
    )(*pieces, weight)


def ring_gather(chunk, tok_rows, devices):
    order = ring_order(devices)
    forward = [(order[p], order[(p + 1) % devices]) for p in range(devices)]
    backward = [(target, source) for source, target in forward]
    buffers = [chunk]
    ahead = behind = chunk
    for _ in range(1, devices // 2):
        ahead = lax.ppermute(ahead, "seq", forward)
        behind = lax.ppermute(behind, "seq", backward)
        buffers += [ahead, behind]
    half = tok_rows // 2
    buffers.append(lax.ppermute(ahead[:half], "seq", forward))
    buffers.append(lax.ppermute(behind[half:], "seq", backward))
    return buffers


def per_device(
    tokens,
    w_query,
    w_key,
    w_value,
    w_out,
    window_blocks,
    random_blocks,
    summary_blocks,
    seg_start,
    seg_end,
):
    tok_rows = tokens.shape[0]
    columns = w_query.shape[1]
    heads = columns // HD
    block_count = tok_rows // BLK
    devices = lax.axis_size("seq")
    groups = lax.axis_size("head")
    me = lax.axis_index("seq")
    group = lax.axis_index("head")
    share = seg_start.shape[0] // devices

    order = np.array(ring_order(devices), np.int32)
    position = jnp.asarray(np.argsort(order).astype(np.int32))[me]
    steps = [0] + [s * k for k in range(1, devices // 2) for s in (-1, 1)] + [devices // 2]
    owner_ids = jnp.asarray(order)[(position + jnp.asarray(steps, jnp.int32)) % devices]
    mine = lax.dynamic_slice_in_dim(random_blocks, me * block_count, block_count, 0)
    table = jnp.concatenate([window_blocks, mine, summary_blocks], axis=1)
    first_segment = lax.rem(me + devices // 2, devices) * share
    start = lax.dynamic_slice_in_dim(seg_start, first_segment, share, 0) - me * tok_rows
    end = lax.dynamic_slice_in_dim(seg_end, first_segment, share, 0) - me * tok_rows

    gathered = [
        ring_gather(
            project_kv(tokens, w_key, w_value, start[:, None], end[:, None], head),
            tok_rows,
            devices,
        )
        for head in range(heads)
    ]
    queries = jnp.dot(tokens, w_query, preferred_element_type=jnp.float32).astype(jnp.bfloat16)

    out_weight = lax.all_to_all(
        w_out.reshape(heads * HD, groups, -1), "head", split_axis=1, concat_axis=0, tiled=True
    ).reshape(groups, heads * HD, -1)
    across = [(g, g ^ 2) for g in range(groups)]
    beside = [(g, g ^ 1) for g in range(groups)]
    pieces = []
    weights = []
    for head in range(heads):
        own = attend(table, owner_ids, queries, gathered[head], head, devices, share)
        other = lax.ppermute(own, "head", across)
        pieces += [own, other, lax.ppermute(own, "head", beside), lax.ppermute(other, "head", beside)]
        for flip in (0, 2, 1, 3):
            rows = lax.dynamic_index_in_dim(out_weight, group ^ flip, 0, keepdims=False)
            weights.append(rows[head * HD : (head + 1) * HD])
    return project_out(pieces, jnp.concatenate(weights, axis=0))


def solution(mesh):
    placed = (
        P("seq", None),
        P(None, "head"),
        P(None, "head"),
        P(None, "head"),
        P("head", None),
        P("seq", None),
        P(),
        P("seq", None),
        P(),
        P(),
    )
    return jax.shard_map(
        per_device, mesh=mesh, in_specs=placed, out_specs=P("seq", "head"), check_vma=False
    )
```

time: 658 us -> 224 us (0.34)
  waiting for transfers between devices: 350 us -> 90.5 us
  local copies, waits for them, and re-layouts: 205 us -> 26.6 us
  starting transfers between devices: 13.7 us -> 60.9 us
  matrix products: 43.8 us -> 2.32 us
  Pallas kernels: 0 us -> 40.9 us
  other arithmetic: 29.3 us -> 1.48 us
  between operations: 13.5 us -> 0.42 us
    psum x1 -> x0, waiting for transfers between devices: 215 us -> none  [per_device(): whole_sums = lax.psum(partial_sums, 'seq')]
    gather x14 -> x1, local copies, waits for them, and re-layouts: 114 us -> 0.64 us  [per_device(): jnp.asarray(order)[(position + jnp.asarray(steps, jnp.int32)) % devices]]
    ppermute x2 -> x44, starting transfers between devices: 6.29 us -> 56.5 us  [the longest x12 22.1 us: ring_gather(): ahead = lax.ppermute(ahead, 'seq', forward)]
    reduce_scatter x1 -> x0, waiting for transfers between devices: 43.3 us -> none  [per_device(): lax.psum_scatter(partial_value.astype(jnp.bfloat16), 'head', scatter_dime...]
    dot_general x9 -> x1, matrix products: 43.8 us -> 2.32 us  [per_device(): jnp.dot(tokens, w_query, preferred_element_type=jnp.float32)]
    pallas_call x0 -> x9, Pallas kernels: none -> 40.9 us  [the longest x4 27.7 us: attend(): pl.pallas_call(functools.partial(attend_kernel, devices), grid=(1,), in_s...]
    reshape x7 -> x1, local copies, waits for them, and re-layouts: 32.1 us -> 3.29 us  [per_device(): w_out.reshape(heads * HD, groups, -1)]
    while x15 -> x0, local copies, waits for them, and re-layouts: 25.8 us -> none
  transfers between devices with their start and end apart: 5 -> 45, of which waited for: 3 -> 21; matrix products, arithmetic and copies ran while one was open for 5% -> 7% of each run, Pallas kernels for 0% -> 17%
where the time goes in v1:
time: 224 us; the launch traced here: 223 us
  waiting for transfers between devices  90.5 us (40%)
  starting transfers between devices  60.9 us (27%)
  Pallas kernels  40.9 us (18%)
  local copies, waits for them, and re-layouts  26.6 us (12%)
  matrix products  2.32 us (1%)
    ppermute x12, waiting for transfers between devices, ring_gather(): ahead = lax.ppermute(ahead, 'seq', forward)  72.8 us
    pallas_call x4, Pallas kernels, attend(): pl.pallas_call(functools.partial(attend_kernel, devices), grid=(1,), in_s...  27.7 us
    ppermute x12, starting transfers between devices, ring_gather(): ahead = lax.ppermute(ahead, 'seq', forward)  22.1 us
    unnamed x56, local copies, waits for them, and re-layouts  15.5 us
    ppermute x12, starting transfers between devices, ring_gather(): behind = lax.ppermute(behind, 'seq', backward)  15.2 us
    ppermute x12, waiting for transfers between devices, ring_gather(): behind = lax.ppermute(behind, 'seq', backward)  11.1 us
    pallas_call x4, Pallas kernels, project_kv(): pl.pallas_call(kv_kernel, grid=(1,), in_specs=[pl.BlockSpec((tok_rows, wi...  9.55 us
    ppermute x4, starting transfers between devices, ring_gather(): buffers.append(lax.ppermute(ahead[:half], 'seq', forward))  7.19 us
  transfers between devices with their start and end apart: 45, of which 21 were waited for; matrix products, arithmetic and copies ran while one was open for 7% of the time, Pallas kernels for 17%

profile of v1, /device:TPU:0, one launch (start us, length us, event | category | flops | bytes accessed | tf_op | source)
XLA Modules:
  0.0 223.2 jit_solution(5963413554760542416)
XLA Ops:
  0.0 3.3 %copy.41 = bf16[64,4,8,512]{3,2,0,1:T(8,128)(2,1)} copy(bf16[64,4,8,512]{3,2,1,0:T(8,128)(2,1)} %bitcast.84) | data formatting | bytes 4194304 | tf_op jit(solution)/shard_map/reshape | solution.py:225
  3.3 4.4 %all-to-all-start = ((bf16[512,4,512]{2,0,1:T(8,128)(2,1)}), bf16[512,4,512]{2,0,1:T(8,128)(2,1)}, u32[]{:S(2)}, u32[]{:S(2)}) async-start(bf16[512,4,512]{2,0,1:T(8,128)(2,1)} %bitcast.83), calls=%async_computation | async-start | bytes 4194304 | tf_op jit(solution)/shard_map/all_to_all | solution.py:224
  14.1 2.4 %project_kv.4.refs_0_ = bf16[1088,256]{1,0:T(8,128)(2,1)} custom-call(bf16[1024,2048]{1,0:T(8,128)(2,1)S(1)} %copy-done.1, bf16[2048,512]{1,0:T(8,128)(2,1)S(1)} %copy-done.3, bf16[2048,512]{1,0:T(8,128)(2,1)S(1)} %copy-done.5, s32[64,1]{1,0:T(8,128)S(1)} %copy.29.start_ref, s32[64,1]{1,0:T(8,128)S(1)} %copy.30.end_ref), custom_call_target="tpu_custom_call" | custom-call | flops 1073741824 | bytes 6291456 | tf_op jit(solution)/shard_map/project_kv/pallas_call | solution.py:39
  16.5 3.0 %collective-permute-start = (bf16[1088,256]{1,0:T(8,128)(2,1)}, bf16[1088,256]{1,0:T(8,128)(2,1)}, u32[]{:S(2)}, u32[]{:S(2)}) collective-permute-start(bf16[1088,256]{1,0:T(8,128)(2,1)} %project_kv.4.refs_0_), channel_id=1, source_target_pairs={{0,8},{8,16},{16,24},{24,28},{28,20},{20,12},{12,4},{4,0},{1,9},{9... | collective-permute-start | bytes 1671176 | tf_op jit(solution)/shard_map/ppermute | solution.py:173
  19.5 2.4 %project_kv.5.refs_0_ = bf16[1088,256]{1,0:T(8,128)(2,1)} custom-call(bf16[1024,2048]{1,0:T(8,128)(2,1)S(1)} %copy-done.1, bf16[2048,512]{1,0:T(8,128)(2,1)S(1)} %copy-done.3, bf16[2048,512]{1,0:T(8,128)(2,1)S(1)} %copy-done.5, s32[64,1]{1,0:T(8,128)S(1)} %copy.29.start_ref, s32[64,1]{1,0:T(8,128)S(1)} %copy.30.end_ref), custom_call_target="tpu_custom_call" | custom-call | flops 1073741824 | bytes 6291456 | tf_op jit(solution)/shard_map/project_kv/pallas_call | solution.py:39
  23.9 2.4 %project_kv.6.refs_0_ = bf16[1088,256]{1,0:T(8,128)(2,1)} custom-call(bf16[1024,2048]{1,0:T(8,128)(2,1)S(1)} %copy-done.1, bf16[2048,512]{1,0:T(8,128)(2,1)S(1)} %copy-done.3, bf16[2048,512]{1,0:T(8,128)(2,1)S(1)} %copy-done.5, s32[64,1]{1,0:T(8,128)S(1)} %copy.29.start_ref, s32[64,1]{1,0:T(8,128)S(1)} %copy.30.end_ref), custom_call_target="tpu_custom_call" | custom-call | flops 1073741824 | bytes 6291456 | tf_op jit(solution)/shard_map/project_kv/pallas_call | solution.py:39
  36.7 2.4 %project_kv.7.refs_0_ = bf16[1088,256]{1,0:T(8,128)(2,1)} custom-call(bf16[1024,2048]{1,0:T(8,128)(2,1)S(1)} %copy-done.2, bf16[2048,512]{1,0:T(8,128)(2,1)S(1)} %copy-done.4, bf16[2048,512]{1,0:T(8,128)(2,1)S(1)} %copy-done.6, s32[64,1]{1,0:T(8,128)S(1)} %copy.29.start_ref, s32[64,1]{1,0:T(8,128)S(1)} %copy.30.end_ref), custom_call_target="tpu_custom_call" | custom-call | flops 1073741824 | bytes 6291456 | tf_op jit(solution)/shard_map/project_kv/pallas_call | solution.py:39
  41.8 3.4 %collective-permute-done.11.refs_1_ = bf16[1088,256]{1,0:T(8,128)(2,1)} collective-permute-done((bf16[1088,256]{1,0:T(8,128)(2,1)}, bf16[1088,256]{1,0:T(8,128)(2,1)}, u32[]{:S(2)}, u32[]{:S(2)}) %collective-permute-start.11) | collective-permute-done | bytes 557088 | tf_op jit(solution)/shard_map/ppermute | solution.py:173
  51.6 5.6 %collective-permute-done.22.refs_1_ = bf16[1088,256]{1,0:T(8,128)(2,1)} collective-permute-done((bf16[1088,256]{1,0:T(8,128)(2,1)}, bf16[1088,256]{1,0:T(8,128)(2,1)}, u32[]{:S(2)}, u32[]{:S(2)}) %collective-permute-start.22) | collective-permute-done | bytes 557088 | tf_op jit(solution)/shard_map/ppermute | solution.py:173
  60.8 8.3 %collective-permute-done.33.refs_1_ = bf16[1088,256]{1,0:T(8,128)(2,1)} collective-permute-done((bf16[1088,256]{1,0:T(8,128)(2,1)}, bf16[1088,256]{1,0:T(8,128)(2,1)}, u32[]{:S(2)}, u32[]{:S(2)}) %collective-permute-start.33) | collective-permute-done | bytes 557088 | tf_op jit(solution)/shard_map/ppermute | solution.py:173
  72.7 8.3 %collective-permute-done.2.refs_3_ = bf16[1088,256]{1,0:T(8,128)(2,1)} collective-permute-done((bf16[1088,256]{1,0:T(8,128)(2,1)}, bf16[1088,256]{1,0:T(8,128)(2,1)}, u32[]{:S(2)}, u32[]{:S(2)}) %collective-permute-start.2) | collective-permute-done | bytes 557088 | tf_op jit(solution)/shard_map/ppermute | solution.py:173
  84.5 8.3 %collective-permute-done.13.refs_3_ = bf16[1088,256]{1,0:T(8,128)(2,1)S(1)} collective-permute-done((bf16[1088,256]{1,0:T(8,128)(2,1)}, bf16[1088,256]{1,0:T(8,128)(2,1)S(1)}, u32[]{:S(2)}, u32[]{:S(2)}) %collective-permute-start.13) | collective-permute-done | bytes 557088 | tf_op jit(solution)/shard_map/ppermute | solution.py:173
  96.5 8.3 %collective-permute-done.24.refs_3_ = bf16[1088,256]{1,0:T(8,128)(2,1)S(1)} collective-permute-done((bf16[1088,256]{1,0:T(8,128)(2,1)}, bf16[1088,256]{1,0:T(8,128)(2,1)S(1)}, u32[]{:S(2)}, u32[]{:S(2)}) %collective-permute-start.24) | collective-permute-done | bytes 557088 | tf_op jit(solution)/shard_map/ppermute | solution.py:173
  108.3 8.4 %collective-permute-done.35.refs_3_ = bf16[1088,256]{1,0:T(8,128)(2,1)S(1)} collective-permute-done((bf16[1088,256]{1,0:T(8,128)(2,1)}, bf16[1088,256]{1,0:T(8,128)(2,1)S(1)}, u32[]{:S(2)}, u32[]{:S(2)}) %collective-permute-start.35) | collective-permute-done | bytes 557088 | tf_op jit(solution)/shard_map/ppermute | solution.py:173
  120.3 8.3 %collective-permute-done.4.refs_5_ = bf16[1088,256]{1,0:T(8,128)(2,1)S(1)} collective-permute-done((bf16[1088,256]{1,0:T(8,128)(2,1)}, bf16[1088,256]{1,0:T(8,128)(2,1)S(1)}, u32[]{:S(2)}, u32[]{:S(2)}) %collective-permute-start.4) | collective-permute-done | bytes 557088 | tf_op jit(solution)/shard_map/ppermute | solution.py:173
  132.3 10.4 %collective-permute-done.16.refs_6_ = bf16[1088,256]{1,0:T(8,128)(2,1)S(1)} collective-permute-done((bf16[1088,256]{1,0:T(8,128)(2,1)S(1)}, bf16[1088,256]{1,0:T(8,128)(2,1)S(1)}, u32[]{:S(2)}, u32[]{:S(2)}) %collective-permute-start.16) | collective-permute-done | bytes 557088 | tf_op jit(solution)/shard_map/ppermute | solution.py:174
  145.5 7.0 %collective-permute-done.26.refs_5_ = bf16[1088,256]{1,0:T(8,128)(2,1)S(1)} collective-permute-done((bf16[1088,256]{1,0:T(8,128)(2,1)S(1)}, bf16[1088,256]{1,0:T(8,128)(2,1)S(1)}, u32[]{:S(2)}, u32[]{:S(2)}) %collective-permute-start.26) | collective-permute-done | bytes 557088 | tf_op jit(solution)/shard_map/ppermute | solution.py:173
  157.6 6.9 %collective-permute-done.37.refs_5_ = bf16[1088,256]{1,0:T(8,128)(2,1)S(1)} collective-permute-done((bf16[1088,256]{1,0:T(8,128)(2,1)S(1)}, bf16[1088,256]{1,0:T(8,128)(2,1)S(1)}, u32[]{:S(2)}, u32[]{:S(2)}) %collective-permute-start.37) | collective-permute-done | bytes 557088 | tf_op jit(solution)/shard_map/ppermute | solution.py:173
  174.4 7.1 %attend.4.refs_0_ = bf16[1024,128]{1,0:T(8,128)(2,1)S(1)} custom-call(s32[8,9]{1,0:T(8,128)S(1)} %pad_add_fusion.table_ref, s32[8]{0:T(128)S(1)} %gather_fusion, bf16[1024,512]{1,0:T(8,128)(2,1)S(1)} %convolution_convert_fusion.q_ref, bf16[1088,256]{1,0:T(8,128)(2,1)} %project_kv.4.refs_0_, bf16[1088,256]{1,0:T(8,128)(2,1)} %collective-permute-done.refs_1_, ...), custom_call_target="tpu_custom_call" | custom-call | flops 603979776 | bytes 4194304 | tf_op jit(solution)/shard_map/attend/pallas_call | solution.py:117
  185.7 6.9 %attend.5.refs_4_ = bf16[1024,128]{1,0:T(8,128)(2,1)S(1)} custom-call(s32[8,9]{1,0:T(8,128)S(1)} %pad_add_fusion.table_ref, s32[8]{0:T(128)S(1)} %gather_fusion, bf16[1024,512]{1,0:T(8,128)(2,1)S(1)} %convolution_convert_fusion.q_ref, bf16[1088,256]{1,0:T(8,128)(2,1)} %project_kv.5.refs_0_, bf16[1088,256]{1,0:T(8,128)(2,1)} %collective-permute-done.11.refs_1_, ...), custom_call_target="tpu_custom_call" | custom-call | flops 603979776 | bytes 4194304 | tf_op jit(solution)/shard_map/attend/pallas_call | solution.py:117
  192.8 6.9 %attend.6.refs_8_ = bf16[1024,128]{1,0:T(8,128)(2,1)S(1)} custom-call(s32[8,9]{1,0:T(8,128)S(1)} %pad_add_fusion.table_ref, s32[8]{0:T(128)S(1)} %gather_fusion, bf16[1024,512]{1,0:T(8,128)(2,1)S(1)} %convolution_convert_fusion.q_ref, bf16[1088,256]{1,0:T(8,128)(2,1)} %project_kv.6.refs_0_, bf16[1088,256]{1,0:T(8,128)(2,1)} %collective-permute-done.22.refs_1_, ...), custom_call_target="tpu_custom_call" | custom-call | flops 603979776 | bytes 4194304 | tf_op jit(solution)/shard_map/attend/pallas_call | solution.py:117
  202.0 6.9 %attend.7.refs_12_ = bf16[1024,128]{1,0:T(8,128)(2,1)S(1)} custom-call(s32[8,9]{1,0:T(8,128)S(1)} %pad_add_fusion.table_ref, s32[8]{0:T(128)S(1)} %gather_fusion, bf16[1024,512]{1,0:T(8,128)(2,1)S(1)} %convolution_convert_fusion.q_ref, bf16[1088,256]{1,0:T(8,128)(2,1)} %project_kv.7.refs_0_, bf16[1088,256]{1,0:T(8,128)(2,1)} %collective-permute-done.33.refs_1_, ...), custom_call_target="tpu_custom_call" | custom-call | flops 603979776 | bytes 4194304 | tf_op jit(solution)/shard_map/attend/pallas_call | solution.py:117
  212.3 5.4 %collective-permute-done.41.refs_13_ = bf16[1024,128]{1,0:T(8,128)(2,1)S(1)} collective-permute-done((bf16[1024,128]{1,0:T(8,128)(2,1)S(1)}, bf16[1024,128]{1,0:T(8,128)(2,1)S(1)}, u32[]{:S(2)}, u32[]{:S(2)}) %collective-permute-start.41) | collective-permute-done | bytes 262176 | tf_op jit(solution)/shard_map/ppermute | solution.py:233
  219.6 3.6 %project_out.1 = bf16[1024,512]{1,0:T(8,128)(2,1)} custom-call(bf16[1024,128]{1,0:T(8,128)(2,1)S(1)} %attend.4.refs_0_, bf16[1024,128]{1,0:T(8,128)(2,1)S(1)} %collective-permute-done.8.refs_1_, bf16[1024,128]{1,0:T(8,128)(2,1)S(1)} %collective-permute-done.9.refs_2_, bf16[1024,128]{1,0:T(8,128)(2,1)S(1)} %collective-permute-done.10.refs_3_, ...), custom_call_target="tpu_custom_call" | custom-call | flops 2147483648 | bytes 7340032 | tf_op jit(solution)/shard_map/project_out/pallas_call | solution.py:151
  (152 shorter events, 82.6 us)
Async XLA Ops:
  3.3 46.6 %all-to-all-start = ((bf16[512,4,512]{2,0,1:T(8,128)(2,1)}), bf16[512,4,512]{2,0,1:T(8,128)(2,1)}, u32[]{:S(2)}, u32[]{:S(2)}) async-start(bf16[512,4,512]{2,0,1:T(8,128)(2,1)} %bitcast.83), calls=%async_computation | async-start | bytes 4194304 | tf_op jit(solution)/shard_map/all_to_all | solution.py:224
  26.3 30.8 %collective-permute-start.22 = (bf16[1088,256]{1,0:T(8,128)(2,1)}, bf16[1088,256]{1,0:T(8,128)(2,1)}, u32[]{:S(2)}, u32[]{:S(2)}) collective-permute-start(bf16[1088,256]{1,0:T(8,128)(2,1)} %project_kv.6.refs_0_), channel_id=1, source_target_pairs={{0,8},{8,16},{16,24},{24,28},{28,20},{20,12},{12,4},{4,0},{1,9},{9... | collective-permute-start | bytes 1671176 | tf_op jit(solution)/shard_map/ppermute | solution.py:173
  39.1 30.0 %collective-permute-start.33 = (bf16[1088,256]{1,0:T(8,128)(2,1)}, bf16[1088,256]{1,0:T(8,128)(2,1)}, u32[]{:S(2)}, u32[]{:S(2)}) collective-permute-start(bf16[1088,256]{1,0:T(8,128)(2,1)} %project_kv.7.refs_0_), channel_id=1, source_target_pairs={{0,8},{8,16},{16,24},{24,28},{28,20},{20,12},{12,4},{4,0},{1,9},{9... | collective-permute-start | bytes 1671176 | tf_op jit(solution)/shard_map/ppermute | solution.py:173
  45.2 25.9 %collective-permute-start.34 = (bf16[1088,256]{1,0:T(8,128)(2,1)}, bf16[1088,256]{1,0:T(8,128)(2,1)}, u32[]{:S(2)}, u32[]{:S(2)}) collective-permute-start(bf16[1088,256]{1,0:T(8,128)(2,1)} %project_kv.7.refs_0_), channel_id=1, source_target_pairs={{8,0},{16,8},{24,16},{28,24},{20,28},{12,20},{4,12},{0,4},{9,1},{1... | collective-permute-start | bytes 1671176 | tf_op jit(solution)/shard_map/ppermute | solution.py:174
  47.2 33.8 %collective-permute-start.2 = (bf16[1088,256]{1,0:T(8,128)(2,1)}, bf16[1088,256]{1,0:T(8,128)(2,1)}, u32[]{:S(2)}, u32[]{:S(2)}) collective-permute-start(bf16[1088,256]{1,0:T(8,128)(2,1)} %collective-permute-done.refs_1_), channel_id=1, source_target_pairs={{0,8},{8,16},{16,24},{24,28},{28,20},{20,12},{12,4},{4,0},{1,9},{9... | collective-permute-start | bytes 1671176 | tf_op jit(solution)/shard_map/ppermute | solution.py:173
  57.1 25.9 %collective-permute-start.3 = (bf16[1088,256]{1,0:T(8,128)(2,1)}, bf16[1088,256]{1,0:T(8,128)(2,1)S(1)}, u32[]{:S(2)}, u32[]{:S(2)}) collective-permute-start(bf16[1088,256]{1,0:T(8,128)(2,1)} %collective-permute-done.1.refs_2_), channel_id=1, source_target_pairs={{8,0},{16,8},{24,16},{28,24},{20,28},{12,20},{4,12},{0,4},{9,1},{1... | collective-permute-start | bytes 1671176 | tf_op jit(solution)/shard_map/ppermute | solution.py:174
  59.2 33.7 %collective-permute-start.13 = (bf16[1088,256]{1,0:T(8,128)(2,1)}, bf16[1088,256]{1,0:T(8,128)(2,1)S(1)}, u32[]{:S(2)}, u32[]{:S(2)}) collective-permute-start(bf16[1088,256]{1,0:T(8,128)(2,1)} %collective-permute-done.11.refs_1_), channel_id=1, source_target_pairs={{0,8},{8,16},{16,24},{24,28},{28,20},{20,12},{12,4},{4,0},{1,9},{9... | collective-permute-start | bytes 1671176 | tf_op jit(solution)/shard_map/ppermute | solution.py:173
  69.1 25.8 %collective-permute-start.14 = (bf16[1088,256]{1,0:T(8,128)(2,1)}, bf16[1088,256]{1,0:T(8,128)(2,1)S(1)}, u32[]{:S(2)}, u32[]{:S(2)}) collective-permute-start(bf16[1088,256]{1,0:T(8,128)(2,1)} %collective-permute-done.12.refs_2_), channel_id=1, source_target_pairs={{8,0},{16,8},{24,16},{28,24},{20,28},{12,20},{4,12},{0,4},{9,1},{1... | collective-permute-start | bytes 1671176 | tf_op jit(solution)/shard_map/ppermute | solution.py:174
  71.1 33.7 %collective-permute-start.24 = (bf16[1088,256]{1,0:T(8,128)(2,1)}, bf16[1088,256]{1,0:T(8,128)(2,1)S(1)}, u32[]{:S(2)}, u32[]{:S(2)}) collective-permute-start(bf16[1088,256]{1,0:T(8,128)(2,1)} %collective-permute-done.22.refs_1_), channel_id=1, source_target_pairs={{0,8},{8,16},{16,24},{24,28},{28,20},{20,12},{12,4},{4,0},{1,9},{9... | collective-permute-start | bytes 1671176 | tf_op jit(solution)/shard_map/ppermute | solution.py:173
  81.0 25.8 %collective-permute-start.25 = (bf16[1088,256]{1,0:T(8,128)(2,1)}, bf16[1088,256]{1,0:T(8,128)(2,1)S(1)}, u32[]{:S(2)}, u32[]{:S(2)}) collective-permute-start(bf16[1088,256]{1,0:T(8,128)(2,1)} %collective-permute-done.23.refs_2_), channel_id=1, source_target_pairs={{8,0},{16,8},{24,16},{28,24},{20,28},{12,20},{4,12},{0,4},{9,1},{1... | collective-permute-start | bytes 1671176 | tf_op jit(solution)/shard_map/ppermute | solution.py:174
  83.0 33.7 %collective-permute-start.35 = (bf16[1088,256]{1,0:T(8,128)(2,1)}, bf16[1088,256]{1,0:T(8,128)(2,1)S(1)}, u32[]{:S(2)}, u32[]{:S(2)}) collective-permute-start(bf16[1088,256]{1,0:T(8,128)(2,1)} %collective-permute-done.33.refs_1_), channel_id=1, source_target_pairs={{0,8},{8,16},{16,24},{24,28},{28,20},{20,12},{12,4},{4,0},{1,9},{9... | collective-permute-start | bytes 1671176 | tf_op jit(solution)/shard_map/ppermute | solution.py:173
  92.8 25.9 %collective-permute-start.36 = (bf16[1088,256]{1,0:T(8,128)(2,1)}, bf16[1088,256]{1,0:T(8,128)(2,1)S(1)}, u32[]{:S(2)}, u32[]{:S(2)}) collective-permute-start(bf16[1088,256]{1,0:T(8,128)(2,1)} %collective-permute-done.34.refs_2_), channel_id=1, source_target_pairs={{8,0},{16,8},{24,16},{28,24},{20,28},{12,20},{4,12},{0,4},{9,1},{1... | collective-permute-start | bytes 1671176 | tf_op jit(solution)/shard_map/ppermute | solution.py:174
  94.9 33.8 %collective-permute-start.4 = (bf16[1088,256]{1,0:T(8,128)(2,1)}, bf16[1088,256]{1,0:T(8,128)(2,1)S(1)}, u32[]{:S(2)}, u32[]{:S(2)}) collective-permute-start(bf16[1088,256]{1,0:T(8,128)(2,1)} %collective-permute-done.2.refs_3_), channel_id=1, source_target_pairs={{0,8},{8,16},{16,24},{24,28},{28,20},{20,12},{12,4},{4,0},{1,9},{9... | collective-permute-start | bytes 1671176 | tf_op jit(solution)/shard_map/ppermute | solution.py:173
  104.8 25.9 %collective-permute-start.5 = (bf16[1088,256]{1,0:T(8,128)(2,1)S(1)}, bf16[1088,256]{1,0:T(8,128)(2,1)S(1)}, u32[]{:S(2)}, u32[]{:S(2)}) collective-permute-start(bf16[1088,256]{1,0:T(8,128)(2,1)S(1)} %collective-permute-done.3.refs_4_), channel_id=1, source_target_pairs={{8,0},{16,8},{24,16},{28,24},{20,28},{12,20},{4,12},{0,4},{9,1},{1... | collective-permute-start | bytes 1671176 | tf_op jit(solution)/shard_map/ppermute | solution.py:174
  106.8 35.8 %collective-permute-start.16 = (bf16[1088,256]{1,0:T(8,128)(2,1)S(1)}, bf16[1088,256]{1,0:T(8,128)(2,1)S(1)}, u32[]{:S(2)}, u32[]{:S(2)}) collective-permute-start(bf16[1088,256]{1,0:T(8,128)(2,1)S(1)} %collective-permute-done.14.refs_4_), channel_id=1, source_target_pairs={{8,0},{16,8},{24,16},{28,24},{20,28},{12,20},{4,12},{0,4},{9,1},{1... | collective-permute-start | bytes 1671176 | tf_op jit(solution)/shard_map/ppermute | solution.py:174
  116.7 26.8 %collective-permute-start.15 = (bf16[1088,256]{1,0:T(8,128)(2,1)S(1)}, bf16[1088,256]{1,0:T(8,128)(2,1)S(1)}, u32[]{:S(2)}, u32[]{:S(2)}) collective-permute-start(bf16[1088,256]{1,0:T(8,128)(2,1)S(1)} %collective-permute-done.13.refs_3_), channel_id=1, source_target_pairs={{0,8},{8,16},{16,24},{24,28},{28,20},{20,12},{12,4},{4,0},{1,9},{9... | collective-permute-start | bytes 1671176 | tf_op jit(solution)/shard_map/ppermute | solution.py:173
  118.8 33.8 %collective-permute-start.26 = (bf16[1088,256]{1,0:T(8,128)(2,1)S(1)}, bf16[1088,256]{1,0:T(8,128)(2,1)S(1)}, u32[]{:S(2)}, u32[]{:S(2)}) collective-permute-start(bf16[1088,256]{1,0:T(8,128)(2,1)S(1)} %collective-permute-done.24.refs_3_), channel_id=1, source_target_pairs={{0,8},{8,16},{16,24},{24,28},{28,20},{20,12},{12,4},{4,0},{1,9},{9... | collective-permute-start | bytes 1671176 | tf_op jit(solution)/shard_map/ppermute | solution.py:173
  128.7 25.9 %collective-permute-start.27 = (bf16[1088,256]{1,0:T(8,128)(2,1)S(1)}, bf16[1088,256]{1,0:T(8,128)(2,1)S(1)}, u32[]{:S(2)}, u32[]{:S(2)}) collective-permute-start(bf16[1088,256]{1,0:T(8,128)(2,1)S(1)} %collective-permute-done.25.refs_4_), channel_id=1, source_target_pairs={{8,0},{16,8},{24,16},{28,24},{20,28},{12,20},{4,12},{0,4},{9,1},{1... | collective-permute-start | bytes 1671176 | tf_op jit(solution)/shard_map/ppermute | solution.py:174
  130.7 33.8 %collective-permute-start.37 = (bf16[1088,256]{1,0:T(8,128)(2,1)S(1)}, bf16[1088,256]{1,0:T(8,128)(2,1)S(1)}, u32[]{:S(2)}, u32[]{:S(2)}) collective-permute-start(bf16[1088,256]{1,0:T(8,128)(2,1)S(1)} %collective-permute-done.35.refs_3_), channel_id=1, source_target_pairs={{0,8},{8,16},{16,24},{24,28},{28,20},{20,12},{12,4},{4,0},{1,9},{9... | collective-permute-start | bytes 1671176 | tf_op jit(solution)/shard_map/ppermute | solution.py:173
  143.5 26.6 %collective-permute-start.6 = (bf16[512,256]{1,0:T(8,128)(2,1)S(1)}, bf16[512,256]{1,0:T(8,128)(2,1)S(1)}, u32[]{:S(2)}, u32[]{:S(2)}) collective-permute-start(bf16[512,256]{1,0:T(8,128)(2,1)S(1)} %slice.162), channel_id=1, source_target_pairs={{0,8},{8,16},{16,24},{24,28},{28,20},{20,12},{12,4},{4,0},{1,9},{9... | collective-permute-start | bytes 786440 | tf_op jit(solution)/shard_map/ppermute | solution.py:177
  154.6 29.6 %collective-permute-start.18 = (bf16[576,256]{1,0:T(8,128)(2,1)}, bf16[576,256]{1,0:T(8,128)(2,1)S(1)}, u32[]{:S(2)}, u32[]{:S(2)}) collective-permute-start(bf16[576,256]{1,0:T(8,128)(2,1)} %slice.165), channel_id=1, source_target_pairs={{8,0},{16,8},{24,16},{28,24},{20,28},{12,20},{4,12},{0,4},{9,1},{1... | collective-permute-start | bytes 884744 | tf_op jit(solution)/shard_map/ppermute | solution.py:178
  172.8 26.9 %collective-permute-start.39 = (bf16[512,256]{1,0:T(8,128)(2,1)}, bf16[512,256]{1,0:T(8,128)(2,1)S(1)}, u32[]{:S(2)}, u32[]{:S(2)}) collective-permute-start(bf16[512,256]{1,0:T(8,128)(2,1)} %slice.168), channel_id=1, source_target_pairs={{0,8},{8,16},{16,24},{24,28},{28,20},{20,12},{12,4},{4,0},{1,9},{9... | collective-permute-start | bytes 786440 | tf_op jit(solution)/shard_map/ppermute | solution.py:177
  182.2 26.7 %collective-permute-start.8 = (bf16[1024,128]{1,0:T(8,128)(2,1)S(1)}, bf16[1024,128]{1,0:T(8,128)(2,1)S(1)}, u32[]{:S(2)}, u32[]{:S(2)}) collective-permute-start(bf16[1024,128]{1,0:T(8,128)(2,1)S(1)} %attend.4.refs_0_), channel_id=1, source_target_pairs={{0,2},{1,3},{2,0},{3,1},{4,6},{5,7},{6,4},{7,5},{8,10},{9,11},{10,... | collective-permute-start | bytes 786440 | tf_op jit(solution)/shard_map/ppermute | solution.py:233
  184.2 24.8 %collective-permute-start.9 = (bf16[1024,128]{1,0:T(8,128)(2,1)S(1)}, bf16[1024,128]{1,0:T(8,128)(2,1)S(1)}, u32[]{:S(2)}, u32[]{:S(2)}) collective-permute-start(bf16[1024,128]{1,0:T(8,128)(2,1)S(1)} %attend.4.refs_0_), channel_id=1, source_target_pairs={{0,1},{1,0},{2,3},{3,2},{4,5},{5,4},{6,7},{7,6},{8,9},{9,8},{10,11... | collective-permute-start | bytes 786440 | tf_op jit(solution)/shard_map/ppermute | solution.py:234
  (40 other events, 838.5 us)

commit v2 on v1

--- a/solution.py
+++ b/solution.py
@@ -18,67 +18,151 @@
     return [2 * i for i in range(half)] + [2 * i + 1 for i in reversed(range(half))]
 
 
-def kv_kernel(tokens_ref, wk_ref, wv_ref, start_ref, end_ref, out_ref):
+def kv_kernel(token_rows, heads, tokens_ref, wk_ref, wv_ref, start_ref, end_ref, own_ref, chunk_ref, w_ref):
     tok_rows = tokens_ref.shape[0]
     share = start_ref.shape[0]
-    weight = jnp.concatenate([wk_ref[...], wv_ref[...]], axis=1)
-    kv = jnp.dot(tokens_ref[...], weight, preferred_element_type=jnp.float32).astype(jnp.bfloat16)
-    out_ref[:tok_rows, :] = kv
+    for head in range(heads):
+        at = slice(head * HD, (head + 1) * HD)
+        w_ref[:, 2 * head * HD : (2 * head + 1) * HD] = wk_ref[:, at]
+        w_ref[:, (2 * head + 1) * HD : (2 * head + 2) * HD] = wv_ref[:, at]
+    kv = jnp.dot(tokens_ref[...], w_ref[...], preferred_element_type=jnp.float32)
+    kv = kv.astype(jnp.bfloat16)
+    own_ref[...] = kv[:token_rows]
+    chunk_ref[: tok_rows - token_rows, :] = kv[token_rows:]
     position = lax.broadcasted_iota(jnp.int32, (share, tok_rows), 1)
     start = start_ref[...]
     end = end_ref[...]
     member = ((position >= start) & (position < end)).astype(jnp.float32).astype(jnp.bfloat16)
     sums = jnp.dot(member, kv, preferred_element_type=jnp.float32)
     counts = (end - start).astype(jnp.float32)
-    out_ref[tok_rows:, :] = (sums / counts).astype(jnp.bfloat16)
-
-
-def project_kv(tokens, w_key, w_value, start, end, head):
+    chunk_ref[tok_rows - token_rows :, :] = (sums / counts).astype(jnp.bfloat16)
+
+
+def project_kv(tokens, w_key, w_value, start, end, token_rows, group, heads):
     tok_rows, width = tokens.shape
     share = start.shape[0]
+    columns = 2 * heads * HD
+    sent = tok_rows - token_rows + share
     return pl.pallas_call(
-        kv_kernel,
+        functools.partial(kv_kernel, token_rows, heads),
         grid=(1,),
         in_specs=[
             pl.BlockSpec((tok_rows, width), lambda i: (0, 0)),
-            pl.BlockSpec((width, HD), lambda i: (0, head)),
-            pl.BlockSpec((width, HD), lambda i: (0, head)),
+            pl.BlockSpec((width, heads * HD), lambda i: (0, group)),
+            pl.BlockSpec((width, heads * HD), lambda i: (0, group)),
             pl.BlockSpec((share, 1), lambda i: (0, 0)),
             pl.BlockSpec((share, 1), lambda i: (0, 0)),
         ],
-        out_specs=pl.BlockSpec((tok_rows + share, 2 * HD), lambda i: (0, 0)),
-        out_shape=jax.ShapeDtypeStruct((tok_rows + share, 2 * HD), jnp.bfloat16),
-        compiler_params=pltpu.CompilerParams(vmem_limit_bytes=40 * MIB),
+        out_specs=[
+            pl.BlockSpec((token_rows, columns), lambda i: (0, 0)),
+            pl.BlockSpec((sent, columns), lambda i: (0, 0)),
+            pl.BlockSpec((width, columns), lambda i: (0, 0)),
+        ],
+        out_shape=[
+            jax.ShapeDtypeStruct((token_rows, columns), jnp.bfloat16),
+            jax.ShapeDtypeStruct((sent, columns), jnp.bfloat16),
+            jax.ShapeDtypeStruct((width, columns), jnp.bfloat16),
+        ],
+        compiler_params=pltpu.CompilerParams(vmem_limit_bytes=48 * MIB),
         cost_estimate=pl.CostEstimate(
-            flops=2 * tok_rows * width * 2 * HD, bytes_accessed=6 * MIB, transcendentals=0
+            flops=2 * tok_rows * width * columns, bytes_accessed=10 * MIB, transcendentals=0
         ),
         name="project_kv",
     )(tokens, w_key, w_value, start, end)
 
 
-def attend_kernel(devices, table_ref, owner_ref, q_ref, *refs):
+def rows_kernel(runs, piece, count, parts, group_ref, *refs):
+    sources = refs[:parts]
+    weights = refs[parts : parts + count]
+    outs = refs[parts + count : parts + 2 * count]
+    held = refs[parts + 2 * count : 2 * parts + 2 * count]
+    held_weights, sems = refs[2 * parts + 2 * count :]
+    columns = held_weights.shape[1] // count
+    copies = []
+    for at in range(count):
+        copies.append((weights[at], held_weights.at[:, pl.ds(at * columns, columns)]))
+    copies += [(source, held[at]) for at, source in enumerate(sources)]
+    started = []
+    for at, (source, target) in enumerate(copies):
+        started.append(pltpu.make_async_copy(source, target, sems.at[at]))
+        started[-1].start()
+    for at in range(count):
+        started[at].wait()
+    for at in range(parts):
+        started[count + at].wait()
+        rows = jnp.dot(held[at][...], held_weights[...], preferred_element_type=jnp.float32)
+        rows = rows.astype(jnp.bfloat16)
+        flip = at if parts == 4 else at // 2
+        first = 0 if parts == 4 else (at % 2) * (piece // 2)
+        slot = group_ref[flip]
+        for run in range(runs):
+            size = rows.shape[0] // runs
+            base = pl.multiple_of(run * 4 * piece + slot * piece + first, 16)
+            for to in range(count):
+                outs[to][pl.ds(base, size), :] = rows[
+                    run * size : (run + 1) * size, to * columns : (to + 1) * columns
+                ]
+
+
+def project_rows(parts, weights, slots, runs, piece):
+    width = parts[0].shape[1]
+    columns = weights[0].shape[1]
+    count = len(weights)
+    rows = runs * 4 * piece
+    any_spec = pl.BlockSpec(memory_space=pl.ANY)
+    return pl.pallas_call(
+        functools.partial(rows_kernel, runs, piece, count, len(parts)),
+        grid=(1,),
+        in_specs=[pl.BlockSpec(memory_space=pltpu.SMEM)] + [any_spec] * (len(parts) + count),
+        out_specs=[pl.BlockSpec((rows, columns), lambda i: (0, 0))] * count,
+        out_shape=[jax.ShapeDtypeStruct((rows, columns), jnp.bfloat16)] * count,
+        scratch_shapes=[pltpu.VMEM(part.shape, jnp.bfloat16) for part in parts]
+        + [
+            pltpu.VMEM((width, count * columns), jnp.bfloat16),
+            pltpu.SemaphoreType.DMA((len(parts) + count,)),
+        ],
+        compiler_params=pltpu.CompilerParams(vmem_limit_bytes=48 * MIB),
+        cost_estimate=pl.CostEstimate(
+            flops=2 * rows * width * count * columns, bytes_accessed=12 * MIB, transcendentals=0
+        ),
+        name="project_rows",
+    )(slots, *parts, *weights)
+
+
+def attend_kernel(devices, token_rows, column, table_ref, owner_ref, q_ref, own_ref, *refs):
     buffers = refs[: devices + 1]
-    out_ref, kv, summary, sems = refs[devices + 1 :]
+    steps = devices // 2
+    projected = refs[devices + 1 : devices + 1 + steps]
+    out_ref, kv, summary, sems = refs[devices + 1 + steps :]
     tok_rows = q_ref.shape[0]
-    half = tok_rows // 2
+    sent = tok_rows - token_rows
     share = summary.shape[0] // devices
+    half = buffers[devices - 1].shape[0]
+    columns = pl.ds(column, 2 * HD)
     copies = []
 
-    def copy(source, target):
-        done = pltpu.make_async_copy(source, target, sems.at[len(copies)])
+    def copy(source, first, rows, target, base):
+        done = pltpu.make_async_copy(
+            source.at[pl.ds(first, rows), columns],
+            target.at[pl.ds(pl.multiple_of(base, 16), rows)],
+            sems.at[len(copies)],
+        )
         done.start()
         copies.append(done)
 
+    copy(own_ref, 0, token_rows, kv, owner_ref[0] * tok_rows)
+    for step in range(1, steps + 1):
+        for run in range(2 if step < steps else 1):
+            owner = owner_ref[2 * step - 1 + run]
+            copy(projected[step - 1], run * token_rows, token_rows, kv, owner * tok_rows)
     for at, buffer in enumerate(buffers):
         owner = owner_ref[min(at, devices - 1)]
         first = half if at == devices else 0
-        rows = tok_rows if at < devices - 1 else half
-        base = pl.multiple_of(owner * tok_rows + first, BLK)
-        copy(buffer.at[pl.ds(0, rows)], kv.at[pl.ds(base, rows)])
+        rows = half if at == devices - 1 else sent - first
+        copy(buffer, 0, rows, kv, owner * tok_rows + token_rows + first)
         if at != devices - 1:
             segment = lax.rem(owner + devices // 2, devices)
-            base = pl.multiple_of(segment * share, 16)
-            copy(buffer.at[pl.ds(rows, share)], summary.at[pl.ds(base, share)])
+            copy(buffer, rows, share, summary, segment * share)
     for done in copies:
         done.wait()
     factor = HD**-0.5 * float(np.log2(np.e))
@@ -110,21 +194,21 @@
     lax.fori_loop(0, tok_rows // BLK, one_block, 0)
 
 
-def attend(table, owner_ids, queries, buffers, head, devices, share):
+def attend(table, owner_ids, queries, own, buffers, projected, head, column, devices, share):
     tok_rows = queries.shape[0]
     any_spec = pl.BlockSpec(memory_space=pl.ANY)
     smem = pl.BlockSpec(memory_space=pltpu.SMEM)
     return pl.pallas_call(
-        functools.partial(attend_kernel, devices),
+        functools.partial(attend_kernel, devices, own.shape[0], column),
         grid=(1,),
         in_specs=[smem, smem, pl.BlockSpec((tok_rows, HD), lambda i: (0, head))]
-        + [any_spec] * len(buffers),
+        + [any_spec] * (1 + len(buffers) + len(projected)),
         out_specs=pl.BlockSpec((tok_rows, HD), lambda i: (0, 0)),
         out_shape=jax.ShapeDtypeStruct((tok_rows, HD), jnp.bfloat16),
         scratch_shapes=[
             pltpu.VMEM((devices * tok_rows, 2 * HD), jnp.bfloat16),
             pltpu.VMEM((devices * share, 2 * HD), jnp.bfloat16),
-            pltpu.SemaphoreType.DMA((2 * devices + 1,)),
+            pltpu.SemaphoreType.DMA((3 * devices + 1,)),
         ],
         compiler_params=pltpu.CompilerParams(vmem_limit_bytes=48 * MIB),
         cost_estimate=pl.CostEstimate(
@@ -133,7 +217,7 @@
             transcendentals=tok_rows * 1152,
         ),
         name="attend",
-    )(table, owner_ids, queries, *buffers)
+    )(table, owner_ids, queries, own, *buffers, *projected)
 
 
 def out_kernel(pieces, *refs):
@@ -163,7 +247,7 @@
     )(*pieces, weight)
 
 
-def ring_gather(chunk, tok_rows, devices):
+def ring_gather(chunk, half, devices):
     order = ring_order(devices)
     forward = [(order[p], order[(p + 1) % devices]) for p in range(devices)]
     backward = [(target, source) for source, target in forward]
@@ -173,7 +257,6 @@
         ahead = lax.ppermute(ahead, "seq", forward)
         behind = lax.ppermute(behind, "seq", backward)
         buffers += [ahead, behind]
-    half = tok_rows // 2
     buffers.append(lax.ppermute(ahead[:half], "seq", forward))
     buffers.append(lax.ppermute(behind[half:], "seq", backward))
     return buffers
@@ -211,31 +294,65 @@
     start = lax.dynamic_slice_in_dim(seg_start, first_segment, share, 0) - me * tok_rows
     end = lax.dynamic_slice_in_dim(seg_end, first_segment, share, 0) - me * tok_rows
 
-    gathered = [
-        ring_gather(
-            project_kv(tokens, w_key, w_value, start[:, None], end[:, None], head),
-            tok_rows,
-            devices,
-        )
-        for head in range(heads)
-    ]
+    across = [(g, g ^ 2) for g in range(groups)]
+    beside = [(g, g ^ 1) for g in range(groups)]
+    token_rows = tok_rows * 5 // 8
+    piece = token_rows // groups
+    group_heads = 2
+    slots = group ^ jnp.arange(4, dtype=jnp.int32)
+
+    own_piece = lax.dynamic_slice_in_dim(tokens, group * piece, piece, 0)
+    token_ring = ring_gather(own_piece, piece // 2, devices)
+    owns, rings, weights = [], [], []
+    for at in range(heads // group_heads):
+        own, chunk, weight = project_kv(
+            tokens, w_key, w_value, start[:, None], end[:, None], token_rows, at, group_heads
+        )
+        owns.append(own)
+        weights.append(weight)
+        rings.append(ring_gather(chunk, chunk.shape[0] // 32 * 16, devices))
     queries = jnp.dot(tokens, w_query, preferred_element_type=jnp.float32).astype(jnp.bfloat16)
+
+    projected = []
+    for step in range(1, devices // 2 + 1):
+        pair = token_ring[2 * step - 1 : 2 * step + 1]
+        last = step == devices // 2
+        local = jnp.concatenate(pair, axis=0)
+        other = lax.ppermute(local, "head", across)
+        parts = [
+            local,
+            lax.ppermute(local, "head", beside),
+            other,
+            lax.ppermute(other, "head", beside),
+        ]
+        runs = 1 if last else 2
+        projected.append(project_rows(parts, weights, slots, runs, piece))
 
     out_weight = lax.all_to_all(
         w_out.reshape(heads * HD, groups, -1), "head", split_axis=1, concat_axis=0, tiled=True
     ).reshape(groups, heads * HD, -1)
-    across = [(g, g ^ 2) for g in range(groups)]
-    beside = [(g, g ^ 1) for g in range(groups)]
     pieces = []
-    weights = []
+    out_rows = []
     for head in range(heads):
-        own = attend(table, owner_ids, queries, gathered[head], head, devices, share)
+        at, within = divmod(head, group_heads)
+        own = attend(
+            table,
+            owner_ids,
+            queries,
+            owns[at],
+            rings[at],
+            [outs[at] for outs in projected],
+            head,
+            within * 2 * HD,
+            devices,
+            share,
+        )
         other = lax.ppermute(own, "head", across)
         pieces += [own, other, lax.ppermute(own, "head", beside), lax.ppermute(other, "head", beside)]
         for flip in (0, 2, 1, 3):
             rows = lax.dynamic_index_in_dim(out_weight, group ^ flip, 0, keepdims=False)
-            weights.append(rows[head * HD : (head + 1) * HD])
-    return project_out(pieces, jnp.concatenate(weights, axis=0))
+            out_rows.append(rows[head * HD : (head + 1) * HD])
+    return project_out(pieces, jnp.concatenate(out_rows, axis=0))
 
 
 def solution(mesh):

time: 224 us -> 284 us (1.27)
  Pallas kernels: 40.9 us -> 80 us
  waiting for transfers between devices: 90.5 us -> 109 us
  local copies, waits for them, and re-layouts: 26.6 us -> 39.9 us
  starting transfers between devices: 60.9 us -> 48.6 us
    ppermute x0 -> x8, waiting for transfers between devices: none -> 53.9 us  [the longest x4 53.9 us: per_device(): other = lax.ppermute(local, 'head', across)]
    ppermute x12 -> x9, waiting for transfers between devices: 72.8 us -> 29.2 us  [ring_gather(): ahead = lax.ppermute(ahead, 'seq', forward)]
    pallas_call x8 -> x10, Pallas kernels: 37.3 us -> 76.4 us  [the longest x4 33.3 us: project_rows(): pl.pallas_call(functools.partial(rows_kernel, runs, piece, count, len(par...]
    unnamed x56 -> x94, local copies, waits for them, and re-layouts: 15.5 us -> 23 us
    ppermute x0 -> x8, starting transfers between devices: none -> 7.11 us  [the longest x4 6.47 us: per_device(): other = lax.ppermute(local, 'head', across)]
    ppermute x12 -> x9, starting transfers between devices: 15.2 us -> 8.32 us  [ring_gather(): behind = lax.ppermute(behind, 'seq', backward)]
    ppermute x12 -> x9, starting transfers between devices: 22.1 us -> 15.9 us  [ring_gather(): ahead = lax.ppermute(ahead, 'seq', forward)]
    ppermute x12 -> x9, waiting for transfers between devices: 11.1 us -> 15.6 us  [ring_gather(): behind = lax.ppermute(behind, 'seq', backward)]
  transfers between devices with their start and end apart: 45 -> 49, of which waited for: 21 -> 16; matrix products, arithmetic and copies ran while one was open for 7% -> 9% of each run, Pallas kernels for 17% -> 27%
where the time goes in v2:
time: 284 us; the launch traced here: 283 us
  waiting for transfers between devices  109 us (38%)
  Pallas kernels  80 us (28%)
  starting transfers between devices  48.6 us (17%)
  local copies, waits for them, and re-layouts  39.9 us (14%)
  matrix products  3.29 us (1%)
    ppermute x4, waiting for transfers between devices, per_device(): other = lax.ppermute(local, 'head', across)  53.9 us
    pallas_call x4, Pallas kernels, project_rows(): pl.pallas_call(functools.partial(rows_kernel, runs, piece, count, len(par...  33.3 us
    pallas_call x4, Pallas kernels, attend(): pl.pallas_call(functools.partial(attend_kernel, devices, own.shape[0], co...  30.6 us
    ppermute x9, waiting for transfers between devices, ring_gather(): ahead = lax.ppermute(ahead, 'seq', forward)  29.2 us
    unnamed x94, local copies, waits for them, and re-layouts  23 us
    ppermute x9, starting transfers between devices, ring_gather(): ahead = lax.ppermute(ahead, 'seq', forward)  15.9 us
    ppermute x9, waiting for transfers between devices, ring_gather(): behind = lax.ppermute(behind, 'seq', backward)  15.6 us
    pallas_call x2, Pallas kernels, project_kv(): pl.pallas_call(functools.partial(kv_kernel, token_rows, heads), grid=(1,)...  12.5 us
  transfers between devices with their start and end apart: 49, of which 16 were waited for; matrix products, arithmetic and copies ran while one was open for 9% of the time, Pallas kernels for 27%

profile of v2, /device:TPU:0, one launch (start us, length us, event | category | flops | bytes accessed | tf_op | source)
XLA Modules:
  0.0 282.9 jit_solution(5255782630506472891)
XLA Ops:
  2.1 3.0 %collective-permute-start.8 = (bf16[160,2048]{1,0:T(8,128)(2,1)}, bf16[160,2048]{1,0:T(8,128)(2,1)}, u32[]{:S(2)}, u32[]{:S(2)}) collective-permute-start(bf16[160,2048]{1,0:T(8,128)(2,1)} %constant_dynamic-slice_fusion), channel_id=1, source_target_pairs={{0,8},{8,16},{16,24},{24,28},{28,20},{20,12},{12,4},{4,0},{1,9},{9... | collective-permute-start | bytes 1966088 | tf_op jit(solution)/shard_map/ppermute | solution.py:257
  7.7 6.2 %project_kv.3 = (bf16[640,512]{1,0:T(8,128)(2,1)S(1)}, bf16[448,512]{1,0:T(8,128)(2,1)}, bf16[2048,512]{1,0:T(8,128)(2,1)S(1)}) custom-call(bf16[1024,2048]{1,0:T(8,128)(2,1)} %tokens_ref.3, bf16[2048,512]{1,0:T(8,128)(2,1)S(1)} %copy-done.2, bf16[2048,512]{1,0:T(8,128)(2,1)} %wv_ref.3, s32[64,1]{1,0:T(8,128)S(1)} %copy.25.start_ref, s32[64,1]{1,0:T(8,128)S(1)} %copy.26.end_ref), custom_call_target="tpu_custom_call" | custom-call | flops 2147483648 | bytes 10485760 | tf_op jit(solution)/shard_map/project_kv/pallas_call | solution.py:46
  17.6 4.5 %all-to-all-start = ((bf16[512,4,512]{2,0,1:T(8,128)(2,1)}), bf16[512,4,512]{2,0,1:T(8,128)(2,1)}, u32[]{:S(2)}, u32[]{:S(2)}) async-start(bf16[512,4,512]{2,0,1:T(8,128)(2,1)} %bitcast.83), calls=%async_computation | async-start | bytes 4194304 | tf_op jit(solution)/shard_map/all_to_all | solution.py:331
  23.7 6.2 %project_kv.2 = (bf16[640,512]{1,0:T(8,128)(2,1)S(1)}, bf16[448,512]{1,0:T(8,128)(2,1)}, bf16[2048,512]{1,0:T(8,128)(2,1)S(1)}) custom-call(bf16[1024,2048]{1,0:T(8,128)(2,1)} %tokens_ref.3, bf16[2048,512]{1,0:T(8,128)(2,1)S(1)} %copy-done.3, bf16[2048,512]{1,0:T(8,128)(2,1)} %wv_ref.3, s32[64,1]{1,0:T(8,128)S(1)} %copy.25.start_ref, s32[64,1]{1,0:T(8,128)S(1)} %copy.26.end_ref), custom_call_target="tpu_custom_call" | custom-call | flops 2147483648 | bytes 10485760 | tf_op jit(solution)/shard_map/project_kv/pallas_call | solution.py:46
  33.4 3.3 %convolution_convert_fusion.q_ref = bf16[1024,512]{1,0:T(8,128)(2,1)} fusion(bf16[1024,2048]{1,0:T(8,128)(2,1)S(1)} %copy-done.26, bf16[2048,512]{1,0:T(8,128)(2,1)S(1)} %copy-done), kind=kOutput, calls=%fused_computation.2 | convolution fusion | flops 2148007936 | bytes 7340032 | tf_op jit(solution)/shard_map/dot_general | solution.py:314
  47.0 4.2 %collective-permute-done.1.refs_2_ = bf16[448,512]{1,0:T(8,128)(2,1)S(1)} collective-permute-done((bf16[448,512]{1,0:T(8,128)(2,1)}, bf16[448,512]{1,0:T(8,128)(2,1)S(1)}, u32[]{:S(2)}, u32[]{:S(2)}) %collective-permute-start.1) | collective-permute-done | bytes 458784 | tf_op jit(solution)/shard_map/ppermute | solution.py:258
  62.6 16.1 %collective-permute-done.2.refs_3_ = bf16[448,512]{1,0:T(8,128)(2,1)S(1)} collective-permute-done((bf16[448,512]{1,0:T(8,128)(2,1)}, bf16[448,512]{1,0:T(8,128)(2,1)S(1)}, u32[]{:S(2)}, u32[]{:S(2)}) %collective-permute-start.2) | collective-permute-done | bytes 458784 | tf_op jit(solution)/shard_map/ppermute | solution.py:257
  89.7 5.0 %collective-permute-done.39.refs_6_ = bf16[448,512]{1,0:T(8,128)(2,1)S(1)} collective-permute-done((bf16[448,512]{1,0:T(8,128)(2,1)S(1)}, bf16[448,512]{1,0:T(8,128)(2,1)S(1)}, u32[]{:S(2)}, u32[]{:S(2)}) %collective-permute-start.39) | collective-permute-done | bytes 458784 | tf_op jit(solution)/shard_map/ppermute | solution.py:258
  100.6 3.2 %collective-permute-done.5.refs_6_ = bf16[448,512]{1,0:T(8,128)(2,1)S(1)} collective-permute-done((bf16[448,512]{1,0:T(8,128)(2,1)S(1)}, bf16[448,512]{1,0:T(8,128)(2,1)S(1)}, u32[]{:S(2)}, u32[]{:S(2)}) %collective-permute-start.5) | collective-permute-done | bytes 458784 | tf_op jit(solution)/shard_map/ppermute | solution.py:258
  106.6 8.4 %collective-permute-done.18 = bf16[160,2048]{1,0:T(8,128)(2,1)} collective-permute-done((bf16[160,2048]{1,0:T(8,128)(2,1)}, bf16[160,2048]{1,0:T(8,128)(2,1)}, u32[]{:S(2)}, u32[]{:S(2)}) %collective-permute-start.18) | collective-permute-done | bytes 655392 | tf_op jit(solution)/shard_map/ppermute | solution.py:257
  117.6 2.6 collective-permute-done.19
  125.8 3.8 %collective-permute-done.24 = bf16[80,2048]{1,0:T(8,128)(2,1)S(1)} collective-permute-done((bf16[80,2048]{1,0:T(8,128)(2,1)S(1)}, bf16[80,2048]{1,0:T(8,128)(2,1)S(1)}, u32[]{:S(2)}, u32[]{:S(2)}) %collective-permute-start.24) | collective-permute-done | bytes 327712 | tf_op jit(solution)/shard_map/ppermute | solution.py:261
  130.8 14.3 %collective-permute-done.16.refs_2_ = bf16[320,2048]{1,0:T(8,128)(2,1)} collective-permute-done((bf16[320,2048]{1,0:T(8,128)(2,1)}, bf16[320,2048]{1,0:T(8,128)(2,1)}, u32[]{:S(2)}, u32[]{:S(2)}) %collective-permute-start.16) | collective-permute-done | bytes 1310752 | tf_op jit(solution)/shard_map/ppermute | solution.py:321
  145.1 39.6 %collective-permute-done.26.refs_2_ = bf16[160,2048]{1,0:T(8,128)(2,1)S(1)} collective-permute-done((bf16[160,2048]{1,0:T(8,128)(2,1)S(1)}, bf16[160,2048]{1,0:T(8,128)(2,1)S(1)}, u32[]{:S(2)}, u32[]{:S(2)}) %collective-permute-start.26) | collective-permute-done | bytes 655392 | tf_op jit(solution)/shard_map/ppermute | solution.py:321
  186.5 9.2 %project_rows.4 = (bf16[1280,512]{1,0:T(8,128)(2,1)S(1)}, bf16[1280,512]{1,0:T(8,128)(2,1)S(1)}) custom-call(s32[4]{0:T(128)S(1)} %iota_xor_fusion.group_ref, bf16[320,2048]{1,0:T(8,128)(2,1)} %constant_dynamic-update-slice_fusion.refs_0_, bf16[320,2048]{1,0:T(8,128)(2,1)} %collective-permute-done.10.refs_1_, ...), custom_call_target="tpu_custom_call" | custom-call | flops 5368709120 | bytes 12582912 | tf_op jit(solution)/shard_map/project_rows/pallas_call | solution.py:113
  203.3 5.9 %project_rows.7 = (bf16[640,512]{1,0:T(8,128)(2,1)S(1)}, bf16[640,512]{1,0:T(8,128)(2,1)S(1)}) custom-call(s32[4]{0:T(128)S(1)} %iota_xor_fusion.group_ref, bf16[160,2048]{1,0:T(8,128)(2,1)S(1)} %constant_dynamic-update-slice_fusion.6.refs_0_, bf16[160,2048]{1,0:T(8,128)(2,1)S(1)} %copy-done.24, bf16[160,2048]{1,0:T(8,128)(2,1)S(1)} %copy-done.22, ...), custom_call_target="tpu_custom_call" | custom-call | flops 2684354560 | bytes 12582912 | tf_op jit(solution)/shard_map/project_rows/pallas_call | solution.py:113
  211.3 9.2 %project_rows.5 = (bf16[1280,512]{1,0:T(8,128)(2,1)S(1)}, bf16[1280,512]{1,0:T(8,128)(2,1)S(1)}) custom-call(s32[4]{0:T(128)S(1)} %iota_xor_fusion.group_ref, bf16[320,2048]{1,0:T(8,128)(2,1)} %constant_dynamic-update-slice_fusion.2.refs_0_, bf16[320,2048]{1,0:T(8,128)(2,1)} %collective-permute-done.15.refs_1_, ...), custom_call_target="tpu_custom_call" | custom-call | flops 5368709120 | bytes 12582912 | tf_op jit(solution)/shard_map/project_rows/pallas_call | solution.py:113
  223.2 8.9 %project_rows.6 = (bf16[1280,512]{1,0:T(8,128)(2,1)S(1)}, bf16[1280,512]{1,0:T(8,128)(2,1)S(1)}) custom-call(s32[4]{0:T(128)S(1)} %iota_xor_fusion.group_ref, bf16[320,2048]{1,0:T(8,128)(2,1)S(1)} %constant_dynamic-update-slice_fusion.4.refs_0_, bf16[320,2048]{1,0:T(8,128)(2,1)S(1)} %collective-permute-done.20.refs_1_, ...), custom_call_target="tpu_custom_call" | custom-call | flops 5368709120 | bytes 12582912 | tf_op jit(solution)/shard_map/project_rows/pallas_call | solution.py:113
  234.4 7.7 %attend.7.refs_12_ = bf16[1024,128]{1,0:T(8,128)(2,1)S(1)} custom-call(s32[8,9]{1,0:T(8,128)S(1)} %pad_add_fusion.table_ref, s32[8]{0:T(128)S(1)} %gather_fusion, bf16[1024,512]{1,0:T(8,128)(2,1)} %convolution_convert_fusion.q_ref, bf16[640,512]{1,0:T(8,128)(2,1)S(1)} %get-tuple-element.27.own_ref, bf16[448,512]{1,0:T(8,128)(2,1)} %get-tuple-element.28.refs_0_, ...), custom_call_target="tpu_custom_call" | custom-call | flops 603979776 | bytes 4194304 | tf_op jit(solution)/shard_map/attend/pallas_call | solution.py:201
  243.6 7.8 %attend.6.refs_8_ = bf16[1024,128]{1,0:T(8,128)(2,1)S(1)} custom-call(s32[8,9]{1,0:T(8,128)S(1)} %pad_add_fusion.table_ref, s32[8]{0:T(128)S(1)} %gather_fusion, bf16[1024,512]{1,0:T(8,128)(2,1)} %convolution_convert_fusion.q_ref, bf16[640,512]{1,0:T(8,128)(2,1)S(1)} %get-tuple-element.27.own_ref, bf16[448,512]{1,0:T(8,128)(2,1)} %get-tuple-element.28.refs_0_, ...), custom_call_target="tpu_custom_call" | custom-call | flops 603979776 | bytes 4194304 | tf_op jit(solution)/shard_map/attend/pallas_call | solution.py:201
  252.4 7.6 %attend.5.refs_4_ = bf16[1024,128]{1,0:T(8,128)(2,1)S(1)} custom-call(s32[8,9]{1,0:T(8,128)S(1)} %pad_add_fusion.table_ref, s32[8]{0:T(128)S(1)} %gather_fusion, bf16[1024,512]{1,0:T(8,128)(2,1)} %convolution_convert_fusion.q_ref, bf16[640,512]{1,0:T(8,128)(2,1)S(1)} %get-tuple-element.19.own_ref, bf16[448,512]{1,0:T(8,128)(2,1)} %get-tuple-element.20.refs_0_, ...), custom_call_target="tpu_custom_call" | custom-call | flops 603979776 | bytes 4194304 | tf_op jit(solution)/shard_map/attend/pallas_call | solution.py:201
  261.4 7.6 %attend.4.refs_0_ = bf16[1024,128]{1,0:T(8,128)(2,1)S(1)} custom-call(s32[8,9]{1,0:T(8,128)S(1)} %pad_add_fusion.table_ref, s32[8]{0:T(128)S(1)} %gather_fusion, bf16[1024,512]{1,0:T(8,128)(2,1)} %convolution_convert_fusion.q_ref, bf16[640,512]{1,0:T(8,128)(2,1)S(1)} %get-tuple-element.19.own_ref, bf16[448,512]{1,0:T(8,128)(2,1)} %get-tuple-element.20.refs_0_, ...), custom_call_target="tpu_custom_call" | custom-call | flops 603979776 | bytes 4194304 | tf_op jit(solution)/shard_map/attend/pallas_call | solution.py:201
  272.8 5.0 %collective-permute-done.28.refs_1_ = bf16[1024,128]{1,0:T(8,128)(2,1)S(1)} collective-permute-done((bf16[1024,128]{1,0:T(8,128)(2,1)S(1)}, bf16[1024,128]{1,0:T(8,128)(2,1)S(1)}, u32[]{:S(2)}, u32[]{:S(2)}) %collective-permute-start.28) | collective-permute-done | bytes 262176 | tf_op jit(solution)/shard_map/ppermute | solution.py:350
  279.3 3.6 %project_out.1 = bf16[1024,512]{1,0:T(8,128)(2,1)} custom-call(bf16[1024,128]{1,0:T(8,128)(2,1)S(1)} %attend.4.refs_0_, bf16[1024,128]{1,0:T(8,128)(2,1)S(1)} %collective-permute-done.28.refs_1_, bf16[1024,128]{1,0:T(8,128)(2,1)S(1)} %collective-permute-done.29.refs_2_, bf16[1024,128]{1,0:T(8,128)(2,1)S(1)} %collective-permute-done.30.refs_3_, ...), custom_call_target="tpu_custom_call" | custom-call | flops 2147483648 | bytes 7340032 | tf_op jit(solution)/shard_map/project_out/pallas_call | solution.py:235
  (204 shorter events, 89.3 us)
Async XLA Ops:
  2.1 38.8 %collective-permute-start.8 = (bf16[160,2048]{1,0:T(8,128)(2,1)}, bf16[160,2048]{1,0:T(8,128)(2,1)}, u32[]{:S(2)}, u32[]{:S(2)}) collective-permute-start(bf16[160,2048]{1,0:T(8,128)(2,1)} %constant_dynamic-slice_fusion), channel_id=1, source_target_pairs={{0,8},{8,16},{16,24},{24,28},{28,20},{20,12},{12,4},{4,0},{1,9},{9... | collective-permute-start | bytes 1966088 | tf_op jit(solution)/shard_map/ppermute | solution.py:257
  5.2 47.6 %collective-permute-start.9 = (bf16[160,2048]{1,0:T(8,128)(2,1)}, bf16[160,2048]{1,0:T(8,128)(2,1)}, u32[]{:S(2)}, u32[]{:S(2)}) collective-permute-start(bf16[160,2048]{1,0:T(8,128)(2,1)} %constant_dynamic-slice_fusion), channel_id=1, source_target_pairs={{8,0},{16,8},{24,16},{28,24},{20,28},{12,20},{4,12},{0,4},{9,1},{1... | collective-permute-start | bytes 1966088 | tf_op jit(solution)/shard_map/ppermute | solution.py:258
  17.6 87.2 %all-to-all-start = ((bf16[512,4,512]{2,0,1:T(8,128)(2,1)}), bf16[512,4,512]{2,0,1:T(8,128)(2,1)}, u32[]{:S(2)}, u32[]{:S(2)}) async-start(bf16[512,4,512]{2,0,1:T(8,128)(2,1)} %bitcast.83), calls=%async_computation | async-start | bytes 4194304 | tf_op jit(solution)/shard_map/all_to_all | solution.py:331
  41.0 39.8 %collective-permute-start.13 = (bf16[160,2048]{1,0:T(8,128)(2,1)}, bf16[160,2048]{1,0:T(8,128)(2,1)}, u32[]{:S(2)}, u32[]{:S(2)}) collective-permute-start(bf16[160,2048]{1,0:T(8,128)(2,1)} %collective-permute-done.8), channel_id=1, source_target_pairs={{0,8},{8,16},{16,24},{24,28},{28,20},{20,12},{12,4},{4,0},{1,9},{9... | collective-permute-start | bytes 1966088 | tf_op jit(solution)/shard_map/ppermute | solution.py:257
  51.2 27.5 %collective-permute-start.2 = (bf16[448,512]{1,0:T(8,128)(2,1)}, bf16[448,512]{1,0:T(8,128)(2,1)S(1)}, u32[]{:S(2)}, u32[]{:S(2)}) collective-permute-start(bf16[448,512]{1,0:T(8,128)(2,1)} %collective-permute-done.refs_1_), channel_id=1, source_target_pairs={{0,8},{8,16},{16,24},{24,28},{28,20},{20,12},{12,4},{4,0},{1,9},{9... | collective-permute-start | bytes 1376264 | tf_op jit(solution)/shard_map/ppermute | solution.py:257
  52.8 27.8 %collective-permute-start.3 = (bf16[448,512]{1,0:T(8,128)(2,1)S(1)}, bf16[448,512]{1,0:T(8,128)(2,1)S(1)}, u32[]{:S(2)}, u32[]{:S(2)}) collective-permute-start(bf16[448,512]{1,0:T(8,128)(2,1)S(1)} %collective-permute-done.1.refs_2_), channel_id=1, source_target_pairs={{8,0},{16,8},{24,16},{28,24},{20,28},{12,20},{4,12},{0,4},{9,1},{1... | collective-permute-start | bytes 1376264 | tf_op jit(solution)/shard_map/ppermute | solution.py:258
  54.9 30.1 %collective-permute-start.14 = (bf16[160,2048]{1,0:T(8,128)(2,1)}, bf16[160,2048]{1,0:T(8,128)(2,1)}, u32[]{:S(2)}, u32[]{:S(2)}) collective-permute-start(bf16[160,2048]{1,0:T(8,128)(2,1)} %collective-permute-done.9), channel_id=1, source_target_pairs={{8,0},{16,8},{24,16},{28,24},{20,28},{12,20},{4,12},{0,4},{9,1},{1... | collective-permute-start | bytes 1966088 | tf_op jit(solution)/shard_map/ppermute | solution.py:258
  61.0 28.0 %collective-permute-start.38 = (bf16[448,512]{1,0:T(8,128)(2,1)}, bf16[448,512]{1,0:T(8,128)(2,1)S(1)}, u32[]{:S(2)}, u32[]{:S(2)}) collective-permute-start(bf16[448,512]{1,0:T(8,128)(2,1)} %collective-permute-done.36.refs_3_), channel_id=1, source_target_pairs={{0,8},{8,16},{16,24},{24,28},{28,20},{20,12},{12,4},{4,0},{1,9},{9... | collective-permute-start | bytes 1376264 | tf_op jit(solution)/shard_map/ppermute | solution.py:257
  85.0 39.3 %collective-permute-start.11 = (bf16[320,2048]{1,0:T(8,128)(2,1)}, bf16[320,2048]{1,0:T(8,128)(2,1)}, u32[]{:S(2)}, u32[]{:S(2)}) collective-permute-start(bf16[320,2048]{1,0:T(8,128)(2,1)} %constant_dynamic-update-slice_fusion.refs_0_), channel_id=1, source_target_pairs={{0,2},{1,3},{2,0},{3,1},{4,6},{5,7},{6,4},{7,5},{8,10},{9,11},{10,... | collective-permute-start | bytes 3932168 | tf_op jit(solution)/shard_map/ppermute | solution.py:321
  89.0 41.7 %collective-permute-start.10 = (bf16[320,2048]{1,0:T(8,128)(2,1)}, bf16[320,2048]{1,0:T(8,128)(2,1)}, u32[]{:S(2)}, u32[]{:S(2)}) collective-permute-start(bf16[320,2048]{1,0:T(8,128)(2,1)} %constant_dynamic-update-slice_fusion.refs_0_), channel_id=1, source_target_pairs={{0,1},{1,0},{2,3},{3,2},{4,5},{5,4},{6,7},{7,6},{8,9},{9,8},{10,11... | collective-permute-start | bytes 3932168 | tf_op jit(solution)/shard_map/ppermute | solution.py:324
  94.7 50.4 %collective-permute-start.16 = (bf16[320,2048]{1,0:T(8,128)(2,1)}, bf16[320,2048]{1,0:T(8,128)(2,1)}, u32[]{:S(2)}, u32[]{:S(2)}) collective-permute-start(bf16[320,2048]{1,0:T(8,128)(2,1)} %constant_dynamic-update-slice_fusion.2.refs_0_), channel_id=1, source_target_pairs={{0,2},{1,3},{2,0},{3,1},{4,6},{5,7},{6,4},{7,5},{8,10},{9,11},{10,... | collective-permute-start | bytes 3932168 | tf_op jit(solution)/shard_map/ppermute | solution.py:321
  124.3 61.0 %collective-permute-start.21 = (bf16[320,2048]{1,0:T(8,128)(2,1)S(1)}, bf16[320,2048]{1,0:T(8,128)(2,1)}, u32[]{:S(2)}, u32[]{:S(2)}) collective-permute-start(bf16[320,2048]{1,0:T(8,128)(2,1)S(1)} %constant_dynamic-update-slice_fusion.4.refs_0_), channel_id=1, source_target_pairs={{0,2},{1,3},{2,0},{3,1},{4,6},{5,7},{6,4},{7,5},{8,10},{9,11},{10,... | collective-permute-start | bytes 3932168 | tf_op jit(solution)/shard_map/ppermute | solution.py:321
  125.7 59.7 %collective-permute-start.12 = (bf16[320,2048]{1,0:T(8,128)(2,1)}, bf16[320,2048]{1,0:T(8,128)(2,1)S(1)}, u32[]{:S(2)}, u32[]{:S(2)}) collective-permute-start(bf16[320,2048]{1,0:T(8,128)(2,1)} %collective-permute-done.11.refs_2_), channel_id=1, source_target_pairs={{0,1},{1,0},{2,3},{3,2},{4,5},{5,4},{6,7},{7,6},{8,9},{9,8},{10,11... | collective-permute-start | bytes 3932168 | tf_op jit(solution)/shard_map/ppermute | solution.py:326
  129.6 55.1 %collective-permute-start.26 = (bf16[160,2048]{1,0:T(8,128)(2,1)S(1)}, bf16[160,2048]{1,0:T(8,128)(2,1)S(1)}, u32[]{:S(2)}, u32[]{:S(2)}) collective-permute-start(bf16[160,2048]{1,0:T(8,128)(2,1)S(1)} %constant_dynamic-update-slice_fusion.6.refs_0_), channel_id=1, source_target_pairs={{0,2},{1,3},{2,0},{3,1},{4,6},{5,7},{6,4},{7,5},{8,10},{9,11},{10,... | collective-permute-start | bytes 1966088 | tf_op jit(solution)/shard_map/ppermute | solution.py:321
  130.7 54.1 %collective-permute-start.25 = (bf16[160,2048]{1,0:T(8,128)(2,1)S(1)}, bf16[160,2048]{1,0:T(8,128)(2,1)S(1)}, u32[]{:S(2)}, u32[]{:S(2)}) collective-permute-start(bf16[160,2048]{1,0:T(8,128)(2,1)S(1)} %constant_dynamic-update-slice_fusion.6.refs_0_), channel_id=1, source_target_pairs={{0,1},{1,0},{2,3},{3,2},{4,5},{5,4},{6,7},{7,6},{8,9},{9,8},{10,11... | collective-permute-start | bytes 1966088 | tf_op jit(solution)/shard_map/ppermute | solution.py:324
  145.1 64.1 %collective-permute-start.15 = (bf16[320,2048]{1,0:T(8,128)(2,1)}, bf16[320,2048]{1,0:T(8,128)(2,1)}, u32[]{:S(2)}, u32[]{:S(2)}) collective-permute-start(bf16[320,2048]{1,0:T(8,128)(2,1)} %constant_dynamic-update-slice_fusion.2.refs_0_), channel_id=1, source_target_pairs={{0,1},{1,0},{2,3},{3,2},{4,5},{5,4},{6,7},{7,6},{8,9},{9,8},{10,11... | collective-permute-start | bytes 3932168 | tf_op jit(solution)/shard_map/ppermute | solution.py:324
  184.8 38.0 %collective-permute-start.20 = (bf16[320,2048]{1,0:T(8,128)(2,1)S(1)}, bf16[320,2048]{1,0:T(8,128)(2,1)S(1)}, u32[]{:S(2)}, u32[]{:S(2)}) collective-permute-start(bf16[320,2048]{1,0:T(8,128)(2,1)S(1)} %constant_dynamic-update-slice_fusion.4.refs_0_), channel_id=1, source_target_pairs={{0,1},{1,0},{2,3},{3,2},{4,5},{5,4},{6,7},{7,6},{8,9},{9,8},{10,11... | collective-permute-start | bytes 3932168 | tf_op jit(solution)/shard_map/ppermute | solution.py:324
  185.4 37.8 %collective-permute-start.22 = (bf16[320,2048]{1,0:T(8,128)(2,1)}, bf16[320,2048]{1,0:T(8,128)(2,1)}, u32[]{:S(2)}, u32[]{:S(2)}) collective-permute-start(bf16[320,2048]{1,0:T(8,128)(2,1)} %collective-permute-done.21.refs_2_), channel_id=1, source_target_pairs={{0,1},{1,0},{2,3},{3,2},{4,5},{5,4},{6,7},{7,6},{8,9},{9,8},{10,11... | collective-permute-start | bytes 3932168 | tf_op jit(solution)/shard_map/ppermute | solution.py:326
  197.9 36.5 %collective-permute-start.40 = (bf16[224,512]{1,0:T(8,128)(2,1)}, bf16[224,512]{1,0:T(8,128)(2,1)S(1)}, u32[]{:S(2)}, u32[]{:S(2)}) collective-permute-start(bf16[224,512]{1,0:T(8,128)(2,1)} %slice.158), channel_id=1, source_target_pairs={{0,8},{8,16},{16,24},{24,28},{28,20},{20,12},{12,4},{4,0},{1,9},{9... | collective-permute-start | bytes 688136 | tf_op jit(solution)/shard_map/ppermute | solution.py:260
  209.2 25.2 %collective-permute-start.41 = (bf16[224,512]{1,0:T(8,128)(2,1)}, bf16[224,512]{1,0:T(8,128)(2,1)S(1)}, u32[]{:S(2)}, u32[]{:S(2)}) collective-permute-start(bf16[224,512]{1,0:T(8,128)(2,1)} %slice.159), channel_id=1, source_target_pairs={{8,0},{16,8},{24,16},{28,24},{20,28},{12,20},{4,12},{0,4},{9,1},{1... | collective-permute-start | bytes 688136 | tf_op jit(solution)/shard_map/ppermute | solution.py:261
  209.7 42.4 %collective-permute-start.6 = (bf16[224,512]{1,0:T(8,128)(2,1)}, bf16[224,512]{1,0:T(8,128)(2,1)S(1)}, u32[]{:S(2)}, u32[]{:S(2)}) collective-permute-start(bf16[224,512]{1,0:T(8,128)(2,1)} %slice.154), channel_id=1, source_target_pairs={{0,8},{8,16},{16,24},{24,28},{28,20},{20,12},{12,4},{4,0},{1,9},{9... | collective-permute-start | bytes 688136 | tf_op jit(solution)/shard_map/ppermute | solution.py:260
  222.8 29.6 %collective-permute-start.7 = (bf16[224,512]{1,0:T(8,128)(2,1)}, bf16[224,512]{1,0:T(8,128)(2,1)S(1)}, u32[]{:S(2)}, u32[]{:S(2)}) collective-permute-start(bf16[224,512]{1,0:T(8,128)(2,1)} %slice.155), channel_id=1, source_target_pairs={{8,0},{16,8},{24,16},{28,24},{20,28},{12,20},{4,12},{0,4},{9,1},{1... | collective-permute-start | bytes 688136 | tf_op jit(solution)/shard_map/ppermute | solution.py:261
  242.1 26.8 %collective-permute-start.45 = (bf16[1024,128]{1,0:T(8,128)(2,1)S(1)}, bf16[1024,128]{1,0:T(8,128)(2,1)S(1)}, u32[]{:S(2)}, u32[]{:S(2)}) collective-permute-start(bf16[1024,128]{1,0:T(8,128)(2,1)S(1)} %attend.7.refs_12_), channel_id=1, source_target_pairs={{0,2},{1,3},{2,0},{3,1},{4,6},{5,7},{6,4},{7,5},{8,10},{9,11},{10,... | collective-permute-start | bytes 786440 | tf_op jit(solution)/shard_map/ppermute | solution.py:350
  243.5 25.5 %collective-permute-start.46 = (bf16[1024,128]{1,0:T(8,128)(2,1)S(1)}, bf16[1024,128]{1,0:T(8,128)(2,1)S(1)}, u32[]{:S(2)}, u32[]{:S(2)}) collective-permute-start(bf16[1024,128]{1,0:T(8,128)(2,1)S(1)} %attend.7.refs_12_), channel_id=1, source_target_pairs={{0,1},{1,0},{2,3},{3,2},{4,5},{5,4},{6,7},{7,6},{8,9},{9,8},{10,11... | collective-permute-start | bytes 786440 | tf_op jit(solution)/shard_map/ppermute | solution.py:351
  (61 other events, 794.2 us)

commit v3 on v1

v3 whole, which is shorter than its diff:
```python
import functools

import jax
import jax.numpy as jnp
import numpy as np
from jax import lax
from jax.experimental import pallas as pl
from jax.experimental.pallas import tpu as pltpu
from jax.sharding import PartitionSpec as P

HD = 128
BLK = 128
MIB = 1 << 20


def ring_order(devices):
    half = devices // 2
    return [2 * i for i in range(half)] + [2 * i + 1 for i in reversed(range(half))]


def after(value, *others):
    return lax.optimization_barrier((value, others))[0]


def kv_kernel(heads, tokens_ref, wk_ref, wv_ref, start_ref, end_ref, *refs):
    outs = refs[: len(heads)]
    rows_held, weight, sems = refs[len(heads) :]
    tok_rows = tokens_ref.shape[0]
    tiles = 4
    tile = tok_rows // tiles
    columns = weight.shape[1]
    copies = []
    for at, head in enumerate(heads):
        for which, source in enumerate((wk_ref, wv_ref)):
            copies.append(
                pltpu.make_async_copy(
                    source.at[:, pl.ds(head * HD, HD)],
                    weight.at[:, pl.ds((2 * at + which) * HD, HD)],
                    sems.at[len(copies)],
                )
            )
    for at in range(tiles):
        rows = pl.ds(at * tile, tile)
        copies.append(
            pltpu.make_async_copy(tokens_ref.at[rows], rows_held.at[rows], sems.at[len(copies)])
        )
    for copy in copies:
        copy.start()
    for copy in copies[: 2 * len(heads)]:
        copy.wait()
    share = start_ref.shape[1]
    start = start_ref[...]
    end = end_ref[...]
    ones = jnp.ones((tile, HD), jnp.bfloat16)
    sums = jnp.zeros((share, columns), jnp.float32)
    counts = jnp.zeros((share, HD), jnp.float32)
    for at in range(tiles):
        copies[2 * len(heads) + at].wait()
        rows = slice(at * tile, (at + 1) * tile)
        kv = jnp.dot(rows_held[rows, :], weight[...], preferred_element_type=jnp.float32)
        kv = kv.astype(jnp.bfloat16)
        for to, out in enumerate(outs):
            out[rows, :] = kv[:, 2 * to * HD : 2 * (to + 1) * HD]
        position = lax.broadcasted_iota(jnp.int32, (tile, share), 0) + at * tile
        member = (position >= start) & (position < end)
        member = member.astype(jnp.float32).astype(jnp.bfloat16)
        over_rows = (((0,), (0,)), ((), ()))
        sums += lax.dot_general(member, kv, over_rows, preferred_element_type=jnp.float32)
        counts += lax.dot_general(member, ones, over_rows, preferred_element_type=jnp.float32)
    means = (sums / counts[:, :1]).astype(jnp.bfloat16)
    for to, out in enumerate(outs):
        out[tok_rows:, :] = means[:, 2 * to * HD : 2 * (to + 1) * HD]


def project_kv(tokens, w_key, w_value, start, end, heads):
    tok_rows, width = tokens.shape
    share = start.shape[1]
    any_spec = pl.BlockSpec(memory_space=pl.ANY)
    out_shape = (tok_rows + share, 2 * HD)
    return pl.pallas_call(
        functools.partial(kv_kernel, heads),
        grid=(1,),
        in_specs=[any_spec] * 3 + [pl.BlockSpec((1, share), lambda i: (0, 0))] * 2,
        out_specs=[pl.BlockSpec(out_shape, lambda i: (0, 0))] * len(heads),
        out_shape=[jax.ShapeDtypeStruct(out_shape, jnp.bfloat16)] * len(heads),
        scratch_shapes=[
            pltpu.VMEM((tok_rows, width), jnp.bfloat16),
            pltpu.VMEM((width, 2 * HD * len(heads)), jnp.bfloat16),
            pltpu.SemaphoreType.DMA((2 * len(heads) + 4,)),
        ],
        compiler_params=pltpu.CompilerParams(vmem_limit_bytes=60 * MIB),
        cost_estimate=pl.CostEstimate(
            flops=2 * tok_rows * width * 2 * HD * len(heads),
            bytes_accessed=6 * MIB,
            transcendentals=0,
        ),
        name="project_kv",
    )(tokens, w_key, w_value, start, end)


def attend_kernel(devices, table_ref, owner_ref, q_ref, *refs):
    buffers = refs[:-4]
    out_ref, kv, summary, sems = refs[-4:]
    tok_rows = q_ref.shape[0]
    share = summary.shape[0] // devices
    copies = []

    def copy(source, target):
        done = pltpu.make_async_copy(source, target, sems.at[len(copies)])
        done.start()
        copies.append(done)

    for at, buffer in enumerate(buffers):
        owner = owner_ref[min(at, devices - 1)]
        first = buffers[devices - 1].shape[0] if at == devices else 0
        rows = min(buffer.shape[0], tok_rows - first)
        base = pl.multiple_of(owner * tok_rows + first, 16)
        copy(buffer.at[pl.ds(0, rows)], kv.at[pl.ds(base, rows)])
        if buffer.shape[0] > rows:
            segment = lax.rem(owner + devices // 2, devices)
            base = pl.multiple_of(segment * share, 16)
            copy(buffer.at[pl.ds(rows, share)], summary.at[pl.ds(base, share)])
    for done in copies:
        done.wait()
    factor = HD**-0.5 * float(np.log2(np.e))
    slots = table_ref.shape[1]
    for block in range(tok_rows // BLK):
        parts = []
        for slot in range(slots):
            base = pl.multiple_of(table_ref[block, slot] * BLK, BLK)
            source = kv if slot < slots - 2 else summary
            parts.append(source[pl.ds(base, BLK), :])
        gathered = jnp.concatenate(parts, axis=0)
        rows = slice(block * BLK, (block + 1) * BLK)
        scores = lax.dot_general(
            gathered[:, :HD],
            q_ref[rows, :],
            (((1,), (1,)), ((), ())),
            preferred_element_type=jnp.float32,
        )
        peak = jnp.max(scores, axis=0, keepdims=True)
        weights = jnp.exp2((scores - peak) * factor)
        total = jnp.sum(weights, axis=0, keepdims=True)
        mixed = lax.dot_general(
            gathered[:, HD:],
            weights.astype(jnp.bfloat16),
            (((0,), (0,)), ((), ())),
            preferred_element_type=jnp.float32,
        )
        out_ref[rows, :] = (mixed / total).T.astype(jnp.bfloat16)


def attend(table, owner_ids, queries, buffers, head, devices, share):
    tok_rows = queries.shape[0]
    any_spec = pl.BlockSpec(memory_space=pl.ANY)
    smem = pl.BlockSpec(memory_space=pltpu.SMEM)
    return pl.pallas_call(
        functools.partial(attend_kernel, devices),
        grid=(1,),
        in_specs=[smem, smem, pl.BlockSpec((tok_rows, HD), lambda i: (0, head))]
        + [any_spec] * len(buffers),
        out_specs=pl.BlockSpec((tok_rows, HD), lambda i: (0, 0)),
        out_shape=jax.ShapeDtypeStruct((tok_rows, HD), jnp.bfloat16),
        scratch_shapes=[
            pltpu.VMEM((devices * tok_rows, 2 * HD), jnp.bfloat16),
            pltpu.VMEM((devices * share, 2 * HD), jnp.bfloat16),
            pltpu.SemaphoreType.DMA((2 * devices + 1,)),
        ],
        compiler_params=pltpu.CompilerParams(vmem_limit_bytes=48 * MIB),
        cost_estimate=pl.CostEstimate(
            flops=4 * tok_rows * 1152 * HD,
            bytes_accessed=devices * tok_rows * 4 * HD,
            transcendentals=tok_rows * 1152,
        ),
        name="attend",
    )(table, owner_ids, queries, *buffers)


def out_kernel(pieces, final, *refs):
    out_ref = refs[-1]
    rows = jnp.concatenate([ref[...] for ref in refs[:pieces]], axis=1)
    weights = refs[pieces : 2 * pieces]
    weight = jnp.concatenate([ref[...] for ref in weights], axis=0)
    total = jnp.dot(rows, weight, preferred_element_type=jnp.float32)
    if final:
        total += refs[2 * pieces][...]
    out_ref[...] = total.astype(out_ref.dtype)


def project_out(pieces, weights, places, total):
    tok_rows = pieces[0].shape[0]
    columns = weights[0].shape[1]
    final = total is not None
    tile = tok_rows if final else 256
    row_spec = pl.BlockSpec((tile, columns), lambda i: (i, 0))

    def weight_spec(head):
        return pl.BlockSpec((HD, columns), lambda i: (head, 0))

    return pl.pallas_call(
        functools.partial(out_kernel, len(pieces), final),
        grid=(tok_rows // tile,),
        in_specs=[pl.BlockSpec((tile, HD), lambda i: (i, 0))] * len(pieces)
        + [weight_spec(head) for _, head in places]
        + [row_spec] * final,
        out_specs=row_spec,
        out_shape=jax.ShapeDtypeStruct(
            (tok_rows, columns), jnp.bfloat16 if final else jnp.float32
        ),
        compiler_params=pltpu.CompilerParams(vmem_limit_bytes=63 * MIB),
        cost_estimate=pl.CostEstimate(
            flops=2 * tok_rows * len(pieces) * HD * columns,
            bytes_accessed=6 * MIB,
            transcendentals=0,
        ),
        name="project_out",
    )(*pieces, *[weights[at] for at, _ in places], *([total] if final else []))


WAYS = ("ahead", "behind", "both", "both")


class Ring:
    def __init__(self, chunk, devices, last_way):
        order = ring_order(devices)
        self.forward = [(order[p], order[(p + 1) % devices]) for p in range(devices)]
        self.backward = [(target, source) for source, target in self.forward]
        self.steps = devices // 2
        self.last_way = last_way
        self.buffers = [chunk]
        self.last = (chunk, chunk)

    def step(self, *others):
        ahead, behind = after(self.last, *others)
        ways = ("ahead", "behind")
        if len(self.buffers) == 2 * self.steps - 1:
            if self.last_way in ways:
                ways = (self.last_way,)
            else:
                half = ahead.shape[0] // 32 * 16
                ahead, behind = ahead[:half], behind[half:]
        given = []
        if "ahead" in ways:
            given.append(lax.ppermute(ahead, "seq", self.forward))
        if "behind" in ways:
            given.append(lax.ppermute(behind, "seq", self.backward))
        self.last = given
        self.buffers += given
        return given


def per_device(
    tokens,
    w_query,
    w_key,
    w_value,
    w_out,
    window_blocks,
    random_blocks,
    summary_blocks,
    seg_start,
    seg_end,
):
    tok_rows = tokens.shape[0]
    columns = w_query.shape[1]
    heads = columns // HD
    block_count = tok_rows // BLK
    devices = lax.axis_size("seq")
    groups = lax.axis_size("head")
    me = lax.axis_index("seq")
    group = lax.axis_index("head")
    share = seg_start.shape[0] // devices

    order = np.array(ring_order(devices), np.int32)
    position = jnp.asarray(np.argsort(order).astype(np.int32))[me]
    steps = [0] + [s * k for k in range(1, devices // 2) for s in (-1, 1)] + [devices // 2]
    owner_ids = jnp.asarray(order)[(position + jnp.asarray(steps, jnp.int32)) % devices]
    mine = lax.dynamic_slice_in_dim(random_blocks, me * block_count, block_count, 0)
    table = jnp.concatenate([window_blocks, mine, summary_blocks], axis=1)
    first_segment = lax.rem(me + devices // 2, devices) * share
    start = lax.dynamic_slice_in_dim(seg_start, first_segment, share, 0) - me * tok_rows
    end = lax.dynamic_slice_in_dim(seg_end, first_segment, share, 0) - me * tok_rows

    start, end = start[None, :], end[None, :]
    steps = devices // 2

    def to_head(value, flip):
        return lax.ppermute(value, "head", [(g, g ^ flip) for g in range(groups)])

    turns = [((at, step),) for step in range(steps - 1) for at in (0, 1)]
    turns += [((2, 0),), ((0, steps - 1), (1, steps - 1)), ((3, 0),)]
    turns += [((at, step),) for step in range(1, steps) for at in (2, 3)]
    joined = 2 * steps - 1
    rings = [
        Ring(chunk, devices, way)
        for chunk, way in zip(
            project_kv(tokens, w_key, w_value, start, end, (0, 1)), WAYS[:2], strict=True
        )
    ]
    started, kernels = [], []
    pieces = {}

    def finish(head, *needed):
        own = attend(
            after(table, *needed), owner_ids, queries, rings[head].buffers, head, devices, share
        )
        pieces[0, head] = own
        pieces[1, head] = to_head(own, 1)
        pieces[2, head] = to_head(own, 2)
        if head < heads - 1:
            pieces[3, head] = to_head(pieces[2, head], 1)
        return own

    out_weights = {0: lax.dynamic_slice_in_dim(w_out, group * columns, columns, 1)}
    for turn, moves in enumerate(turns):
        needed = [*(started[-2] if turn > 1 else ()), *(kernels[-1] if turn > 0 else ())]
        begun, ran = [], []
        for head, _ in moves:
            begun += rings[head].step(*needed)
        if turn == 4:
            chunks = project_kv(after(tokens, *needed), w_key, w_value, start, end, (2, 3))
            rings += [
                Ring(chunk, devices, way) for chunk, way in zip(chunks, WAYS[2:], strict=True)
            ]
            ran += chunks
        if turn == 6:
            queries = jnp.dot(after(tokens, *needed), w_query, preferred_element_type=jnp.float32)
            queries = queries.astype(jnp.bfloat16)
            ran.append(queries)
        if turn in (2, 3):
            for flip in ((2,), (3, 1))[(2, 3).index(turn)]:
                part = lax.dynamic_slice_in_dim(
                    after(w_out, *needed), (group ^ flip) * columns, columns, 1
                )
                out_weights[flip] = to_head(part, flip)
                begun.append(out_weights[flip])
        if turn in (joined + 2, joined + 3):
            ran.append(finish(turn - joined - 2, *needed))
        if turn in (joined + 3, joined + 4):
            begun.append(pieces[2, turn - joined - 3])
        if turn == len(turns) - 1:
            ran.append(finish(2, *needed))
        started.append(begun)
        kernels.append(ran)
    finish(3, pieces[0, 2])
    late = [(flip, heads - 1) for flip in (2, 3)]
    early = [place for place in pieces if place not in late]
    total = project_out([pieces[place] for place in early], out_weights, early, None)
    pieces[3, heads - 1] = to_head(after(pieces[2, heads - 1], total), 1)
    return project_out([pieces[place] for place in late], out_weights, late, total)


def solution(mesh):
    placed = (
        P("seq", None),
        P(None, "head"),
        P(None, "head"),
        P(None, "head"),
        P("head", None),
        P("seq", None),
        P(),
        P("seq", None),
        P(),
        P(),
    )
    return jax.shard_map(
        per_device, mesh=mesh, in_specs=placed, out_specs=P("seq", "head"), check_vma=False
    )
```

time: 224 us -> 207 us (0.924)
  starting transfers between devices: 60.9 us -> 40.3 us
  local copies, waits for them, and re-layouts: 26.6 us -> 13 us
  waiting for transfers between devices: 90.5 us -> 102 us
  matrix products: 2.32 us -> 5.21 us
    ppermute x44 -> x45, starting transfers between devices: 56.5 us -> 40.3 us  [the longest x15 26 us: step(): given.append(lax.ppermute(ahead, 'seq', self.forward))]
    ppermute x44 -> x45, waiting for transfers between devices: 90.5 us -> 102 us  [the longest x15 59 us: step(): given.append(lax.ppermute(ahead, 'seq', self.forward))]
    pallas_call x5 -> x4, Pallas kernels: 13.2 us -> 23.6 us  [the longest x2 14.2 us: project_kv(): pl.pallas_call(functools.partial(kv_kernel, heads), grid=(1,), in_specs=[...]
    unnamed x56 -> x73, local copies, waits for them, and re-layouts: 15.5 us -> 6.11 us
    pallas_call x4, Pallas kernels: 27.7 us -> 19.3 us  [attend(): pl.pallas_call(functools.partial(attend_kernel, devices), grid=(1,), in_s...]
    all_to_all x1 -> x0, starting transfers between devices: 4.45 us -> none  [per_device(): lax.all_to_all(w_out.reshape(heads * HD, groups, -1), 'head', split_axis=...]
    dynamic_slice x1 -> x3, local copies, waits for them, and re-layouts: 1.65 us -> 5.41 us  [the longest x2 3.55 us: per_device(): lax.dynamic_slice_in_dim(after(w_out, *needed), (group ^ flip) * columns,...]
    slice x8 -> x4, local copies, waits for them, and re-layouts: 3.79 us -> 0.08 us  [step(): ahead, behind = (ahead[:half], behind[half:])]
  transfers between devices with their start and end apart: 45 -> 45, of which waited for: 21 -> 28; matrix products, arithmetic and copies ran while one was open for 7% -> 6% of each run, Pallas kernels for 17% -> 16%
where the time goes in v3:
time: 207 us; the launch traced here: 206 us
  waiting for transfers between devices  102 us (49%)
  Pallas kernels  42.9 us (21%)
  starting transfers between devices  40.3 us (19%)
  local copies, waits for them, and re-layouts  13 us (6%)
  matrix products  5.21 us (3%)
  other arithmetic  2.15 us (1%)
    ppermute x15, waiting for transfers between devices, step(): given.append(lax.ppermute(ahead, 'seq', self.forward))  59 us
    ppermute x15, waiting for transfers between devices, step(): given.append(lax.ppermute(behind, 'seq', self.backward))  33.9 us
    ppermute x15, starting transfers between devices, step(): given.append(lax.ppermute(ahead, 'seq', self.forward))  26 us
    pallas_call x4, Pallas kernels, attend(): pl.pallas_call(functools.partial(attend_kernel, devices), grid=(1,), in_s...  19.3 us
    pallas_call x2, Pallas kernels, project_kv(): pl.pallas_call(functools.partial(kv_kernel, heads), grid=(1,), in_specs=[...  14.2 us
    pallas_call x2, Pallas kernels, project_out(): pl.pallas_call(functools.partial(out_kernel, len(pieces), final), grid=(t...  9.33 us
    ppermute x15, waiting for transfers between devices, to_head(): return lax.ppermute(value, 'head', [(g, g ^ flip) for g in range(groups)])  9.02 us
    ppermute x15, starting transfers between devices, to_head(): return lax.ppermute(value, 'head', [(g, g ^ flip) for g in range(groups)])  8.58 us
  transfers between devices with their start and end apart: 45, of which 28 were waited for; matrix products, arithmetic and copies ran while one was open for 6% of the time, Pallas kernels for 16%

profile of v3, /device:TPU:0, one launch (start us, length us, event | category | flops | bytes accessed | tf_op | source)
XLA Modules:
  0.0 205.8 jit_solution(2789423349645354281)
XLA Ops:
  1.4 7.1 %project_kv.2 = (bf16[1088,256]{1,0:T(8,128)(2,1)}, bf16[1088,256]{1,0:T(8,128)(2,1)}) custom-call(bf16[1024,2048]{1,0:T(8,128)(2,1)} %tokens_ref.2, bf16[2048,512]{1,0:T(8,128)(2,1)} %wk_ref.3, bf16[2048,512]{1,0:T(8,128)(2,1)} %wv_ref.3, s32[1,64]{1,0:T(1,128)} %get-tuple-element.94.start_ref, s32[1,64]{1,0:T(1,128)} %get-tuple-element.93.end_ref), custom_call_target="tpu_custom_call" | custom-call | flops 2147483648 | bytes 6291456 | tf_op jit(solution)/shard_map/project_kv/pallas_call | solution.py:80
  8.5 3.1 %collective-permute-start = (bf16[1088,256]{1,0:T(8,128)(2,1)}, bf16[1088,256]{1,0:T(8,128)(2,1)S(1)}, u32[]{:S(2)}, u32[]{:S(2)}) collective-permute-start(bf16[1088,256]{1,0:T(8,128)(2,1)} %get-tuple-element.50.refs_0_), channel_id=1, source_target_pairs={{0,8},{8,16},{16,24},{24,28},{28,20},{20,12},{12,4},{4,0},{1,9},{9... | collective-permute-start | bytes 1671176 | tf_op jit(solution)/shard_map/ppermute | solution.py:244
  13.6 11.6 %collective-permute-done.refs_1_ = bf16[1088,256]{1,0:T(8,128)(2,1)S(1)} collective-permute-done((bf16[1088,256]{1,0:T(8,128)(2,1)}, bf16[1088,256]{1,0:T(8,128)(2,1)S(1)}, u32[]{:S(2)}, u32[]{:S(2)}) %collective-permute-start) | collective-permute-done | bytes 557088 | tf_op jit(solution)/shard_map/ppermute | solution.py:244
  32.2 4.9 %collective-permute-done.11.refs_1_ = bf16[1088,256]{1,0:T(8,128)(2,1)S(1)} collective-permute-done((bf16[1088,256]{1,0:T(8,128)(2,1)}, bf16[1088,256]{1,0:T(8,128)(2,1)S(1)}, u32[]{:S(2)}, u32[]{:S(2)}) %collective-permute-start.11) | collective-permute-done | bytes 557088 | tf_op jit(solution)/shard_map/ppermute | solution.py:244
  39.3 2.3 %constant_dynamic-slice_fusion.1 = (bf16[512,512]{1,0:T(8,128)(2,1)}, bf16[512,512]{1,0:T(8,128)(2,1)S(1)}) fusion(bf16[512,2048]{1,0:T(8,128)(2,1)} %param.17, s32[]{:T(128)S(6)} %select_n.36, s32[]{:T(128)S(6)} %select_n.35), kind=kLoop, calls=%fused_computation.9 | loop fusion | bytes 2097160 | tf_op jit(solution)/shard_map/dynamic_slice | solution.py:332
  43.6 5.6 %collective-permute-done.2.refs_3_ = bf16[1088,256]{1,0:T(8,128)(2,1)} collective-permute-done((bf16[1088,256]{1,0:T(8,128)(2,1)S(1)}, bf16[1088,256]{1,0:T(8,128)(2,1)}, u32[]{:S(2)}, u32[]{:S(2)}) %collective-permute-start.2) | collective-permute-done | bytes 557088 | tf_op jit(solution)/shard_map/ppermute | solution.py:244
  49.2 2.1 %collective-permute-done.3.refs_4_ = bf16[1088,256]{1,0:T(8,128)(2,1)} collective-permute-done((bf16[1088,256]{1,0:T(8,128)(2,1)S(1)}, bf16[1088,256]{1,0:T(8,128)(2,1)}, u32[]{:S(2)}, u32[]{:S(2)}) %collective-permute-start.3) | collective-permute-done | bytes 557088 | tf_op jit(solution)/shard_map/ppermute | solution.py:246
  53.4 2.4 %collective-permute-done.15.refs_17_.refs_21_.refs_25_.refs_3_ = bf16[512,512]{1,0:T(8,128)(2,1)S(1)} collective-permute-done((bf16[512,512]{1,0:T(8,128)(2,1)S(1)}, bf16[512,512]{1,0:T(8,128)(2,1)S(1)}, u32[]{:S(2)}, u32[]{:S(2)}) %collective-permute-start.15) | collective-permute-done | bytes 524320 | tf_op jit(solution)/shard_map/ppermute | solution.py:288
  56.0 7.1 %project_kv.3 = (bf16[1088,256]{1,0:T(8,128)(2,1)}, bf16[1088,256]{1,0:T(8,128)(2,1)}) custom-call(bf16[1024,2048]{1,0:T(8,128)(2,1)} %tokens_ref.2, bf16[2048,512]{1,0:T(8,128)(2,1)} %wk_ref.3, bf16[2048,512]{1,0:T(8,128)(2,1)} %wv_ref.3, s32[1,64]{1,0:T(1,128)} %get-tuple-element.94.start_ref, s32[1,64]{1,0:T(1,128)} %get-tuple-element.93.end_ref), custom_call_target="tpu_custom_call" | custom-call | flops 2147483648 | bytes 6291456 | tf_op jit(solution)/shard_map/project_kv/pallas_call | solution.py:80
  65.4 7.7 %collective-permute-done.5.refs_5_ = bf16[1088,256]{1,0:T(8,128)(2,1)} collective-permute-done((bf16[1088,256]{1,0:T(8,128)(2,1)}, bf16[1088,256]{1,0:T(8,128)(2,1)}, u32[]{:S(2)}, u32[]{:S(2)}) %collective-permute-start.5) | collective-permute-done | bytes 557088 | tf_op jit(solution)/shard_map/ppermute | solution.py:244
  73.1 2.1 %collective-permute-done.6.refs_6_ = bf16[1088,256]{1,0:T(8,128)(2,1)} collective-permute-done((bf16[1088,256]{1,0:T(8,128)(2,1)}, bf16[1088,256]{1,0:T(8,128)(2,1)}, u32[]{:S(2)}, u32[]{:S(2)}) %collective-permute-start.6) | collective-permute-done | bytes 557088 | tf_op jit(solution)/shard_map/ppermute | solution.py:246
  77.2 5.2 %convolution_convert_fusion.q_ref = bf16[1024,512]{1,0:T(8,128)(2,1)S(1)} fusion(bf16[1024,2048]{1,0:T(8,128)(2,1)} %tokens_ref.2, bf16[2048,512]{1,0:T(8,128)(2,1)} %param.14), kind=kOutput, calls=%fused_computation.1 | convolution fusion | flops 2148007936 | bytes 7340032 | tf_op jit(solution)/shard_map/dot_general | solution.py:327
  82.5 2.4 %collective-permute-done.17.refs_5_ = bf16[1088,256]{1,0:T(8,128)(2,1)S(1)} collective-permute-done((bf16[1088,256]{1,0:T(8,128)(2,1)S(1)}, bf16[1088,256]{1,0:T(8,128)(2,1)S(1)}, u32[]{:S(2)}, u32[]{:S(2)}) %collective-permute-start.17) | collective-permute-done | bytes 557088 | tf_op jit(solution)/shard_map/ppermute | solution.py:244
  89.8 7.1 %collective-permute-done.7.refs_1_ = bf16[1088,256]{1,0:T(8,128)(2,1)} collective-permute-done((bf16[1088,256]{1,0:T(8,128)(2,1)}, bf16[1088,256]{1,0:T(8,128)(2,1)}, u32[]{:S(2)}, u32[]{:S(2)}) %collective-permute-start.7) | collective-permute-done | bytes 557088 | tf_op jit(solution)/shard_map/ppermute | solution.py:244
  101.8 9.2 %collective-permute-done.20.refs_7_ = bf16[1088,256]{1,0:T(8,128)(2,1)} collective-permute-done((bf16[1088,256]{1,0:T(8,128)(2,1)}, bf16[1088,256]{1,0:T(8,128)(2,1)}, u32[]{:S(2)}, u32[]{:S(2)}) %collective-permute-start.20) | collective-permute-done | bytes 557088 | tf_op jit(solution)/shard_map/ppermute | solution.py:246
  116.2 5.0 %attend.4.refs_0_ = bf16[1024,128]{1,0:T(8,128)(2,1)S(1)} custom-call(s32[8,9]{1,0:T(8,128)S(1)} %pad_add_fusion.table_ref, s32[8]{0:T(128)S(1)} %gather_fusion, bf16[1024,512]{1,0:T(8,128)(2,1)S(1)} %convolution_convert_fusion.q_ref, bf16[1088,256]{1,0:T(8,128)(2,1)S(1)} %copy-done.9, bf16[1088,256]{1,0:T(8,128)(2,1)S(1)} %copy-done.11, ...), custom_call_target="tpu_custom_call" | custom-call | flops 603979776 | bytes 4194304 | tf_op jit(solution)/shard_map/attend/pallas_call | solution.py:157
  126.5 4.7 %attend.5.refs_4_ = bf16[1024,128]{1,0:T(8,128)(2,1)S(1)} custom-call(s32[8,9]{1,0:T(8,128)S(1)} %pad_add_fusion.table_ref, s32[8]{0:T(128)S(1)} %gather_fusion, bf16[1024,512]{1,0:T(8,128)(2,1)S(1)} %convolution_convert_fusion.q_ref, bf16[1088,256]{1,0:T(8,128)(2,1)S(1)} %copy-done.4, bf16[1088,256]{1,0:T(8,128)(2,1)S(1)} %collective-permute-done.11.refs_1_, ...), custom_call_target="tpu_custom_call" | custom-call | flops 603979776 | bytes 4194304 | tf_op jit(solution)/shard_map/attend/pallas_call | solution.py:157
  136.9 7.7 %collective-permute-done.21.refs_3_ = bf16[1088,256]{1,0:T(8,128)(2,1)S(1)} collective-permute-done((bf16[1088,256]{1,0:T(8,128)(2,1)}, bf16[1088,256]{1,0:T(8,128)(2,1)S(1)}, u32[]{:S(2)}, u32[]{:S(2)}) %collective-permute-start.21) | collective-permute-done | bytes 557088 | tf_op jit(solution)/shard_map/ppermute | solution.py:244
  150.2 4.9 %collective-permute-done.30.refs_6_ = bf16[1024,128]{1,0:T(8,128)(2,1)S(1)} collective-permute-done((bf16[1024,128]{1,0:T(8,128)(2,1)S(1)}, bf16[1024,128]{1,0:T(8,128)(2,1)S(1)}, u32[]{:S(2)}, u32[]{:S(2)}) %collective-permute-start.30) | collective-permute-done | bytes 262176 | tf_op jit(solution)/shard_map/ppermute | solution.py:288
  160.8 7.6 %collective-permute-done.24.refs_5_ = bf16[1088,256]{1,0:T(8,128)(2,1)S(1)} collective-permute-done((bf16[1088,256]{1,0:T(8,128)(2,1)S(1)}, bf16[1088,256]{1,0:T(8,128)(2,1)S(1)}, u32[]{:S(2)}, u32[]{:S(2)}) %collective-permute-start.24) | collective-permute-done | bytes 557088 | tf_op jit(solution)/shard_map/ppermute | solution.py:244
  176.6 4.6 %attend.6.refs_8_ = bf16[1024,128]{1,0:T(8,128)(2,1)S(1)} custom-call(s32[8,9]{1,0:T(8,128)S(1)} %pad_add_fusion.table_ref, s32[8]{0:T(128)S(1)} %gather_fusion, bf16[1024,512]{1,0:T(8,128)(2,1)S(1)} %convolution_convert_fusion.q_ref, bf16[1088,256]{1,0:T(8,128)(2,1)S(1)} %copy-done.14, bf16[1088,256]{1,0:T(8,128)(2,1)} %collective-permute-done.7.refs_1_, ...), custom_call_target="tpu_custom_call" | custom-call | flops 603979776 | bytes 4194304 | tf_op jit(solution)/shard_map/attend/pallas_call | solution.py:157
  183.4 5.0 %attend.7.refs_12_ = bf16[1024,128]{1,0:T(8,128)(2,1)} custom-call(s32[8,9]{1,0:T(8,128)S(1)} %pad_add_fusion.table_ref, s32[8]{0:T(128)S(1)} %gather_fusion, bf16[1024,512]{1,0:T(8,128)(2,1)S(1)} %convolution_convert_fusion.q_ref, bf16[1088,256]{1,0:T(8,128)(2,1)S(1)} %copy-done.6, bf16[1088,256]{1,0:T(8,128)(2,1)} %collective-permute-done.9.refs_1_, ...), custom_call_target="tpu_custom_call" | custom-call | flops 603979776 | bytes 4194304 | tf_op jit(solution)/shard_map/attend/pallas_call | solution.py:157
  194.0 6.1 %project_out.2.refs_4_ = f32[1024,512]{1,0:T(8,128)} custom-call(bf16[1024,128]{1,0:T(8,128)(2,1)} %copy-done.1, bf16[1024,128]{1,0:T(8,128)(2,1)} %copy-done.24, bf16[1024,128]{1,0:T(8,128)(2,1)} %copy-done.22, bf16[1024,128]{1,0:T(8,128)(2,1)} %copy-done.26, bf16[1024,128]{1,0:T(8,128)(2,1)} %copy-done.2, ...), custom_call_target="tpu_custom_call" | custom-call | flops 1879048192 | bytes 6291456 | tf_op jit(solution)/shard_map/project_out/pallas_call | solution.py:200
  202.6 3.3 %project_out.3 = bf16[1024,512]{1,0:T(8,128)(2,1)} custom-call(bf16[1024,128]{1,0:T(8,128)(2,1)} %collective-permute-done.35.refs_0_, bf16[1024,128]{1,0:T(8,128)(2,1)} %copy-done.30, bf16[512,512]{1,0:T(8,128)(2,1)} %copy-done.20, bf16[512,512]{1,0:T(8,128)(2,1)} %copy-done.21, f32[1024,512]{1,0:T(8,128)} %project_out.2.refs_4_), custom_call_target="tpu_custom_call" | custom-call | flops 268435456 | bytes 6291456 | tf_op jit(solution)/shard_map/project_out/pallas_call | solution.py:200
  (162 shorter events, 76.8 us)
Async XLA Ops:
  11.6 25.5 %collective-permute-start.11 = (bf16[1088,256]{1,0:T(8,128)(2,1)}, bf16[1088,256]{1,0:T(8,128)(2,1)S(1)}, u32[]{:S(2)}, u32[]{:S(2)}) collective-permute-start(bf16[1088,256]{1,0:T(8,128)(2,1)} %get-tuple-element.65.refs_0_), channel_id=1, source_target_pairs={{0,8},{8,16},{16,24},{24,28},{28,20},{20,12},{12,4},{4,0},{1,9},{9... | collective-permute-start | bytes 1671176 | tf_op jit(solution)/shard_map/ppermute | solution.py:244
  13.6 25.7 %collective-permute-start.12 = (bf16[1088,256]{1,0:T(8,128)(2,1)}, bf16[1088,256]{1,0:T(8,128)(2,1)S(1)}, u32[]{:S(2)}, u32[]{:S(2)}) collective-permute-start(bf16[1088,256]{1,0:T(8,128)(2,1)} %get-tuple-element.65.refs_0_), channel_id=1, source_target_pairs={{8,0},{16,8},{24,16},{28,24},{20,28},{12,20},{4,12},{0,4},{9,1},{1... | collective-permute-start | bytes 1671176 | tf_op jit(solution)/shard_map/ppermute | solution.py:246
  30.2 19.0 %collective-permute-start.2 = (bf16[1088,256]{1,0:T(8,128)(2,1)S(1)}, bf16[1088,256]{1,0:T(8,128)(2,1)}, u32[]{:S(2)}, u32[]{:S(2)}) collective-permute-start(bf16[1088,256]{1,0:T(8,128)(2,1)S(1)} %collective-permute-done.refs_1_), channel_id=1, source_target_pairs={{0,8},{8,16},{16,24},{24,28},{28,20},{20,12},{12,4},{4,0},{1,9},{9... | collective-permute-start | bytes 1671176 | tf_op jit(solution)/shard_map/ppermute | solution.py:244
  31.8 19.6 %collective-permute-start.3 = (bf16[1088,256]{1,0:T(8,128)(2,1)S(1)}, bf16[1088,256]{1,0:T(8,128)(2,1)}, u32[]{:S(2)}, u32[]{:S(2)}) collective-permute-start(bf16[1088,256]{1,0:T(8,128)(2,1)S(1)} %collective-permute-done.1.refs_2_), channel_id=1, source_target_pairs={{8,0},{16,8},{24,16},{28,24},{20,28},{12,20},{4,12},{0,4},{9,1},{1... | collective-permute-start | bytes 1671176 | tf_op jit(solution)/shard_map/ppermute | solution.py:246
  41.6 21.6 %collective-permute-start.13 = (bf16[1088,256]{1,0:T(8,128)(2,1)S(1)}, bf16[1088,256]{1,0:T(8,128)(2,1)S(1)}, u32[]{:S(2)}, u32[]{:S(2)}) collective-permute-start(bf16[1088,256]{1,0:T(8,128)(2,1)S(1)} %collective-permute-done.11.refs_1_), channel_id=1, source_target_pairs={{0,8},{8,16},{16,24},{24,28},{28,20},{20,12},{12,4},{4,0},{1,9},{9... | collective-permute-start | bytes 1671176 | tf_op jit(solution)/shard_map/ppermute | solution.py:244
  43.1 20.1 %collective-permute-start.14 = (bf16[1088,256]{1,0:T(8,128)(2,1)S(1)}, bf16[1088,256]{1,0:T(8,128)(2,1)}, u32[]{:S(2)}, u32[]{:S(2)}) collective-permute-start(bf16[1088,256]{1,0:T(8,128)(2,1)S(1)} %collective-permute-done.12.refs_2_), channel_id=1, source_target_pairs={{8,0},{16,8},{24,16},{28,24},{20,28},{12,20},{4,12},{0,4},{9,1},{1... | collective-permute-start | bytes 1671176 | tf_op jit(solution)/shard_map/ppermute | solution.py:246
  51.3 21.7 %collective-permute-start.5 = (bf16[1088,256]{1,0:T(8,128)(2,1)}, bf16[1088,256]{1,0:T(8,128)(2,1)}, u32[]{:S(2)}, u32[]{:S(2)}) collective-permute-start(bf16[1088,256]{1,0:T(8,128)(2,1)} %collective-permute-done.2.refs_3_), channel_id=1, source_target_pairs={{0,8},{8,16},{16,24},{24,28},{28,20},{20,12},{12,4},{4,0},{1,9},{9... | collective-permute-start | bytes 1671176 | tf_op jit(solution)/shard_map/ppermute | solution.py:244
  52.9 22.3 %collective-permute-start.6 = (bf16[1088,256]{1,0:T(8,128)(2,1)}, bf16[1088,256]{1,0:T(8,128)(2,1)}, u32[]{:S(2)}, u32[]{:S(2)}) collective-permute-start(bf16[1088,256]{1,0:T(8,128)(2,1)} %collective-permute-done.3.refs_4_), channel_id=1, source_target_pairs={{8,0},{16,8},{24,16},{28,24},{20,28},{12,20},{4,12},{0,4},{9,1},{1... | collective-permute-start | bytes 1671176 | tf_op jit(solution)/shard_map/ppermute | solution.py:246
  63.3 21.6 %collective-permute-start.17 = (bf16[1088,256]{1,0:T(8,128)(2,1)S(1)}, bf16[1088,256]{1,0:T(8,128)(2,1)S(1)}, u32[]{:S(2)}, u32[]{:S(2)}) collective-permute-start(bf16[1088,256]{1,0:T(8,128)(2,1)S(1)} %collective-permute-done.13.refs_3_), channel_id=1, source_target_pairs={{0,8},{8,16},{16,24},{24,28},{28,20},{20,12},{12,4},{4,0},{1,9},{9... | collective-permute-start | bytes 1671176 | tf_op jit(solution)/shard_map/ppermute | solution.py:244
  64.9 22.2 %collective-permute-start.18 = (bf16[1088,256]{1,0:T(8,128)(2,1)}, bf16[1088,256]{1,0:T(8,128)(2,1)}, u32[]{:S(2)}, u32[]{:S(2)}) collective-permute-start(bf16[1088,256]{1,0:T(8,128)(2,1)} %collective-permute-done.14.refs_4_), channel_id=1, source_target_pairs={{8,0},{16,8},{24,16},{28,24},{20,28},{12,20},{4,12},{0,4},{9,1},{1... | collective-permute-start | bytes 1671176 | tf_op jit(solution)/shard_map/ppermute | solution.py:246
  75.2 21.7 %collective-permute-start.7 = (bf16[1088,256]{1,0:T(8,128)(2,1)}, bf16[1088,256]{1,0:T(8,128)(2,1)}, u32[]{:S(2)}, u32[]{:S(2)}) collective-permute-start(bf16[1088,256]{1,0:T(8,128)(2,1)} %get-tuple-element.60.refs_0_), channel_id=1, source_target_pairs={{0,8},{8,16},{16,24},{24,28},{28,20},{20,12},{12,4},{4,0},{1,9},{9... | collective-permute-start | bytes 1671176 | tf_op jit(solution)/shard_map/ppermute | solution.py:244
  76.8 22.3 %collective-permute-start.8 = (bf16[1088,256]{1,0:T(8,128)(2,1)}, bf16[1088,256]{1,0:T(8,128)(2,1)}, u32[]{:S(2)}, u32[]{:S(2)}) collective-permute-start(bf16[1088,256]{1,0:T(8,128)(2,1)} %get-tuple-element.60.refs_0_), channel_id=1, source_target_pairs={{8,0},{16,8},{24,16},{28,24},{20,28},{12,20},{4,12},{0,4},{9,1},{1... | collective-permute-start | bytes 1671176 | tf_op jit(solution)/shard_map/ppermute | solution.py:246
  87.1 23.9 %collective-permute-start.20 = (bf16[1088,256]{1,0:T(8,128)(2,1)}, bf16[1088,256]{1,0:T(8,128)(2,1)}, u32[]{:S(2)}, u32[]{:S(2)}) collective-permute-start(bf16[1088,256]{1,0:T(8,128)(2,1)} %collective-permute-done.18.refs_6_), channel_id=1, source_target_pairs={{8,0},{16,8},{24,16},{28,24},{20,28},{12,20},{4,12},{0,4},{9,1},{1... | collective-permute-start | bytes 1671176 | tf_op jit(solution)/shard_map/ppermute | solution.py:246
  87.8 23.2 %collective-permute-start.19 = (bf16[1088,256]{1,0:T(8,128)(2,1)}, bf16[1088,256]{1,0:T(8,128)(2,1)}, u32[]{:S(2)}, u32[]{:S(2)}) collective-permute-start(bf16[1088,256]{1,0:T(8,128)(2,1)} %collective-permute-done.5.refs_5_), channel_id=1, source_target_pairs={{0,8},{8,16},{16,24},{24,28},{28,20},{20,12},{12,4},{4,0},{1,9},{9... | collective-permute-start | bytes 1671176 | tf_op jit(solution)/shard_map/ppermute | solution.py:244
  99.1 23.9 %collective-permute-start.10 = (bf16[1088,256]{1,0:T(8,128)(2,1)S(1)}, bf16[1088,256]{1,0:T(8,128)(2,1)}, u32[]{:S(2)}, u32[]{:S(2)}) collective-permute-start(bf16[1088,256]{1,0:T(8,128)(2,1)S(1)} %copy-done.5), channel_id=1, source_target_pairs={{8,0},{16,8},{24,16},{28,24},{20,28},{12,20},{4,12},{0,4},{9,1},{1... | collective-permute-start | bytes 1671176 | tf_op jit(solution)/shard_map/ppermute | solution.py:246
  99.1 23.9 %collective-permute-start.9 = (bf16[1088,256]{1,0:T(8,128)(2,1)S(1)}, bf16[1088,256]{1,0:T(8,128)(2,1)}, u32[]{:S(2)}, u32[]{:S(2)}) collective-permute-start(bf16[1088,256]{1,0:T(8,128)(2,1)S(1)} %copy-done.5), channel_id=1, source_target_pairs={{0,8},{8,16},{16,24},{24,28},{28,20},{20,12},{12,4},{4,0},{1,9},{9... | collective-permute-start | bytes 1671176 | tf_op jit(solution)/shard_map/ppermute | solution.py:244
  111.0 21.7 %collective-permute-start.26 = (bf16[1088,256]{1,0:T(8,128)(2,1)}, bf16[1088,256]{1,0:T(8,128)(2,1)}, u32[]{:S(2)}, u32[]{:S(2)}) collective-permute-start(bf16[1088,256]{1,0:T(8,128)(2,1)} %collective-permute-done.7.refs_1_), channel_id=1, source_target_pairs={{0,8},{8,16},{16,24},{24,28},{28,20},{20,12},{12,4},{4,0},{1,9},{9... | collective-permute-start | bytes 1671176 | tf_op jit(solution)/shard_map/ppermute | solution.py:244
  112.6 22.3 %collective-permute-start.27 = (bf16[1088,256]{1,0:T(8,128)(2,1)}, bf16[1088,256]{1,0:T(8,128)(2,1)}, u32[]{:S(2)}, u32[]{:S(2)}) collective-permute-start(bf16[1088,256]{1,0:T(8,128)(2,1)} %collective-permute-done.8.refs_2_), channel_id=1, source_target_pairs={{8,0},{16,8},{24,16},{28,24},{20,28},{12,20},{4,12},{0,4},{9,1},{1... | collective-permute-start | bytes 1671176 | tf_op jit(solution)/shard_map/ppermute | solution.py:246
  123.0 21.6 %collective-permute-start.21 = (bf16[1088,256]{1,0:T(8,128)(2,1)}, bf16[1088,256]{1,0:T(8,128)(2,1)S(1)}, u32[]{:S(2)}, u32[]{:S(2)}) collective-permute-start(bf16[1088,256]{1,0:T(8,128)(2,1)} %collective-permute-done.9.refs_1_), channel_id=1, source_target_pairs={{0,8},{8,16},{16,24},{24,28},{28,20},{20,12},{12,4},{4,0},{1,9},{9... | collective-permute-start | bytes 1671176 | tf_op jit(solution)/shard_map/ppermute | solution.py:244
  124.5 22.2 %collective-permute-start.22 = (bf16[1088,256]{1,0:T(8,128)(2,1)}, bf16[1088,256]{1,0:T(8,128)(2,1)S(1)}, u32[]{:S(2)}, u32[]{:S(2)}) collective-permute-start(bf16[1088,256]{1,0:T(8,128)(2,1)} %collective-permute-done.10.refs_2_), channel_id=1, source_target_pairs={{8,0},{16,8},{24,16},{28,24},{20,28},{12,20},{4,12},{0,4},{9,1},{1... | collective-permute-start | bytes 1671176 | tf_op jit(solution)/shard_map/ppermute | solution.py:246
  134.9 21.6 %collective-permute-start.28 = (bf16[1088,256]{1,0:T(8,128)(2,1)}, bf16[1088,256]{1,0:T(8,128)(2,1)S(1)}, u32[]{:S(2)}, u32[]{:S(2)}) collective-permute-start(bf16[1088,256]{1,0:T(8,128)(2,1)} %collective-permute-done.26.refs_3_), channel_id=1, source_target_pairs={{0,8},{8,16},{16,24},{24,28},{28,20},{20,12},{12,4},{4,0},{1,9},{9... | collective-permute-start | bytes 1671176 | tf_op jit(solution)/shard_map/ppermute | solution.py:244
  136.5 22.2 %collective-permute-start.29 = (bf16[1088,256]{1,0:T(8,128)(2,1)}, bf16[1088,256]{1,0:T(8,128)(2,1)S(1)}, u32[]{:S(2)}, u32[]{:S(2)}) collective-permute-start(bf16[1088,256]{1,0:T(8,128)(2,1)} %collective-permute-done.27.refs_4_), channel_id=1, source_target_pairs={{8,0},{16,8},{24,16},{28,24},{20,28},{12,20},{4,12},{0,4},{9,1},{1... | collective-permute-start | bytes 1671176 | tf_op jit(solution)/shard_map/ppermute | solution.py:246
  146.7 21.7 %collective-permute-start.24 = (bf16[1088,256]{1,0:T(8,128)(2,1)S(1)}, bf16[1088,256]{1,0:T(8,128)(2,1)S(1)}, u32[]{:S(2)}, u32[]{:S(2)}) collective-permute-start(bf16[1088,256]{1,0:T(8,128)(2,1)S(1)} %collective-permute-done.21.refs_3_), channel_id=1, source_target_pairs={{0,8},{8,16},{16,24},{24,28},{28,20},{20,12},{12,4},{4,0},{1,9},{9... | collective-permute-start | bytes 1671176 | tf_op jit(solution)/shard_map/ppermute | solution.py:244
  148.3 22.3 %collective-permute-start.25 = (bf16[1088,256]{1,0:T(8,128)(2,1)S(1)}, bf16[1088,256]{1,0:T(8,128)(2,1)S(1)}, u32[]{:S(2)}, u32[]{:S(2)}) collective-permute-start(bf16[1088,256]{1,0:T(8,128)(2,1)S(1)} %collective-permute-done.22.refs_4_), channel_id=1, source_target_pairs={{8,0},{16,8},{24,16},{28,24},{20,28},{12,20},{4,12},{0,4},{9,1},{1... | collective-permute-start | bytes 1671176 | tf_op jit(solution)/shard_map/ppermute | solution.py:246
  (56 other events, 1065.9 us)

commit v4 on v3

--- a/solution.py
+++ b/solution.py
@@ -191,7 +191,7 @@
     tok_rows = pieces[0].shape[0]
     columns = weights[0].shape[1]
     final = total is not None
-    tile = tok_rows if final else 256
+    tile = tok_rows // 2 if final else 512
     row_spec = pl.BlockSpec((tile, columns), lambda i: (i, 0))
 
     def weight_spec(head):
@@ -294,7 +294,9 @@
     rings = [
         Ring(chunk, devices, way)
         for chunk, way in zip(
-            project_kv(tokens, w_key, w_value, start, end, (0, 1)), WAYS[:2], strict=True
+            [project_kv(tokens, w_key, w_value, start, end, (head,))[0] for head in (0, 1)],
+            WAYS[:2],
+            strict=True,
         )
     ]
     started, kernels = [], []
@@ -305,13 +307,13 @@
             after(table, *needed), owner_ids, queries, rings[head].buffers, head, devices, share
         )
         pieces[0, head] = own
+        pieces[2, head] = to_head(own, 2)
         pieces[1, head] = to_head(own, 1)
-        pieces[2, head] = to_head(own, 2)
         if head < heads - 1:
             pieces[3, head] = to_head(pieces[2, head], 1)
         return own
 
-    out_weights = {0: lax.dynamic_slice_in_dim(w_out, group * columns, columns, 1)}
+    out_weights = {}
     for turn, moves in enumerate(turns):
         needed = [*(started[-2] if turn > 1 else ()), *(kernels[-1] if turn > 0 else ())]
         begun, ran = [], []
@@ -327,16 +329,16 @@
             queries = jnp.dot(after(tokens, *needed), w_query, preferred_element_type=jnp.float32)
             queries = queries.astype(jnp.bfloat16)
             ran.append(queries)
-        if turn in (2, 3):
-            for flip in ((2,), (3, 1))[(2, 3).index(turn)]:
+        if turn in (3, 4):
+            for flip in ((2, 0), (3, 1))[(3, 4).index(turn)]:
                 part = lax.dynamic_slice_in_dim(
                     after(w_out, *needed), (group ^ flip) * columns, columns, 1
                 )
-                out_weights[flip] = to_head(part, flip)
+                out_weights[flip] = to_head(part, flip) if flip else part
                 begun.append(out_weights[flip])
         if turn in (joined + 2, joined + 3):
             ran.append(finish(turn - joined - 2, *needed))
-        if turn in (joined + 3, joined + 4):
+        if turn in (joined + 3, joined + 3 + 1):
             begun.append(pieces[2, turn - joined - 3])
         if turn == len(turns) - 1:
             ran.append(finish(2, *needed))

time: 207 us -> 202 us (0.976)
  waiting for transfers between devices: 102 us -> 93.7 us
  Pallas kernels: 42.9 us -> 47.1 us
    ppermute x15, waiting for transfers between devices: 33.9 us -> 27.7 us  [step(): given.append(lax.ppermute(behind, 'seq', self.backward))]
    pallas_call x2 -> x3, Pallas kernels: 14.2 us -> 19.4 us  [project_kv(): pl.pallas_call(functools.partial(kv_kernel, heads), grid=(1,), in_specs=[...]
    unnamed x73 -> x75, local copies, waits for them, and re-layouts: 6.11 us -> 5.43 us
  transfers between devices with their start and end apart: 45 -> 45, of which waited for: 28 -> 29; matrix products, arithmetic and copies ran while one was open for 6% -> 6% of each run, Pallas kernels for 16% -> 19%
where the time goes in v4:
time: 202 us; the launch traced here: 201 us
  waiting for transfers between devices  93.7 us (46%)
  Pallas kernels  47.1 us (23%)
  starting transfers between devices  41.3 us (20%)
  local copies, waits for them, and re-layouts  11.4 us (6%)
  matrix products  5.18 us (3%)
  other arithmetic  2.07 us (1%)
    ppermute x15, waiting for transfers between devices, step(): given.append(lax.ppermute(ahead, 'seq', self.forward))  58.7 us
    ppermute x15, waiting for transfers between devices, step(): given.append(lax.ppermute(behind, 'seq', self.backward))  27.7 us
    ppermute x15, starting transfers between devices, step(): given.append(lax.ppermute(ahead, 'seq', self.forward))  25.9 us
    pallas_call x3, Pallas kernels, project_kv(): pl.pallas_call(functools.partial(kv_kernel, heads), grid=(1,), in_specs=[...  19.4 us
    pallas_call x4, Pallas kernels, attend(): pl.pallas_call(functools.partial(attend_kernel, devices), grid=(1,), in_s...  19.3 us
    ppermute x15, starting transfers between devices, to_head(): return lax.ppermute(value, 'head', [(g, g ^ flip) for g in range(groups)])  9.18 us
    pallas_call x2, Pallas kernels, project_out(): pl.pallas_call(functools.partial(out_kernel, len(pieces), final), grid=(t...  8.34 us
    ppermute x15, waiting for transfers between devices, to_head(): return lax.ppermute(value, 'head', [(g, g ^ flip) for g in range(groups)])  7.26 us
  transfers between devices with their start and end apart: 45, of which 29 were waited for; matrix products, arithmetic and copies ran while one was open for 6% of the time, Pallas kernels for 19%

profile of v4, /device:TPU:0, one launch (start us, length us, event | category | flops | bytes accessed | tf_op | source)
XLA Modules:
  0.0 201.0 jit_solution(2263730130542135923)
XLA Ops:
  1.4 6.2 %project_kv.3.refs_0_ = bf16[1088,256]{1,0:T(8,128)(2,1)} custom-call(bf16[1024,2048]{1,0:T(8,128)(2,1)} %tokens_ref.4, bf16[2048,512]{1,0:T(8,128)(2,1)} %wk_ref.5, bf16[2048,512]{1,0:T(8,128)(2,1)} %wv_ref.5, s32[1,64]{1,0:T(1,128)} %get-tuple-element.92.start_ref, s32[1,64]{1,0:T(1,128)} %get-tuple-element.91.end_ref), custom_call_target="tpu_custom_call" | custom-call | flops 1073741824 | bytes 6291456 | tf_op jit(solution)/shard_map/project_kv/pallas_call | solution.py:80
  7.5 3.1 %collective-permute-start = (bf16[1088,256]{1,0:T(8,128)(2,1)}, bf16[1088,256]{1,0:T(8,128)(2,1)S(1)}, u32[]{:S(2)}, u32[]{:S(2)}) collective-permute-start(bf16[1088,256]{1,0:T(8,128)(2,1)} %project_kv.3.refs_0_), channel_id=1, source_target_pairs={{0,8},{8,16},{16,24},{24,28},{28,20},{20,12},{12,4},{4,0},{1,9},{9... | collective-permute-start | bytes 1671176 | tf_op jit(solution)/shard_map/ppermute | solution.py:244
  10.6 6.2 %project_kv.5.refs_0_ = bf16[1088,256]{1,0:T(8,128)(2,1)} custom-call(bf16[1024,2048]{1,0:T(8,128)(2,1)} %tokens_ref.4, bf16[2048,512]{1,0:T(8,128)(2,1)} %wk_ref.5, bf16[2048,512]{1,0:T(8,128)(2,1)} %wv_ref.5, s32[1,64]{1,0:T(1,128)} %get-tuple-element.92.start_ref, s32[1,64]{1,0:T(1,128)} %get-tuple-element.91.end_ref), custom_call_target="tpu_custom_call" | custom-call | flops 1073741824 | bytes 6291456 | tf_op jit(solution)/shard_map/project_kv/pallas_call | solution.py:80
  18.9 5.3 %collective-permute-done.refs_1_ = bf16[1088,256]{1,0:T(8,128)(2,1)S(1)} collective-permute-done((bf16[1088,256]{1,0:T(8,128)(2,1)}, bf16[1088,256]{1,0:T(8,128)(2,1)S(1)}, u32[]{:S(2)}, u32[]{:S(2)}) %collective-permute-start) | collective-permute-done | bytes 557088 | tf_op jit(solution)/shard_map/ppermute | solution.py:244
  28.4 7.8 %collective-permute-done.12.refs_1_ = bf16[1088,256]{1,0:T(8,128)(2,1)S(1)} collective-permute-done((bf16[1088,256]{1,0:T(8,128)(2,1)}, bf16[1088,256]{1,0:T(8,128)(2,1)S(1)}, u32[]{:S(2)}, u32[]{:S(2)}) %collective-permute-start.12) | collective-permute-done | bytes 557088 | tf_op jit(solution)/shard_map/ppermute | solution.py:244
  39.9 2.2 %constant_dynamic-slice_fusion = (bf16[512,512]{1,0:T(8,128)(2,1)}, bf16[512,512]{1,0:T(8,128)(2,1)}) fusion(bf16[512,2048]{1,0:T(8,128)(2,1)} %param.17, s32[]{:T(128)S(6)} %select_n.37, s32[]{:T(128)S(6)} %select_n.36), kind=kLoop, calls=%fused_computation.8 | loop fusion | bytes 2097160 | tf_op jit(solution)/shard_map/dynamic_slice | solution.py:334
  44.1 4.1 %collective-permute-done.2.refs_3_ = bf16[1088,256]{1,0:T(8,128)(2,1)} collective-permute-done((bf16[1088,256]{1,0:T(8,128)(2,1)S(1)}, bf16[1088,256]{1,0:T(8,128)(2,1)}, u32[]{:S(2)}, u32[]{:S(2)}) %collective-permute-start.2) | collective-permute-done | bytes 557088 | tf_op jit(solution)/shard_map/ppermute | solution.py:244
  52.4 2.3 %constant_dynamic-slice_fusion.2 = (bf16[512,512]{1,0:T(8,128)(2,1)}, bf16[512,512]{1,0:T(8,128)(2,1)}) fusion(bf16[512,2048]{1,0:T(8,128)(2,1)} %param.17, s32[]{:T(128)S(6)} %select_n.35, s32[]{:T(128)S(6)} %select_n.34), kind=kLoop, calls=%fused_computation.10 | loop fusion | bytes 2097160 | tf_op jit(solution)/shard_map/dynamic_slice | solution.py:334
  54.8 5.3 %collective-permute-done.14.refs_3_ = bf16[1088,256]{1,0:T(8,128)(2,1)S(1)} collective-permute-done((bf16[1088,256]{1,0:T(8,128)(2,1)S(1)}, bf16[1088,256]{1,0:T(8,128)(2,1)S(1)}, u32[]{:S(2)}, u32[]{:S(2)}) %collective-permute-start.14) | collective-permute-done | bytes 557088 | tf_op jit(solution)/shard_map/ppermute | solution.py:244
  60.0 7.1 %project_kv.4 = (bf16[1088,256]{1,0:T(8,128)(2,1)}, bf16[1088,256]{1,0:T(8,128)(2,1)}) custom-call(bf16[1024,2048]{1,0:T(8,128)(2,1)} %tokens_ref.4, bf16[2048,512]{1,0:T(8,128)(2,1)} %wk_ref.5, bf16[2048,512]{1,0:T(8,128)(2,1)} %wv_ref.5, s32[1,64]{1,0:T(1,128)} %get-tuple-element.92.start_ref, s32[1,64]{1,0:T(1,128)} %get-tuple-element.91.end_ref), custom_call_target="tpu_custom_call" | custom-call | flops 2147483648 | bytes 6291456 | tf_op jit(solution)/shard_map/project_kv/pallas_call | solution.py:80
  67.3 2.2 %collective-permute-start.17 = (bf16[1088,256]{1,0:T(8,128)(2,1)S(1)}, bf16[1088,256]{1,0:T(8,128)(2,1)S(1)}, u32[]{:S(2)}, u32[]{:S(2)}) collective-permute-start(bf16[1088,256]{1,0:T(8,128)(2,1)S(1)} %collective-permute-done.14.refs_3_), channel_id=1, source_target_pairs={{0,8},{8,16},{16,24},{24,28},{28,20},{20,12},{12,4},{4,0},{1,9},{9... | collective-permute-start | bytes 1671176 | tf_op jit(solution)/shard_map/ppermute | solution.py:244
  75.2 5.2 %convolution_convert_fusion.q_ref = bf16[1024,512]{1,0:T(8,128)(2,1)S(1)} fusion(bf16[1024,2048]{1,0:T(8,128)(2,1)} %tokens_ref.4, bf16[2048,512]{1,0:T(8,128)(2,1)} %param.14), kind=kOutput, calls=%fused_computation.1 | convolution fusion | flops 2148007936 | bytes 7340032 | tf_op jit(solution)/shard_map/dot_general | solution.py:329
  80.4 3.1 %collective-permute-done.17.refs_5_ = bf16[1088,256]{1,0:T(8,128)(2,1)S(1)} collective-permute-done((bf16[1088,256]{1,0:T(8,128)(2,1)S(1)}, bf16[1088,256]{1,0:T(8,128)(2,1)S(1)}, u32[]{:S(2)}, u32[]{:S(2)}) %collective-permute-start.17) | collective-permute-done | bytes 557088 | tf_op jit(solution)/shard_map/ppermute | solution.py:244
  87.1 8.4 %collective-permute-done.8.refs_1_ = bf16[1088,256]{1,0:T(8,128)(2,1)} collective-permute-done((bf16[1088,256]{1,0:T(8,128)(2,1)}, bf16[1088,256]{1,0:T(8,128)(2,1)}, u32[]{:S(2)}, u32[]{:S(2)}) %collective-permute-start.8) | collective-permute-done | bytes 557088 | tf_op jit(solution)/shard_map/ppermute | solution.py:244
  100.6 8.3 %collective-permute-done.20.refs_7_ = bf16[1088,256]{1,0:T(8,128)(2,1)} collective-permute-done((bf16[1088,256]{1,0:T(8,128)(2,1)}, bf16[1088,256]{1,0:T(8,128)(2,1)}, u32[]{:S(2)}, u32[]{:S(2)}) %collective-permute-start.20) | collective-permute-done | bytes 557088 | tf_op jit(solution)/shard_map/ppermute | solution.py:246
  113.8 5.0 %attend.4.refs_0_ = bf16[1024,128]{1,0:T(8,128)(2,1)S(1)} custom-call(s32[8,9]{1,0:T(8,128)S(1)} %pad_add_fusion.table_ref, s32[8]{0:T(128)S(1)} %gather_fusion, bf16[1024,512]{1,0:T(8,128)(2,1)S(1)} %convolution_convert_fusion.q_ref, bf16[1088,256]{1,0:T(8,128)(2,1)S(1)} %copy-done.2, bf16[1088,256]{1,0:T(8,128)(2,1)S(1)} %copy-done.11, ...), custom_call_target="tpu_custom_call" | custom-call | flops 603979776 | bytes 4194304 | tf_op jit(solution)/shard_map/attend/pallas_call | solution.py:157
  124.4 4.7 %attend.5.refs_4_ = bf16[1024,128]{1,0:T(8,128)(2,1)S(1)} custom-call(s32[8,9]{1,0:T(8,128)S(1)} %pad_add_fusion.table_ref, s32[8]{0:T(128)S(1)} %gather_fusion, bf16[1024,512]{1,0:T(8,128)(2,1)S(1)} %convolution_convert_fusion.q_ref, bf16[1088,256]{1,0:T(8,128)(2,1)S(1)} %copy-done.1, bf16[1088,256]{1,0:T(8,128)(2,1)S(1)} %collective-permute-done.12.refs_1_, ...), custom_call_target="tpu_custom_call" | custom-call | flops 603979776 | bytes 4194304 | tf_op jit(solution)/shard_map/attend/pallas_call | solution.py:157
  134.8 8.3 %collective-permute-done.21.refs_3_ = bf16[1088,256]{1,0:T(8,128)(2,1)S(1)} collective-permute-done((bf16[1088,256]{1,0:T(8,128)(2,1)}, bf16[1088,256]{1,0:T(8,128)(2,1)S(1)}, u32[]{:S(2)}, u32[]{:S(2)}) %collective-permute-start.21) | collective-permute-done | bytes 557088 | tf_op jit(solution)/shard_map/ppermute | solution.py:244
  148.2 5.6 %collective-permute-done.30.refs_5_ = bf16[1024,128]{1,0:T(8,128)(2,1)S(1)} collective-permute-done((bf16[1024,128]{1,0:T(8,128)(2,1)S(1)}, bf16[1024,128]{1,0:T(8,128)(2,1)S(1)}, u32[]{:S(2)}, u32[]{:S(2)}) %collective-permute-start.30) | collective-permute-done | bytes 262176 | tf_op jit(solution)/shard_map/ppermute | solution.py:288
  158.8 8.2 %collective-permute-done.24.refs_5_ = bf16[1088,256]{1,0:T(8,128)(2,1)S(1)} collective-permute-done((bf16[1088,256]{1,0:T(8,128)(2,1)S(1)}, bf16[1088,256]{1,0:T(8,128)(2,1)S(1)}, u32[]{:S(2)}, u32[]{:S(2)}) %collective-permute-start.24) | collective-permute-done | bytes 557088 | tf_op jit(solution)/shard_map/ppermute | solution.py:244
  174.5 4.6 %attend.6.refs_8_ = bf16[1024,128]{1,0:T(8,128)(2,1)S(1)} custom-call(s32[8,9]{1,0:T(8,128)S(1)} %pad_add_fusion.table_ref, s32[8]{0:T(128)S(1)} %gather_fusion, bf16[1024,512]{1,0:T(8,128)(2,1)S(1)} %convolution_convert_fusion.q_ref, bf16[1088,256]{1,0:T(8,128)(2,1)S(1)} %copy-done.14, bf16[1088,256]{1,0:T(8,128)(2,1)} %collective-permute-done.8.refs_1_, ...), custom_call_target="tpu_custom_call" | custom-call | flops 603979776 | bytes 4194304 | tf_op jit(solution)/shard_map/attend/pallas_call | solution.py:157
  181.3 5.0 %attend.7.refs_12_ = bf16[1024,128]{1,0:T(8,128)(2,1)} custom-call(s32[8,9]{1,0:T(8,128)S(1)} %pad_add_fusion.table_ref, s32[8]{0:T(128)S(1)} %gather_fusion, bf16[1024,512]{1,0:T(8,128)(2,1)S(1)} %convolution_convert_fusion.q_ref, bf16[1088,256]{1,0:T(8,128)(2,1)S(1)} %copy-done.7, bf16[1088,256]{1,0:T(8,128)(2,1)} %collective-permute-done.10.refs_1_, ...), custom_call_target="tpu_custom_call" | custom-call | flops 603979776 | bytes 4194304 | tf_op jit(solution)/shard_map/attend/pallas_call | solution.py:157
  190.4 5.4 %project_out.2.refs_4_ = f32[1024,512]{1,0:T(8,128)} custom-call(bf16[1024,128]{1,0:T(8,128)(2,1)} %copy-done.3, bf16[1024,128]{1,0:T(8,128)(2,1)} %copy-done.21, bf16[1024,128]{1,0:T(8,128)(2,1)} %copy-done.23, bf16[1024,128]{1,0:T(8,128)(2,1)} %copy-done.25, bf16[1024,128]{1,0:T(8,128)(2,1)} %copy-done.4, bf16[1024,128]{1,0:T(8,128)(2,1)} %copy-done.22, ...), custom_call_target="tpu_custom_call" | custom-call | flops 1879048192 | bytes 6291456 | tf_op jit(solution)/shard_map/project_out/pallas_call | solution.py:200
  198.1 2.9 %project_out.3 = bf16[1024,512]{1,0:T(8,128)(2,1)} custom-call(bf16[1024,128]{1,0:T(8,128)(2,1)} %copy-done.29, bf16[1024,128]{1,0:T(8,128)(2,1)} %copy-done.31, bf16[512,512]{1,0:T(8,128)(2,1)} %copy-done.20, bf16[512,512]{1,0:T(8,128)(2,1)} %collective-permute-done.6.refs_17_.refs_21_.refs_25_.refs_3_, f32[1024,512]{1,0:T(8,128)} %project_out.2.refs_4_), custom_call_target="tpu_custom_call" | custom-call | flops 268435456 | bytes 6291456 | tf_op jit(solution)/shard_map/project_out/pallas_call | solution.py:200
  (164 shorter events, 74.3 us)
Async XLA Ops:
  7.5 16.7 %collective-permute-start = (bf16[1088,256]{1,0:T(8,128)(2,1)}, bf16[1088,256]{1,0:T(8,128)(2,1)S(1)}, u32[]{:S(2)}, u32[]{:S(2)}) collective-permute-start(bf16[1088,256]{1,0:T(8,128)(2,1)} %project_kv.3.refs_0_), channel_id=1, source_target_pairs={{0,8},{8,16},{16,24},{24,28},{28,20},{20,12},{12,4},{4,0},{1,9},{9... | collective-permute-start | bytes 1671176 | tf_op jit(solution)/shard_map/ppermute | solution.py:244
  16.8 19.4 %collective-permute-start.12 = (bf16[1088,256]{1,0:T(8,128)(2,1)}, bf16[1088,256]{1,0:T(8,128)(2,1)S(1)}, u32[]{:S(2)}, u32[]{:S(2)}) collective-permute-start(bf16[1088,256]{1,0:T(8,128)(2,1)} %project_kv.5.refs_0_), channel_id=1, source_target_pairs={{0,8},{8,16},{16,24},{24,28},{28,20},{20,12},{12,4},{4,0},{1,9},{9... | collective-permute-start | bytes 1671176 | tf_op jit(solution)/shard_map/ppermute | solution.py:244
  18.9 19.4 %collective-permute-start.13 = (bf16[1088,256]{1,0:T(8,128)(2,1)}, bf16[1088,256]{1,0:T(8,128)(2,1)S(1)}, u32[]{:S(2)}, u32[]{:S(2)}) collective-permute-start(bf16[1088,256]{1,0:T(8,128)(2,1)} %project_kv.5.refs_0_), channel_id=1, source_target_pairs={{8,0},{16,8},{24,16},{28,24},{20,28},{12,20},{4,12},{0,4},{9,1},{1... | collective-permute-start | bytes 1671176 | tf_op jit(solution)/shard_map/ppermute | solution.py:246
  26.4 21.8 %collective-permute-start.2 = (bf16[1088,256]{1,0:T(8,128)(2,1)S(1)}, bf16[1088,256]{1,0:T(8,128)(2,1)}, u32[]{:S(2)}, u32[]{:S(2)}) collective-permute-start(bf16[1088,256]{1,0:T(8,128)(2,1)S(1)} %collective-permute-done.refs_1_), channel_id=1, source_target_pairs={{0,8},{8,16},{16,24},{24,28},{28,20},{20,12},{12,4},{4,0},{1,9},{9... | collective-permute-start | bytes 1671176 | tf_op jit(solution)/shard_map/ppermute | solution.py:244
  28.0 22.4 %collective-permute-start.3 = (bf16[1088,256]{1,0:T(8,128)(2,1)S(1)}, bf16[1088,256]{1,0:T(8,128)(2,1)}, u32[]{:S(2)}, u32[]{:S(2)}) collective-permute-start(bf16[1088,256]{1,0:T(8,128)(2,1)S(1)} %collective-permute-done.1.refs_2_), channel_id=1, source_target_pairs={{8,0},{16,8},{24,16},{28,24},{20,28},{12,20},{4,12},{0,4},{9,1},{1... | collective-permute-start | bytes 1671176 | tf_op jit(solution)/shard_map/ppermute | solution.py:246
  38.3 21.7 %collective-permute-start.14 = (bf16[1088,256]{1,0:T(8,128)(2,1)S(1)}, bf16[1088,256]{1,0:T(8,128)(2,1)S(1)}, u32[]{:S(2)}, u32[]{:S(2)}) collective-permute-start(bf16[1088,256]{1,0:T(8,128)(2,1)S(1)} %collective-permute-done.12.refs_1_), channel_id=1, source_target_pairs={{0,8},{8,16},{16,24},{24,28},{28,20},{20,12},{12,4},{4,0},{1,9},{9... | collective-permute-start | bytes 1671176 | tf_op jit(solution)/shard_map/ppermute | solution.py:244
  43.6 23.5 %collective-permute-start.15 = (bf16[1088,256]{1,0:T(8,128)(2,1)S(1)}, bf16[1088,256]{1,0:T(8,128)(2,1)S(1)}, u32[]{:S(2)}, u32[]{:S(2)}) collective-permute-start(bf16[1088,256]{1,0:T(8,128)(2,1)S(1)} %collective-permute-done.13.refs_2_), channel_id=1, source_target_pairs={{8,0},{16,8},{24,16},{28,24},{20,28},{12,20},{4,12},{0,4},{9,1},{1... | collective-permute-start | bytes 1671176 | tf_op jit(solution)/shard_map/ppermute | solution.py:246
  50.4 21.2 %collective-permute-start.4 = (bf16[1088,256]{1,0:T(8,128)(2,1)}, bf16[1088,256]{1,0:T(8,128)(2,1)}, u32[]{:S(2)}, u32[]{:S(2)}) collective-permute-start(bf16[1088,256]{1,0:T(8,128)(2,1)} %collective-permute-done.2.refs_3_), channel_id=1, source_target_pairs={{0,8},{8,16},{16,24},{24,28},{28,20},{20,12},{12,4},{4,0},{1,9},{9... | collective-permute-start | bytes 1671176 | tf_op jit(solution)/shard_map/ppermute | solution.py:244
  51.9 21.2 %collective-permute-start.5 = (bf16[1088,256]{1,0:T(8,128)(2,1)}, bf16[1088,256]{1,0:T(8,128)(2,1)}, u32[]{:S(2)}, u32[]{:S(2)}) collective-permute-start(bf16[1088,256]{1,0:T(8,128)(2,1)} %collective-permute-done.3.refs_4_), channel_id=1, source_target_pairs={{8,0},{16,8},{24,16},{28,24},{20,28},{12,20},{4,12},{0,4},{9,1},{1... | collective-permute-start | bytes 1671176 | tf_op jit(solution)/shard_map/ppermute | solution.py:246
  73.1 22.4 %collective-permute-start.8 = (bf16[1088,256]{1,0:T(8,128)(2,1)}, bf16[1088,256]{1,0:T(8,128)(2,1)}, u32[]{:S(2)}, u32[]{:S(2)}) collective-permute-start(bf16[1088,256]{1,0:T(8,128)(2,1)} %get-tuple-element.57.refs_0_), channel_id=1, source_target_pairs={{0,8},{8,16},{16,24},{24,28},{28,20},{20,12},{12,4},{4,0},{1,9},{9... | collective-permute-start | bytes 1671176 | tf_op jit(solution)/shard_map/ppermute | solution.py:244
  74.7 22.3 %collective-permute-start.9 = (bf16[1088,256]{1,0:T(8,128)(2,1)}, bf16[1088,256]{1,0:T(8,128)(2,1)}, u32[]{:S(2)}, u32[]{:S(2)}) collective-permute-start(bf16[1088,256]{1,0:T(8,128)(2,1)} %get-tuple-element.57.refs_0_), channel_id=1, source_target_pairs={{8,0},{16,8},{24,16},{28,24},{20,28},{12,20},{4,12},{0,4},{9,1},{1... | collective-permute-start | bytes 1671176 | tf_op jit(solution)/shard_map/ppermute | solution.py:246
  85.1 23.9 %collective-permute-start.20 = (bf16[1088,256]{1,0:T(8,128)(2,1)}, bf16[1088,256]{1,0:T(8,128)(2,1)}, u32[]{:S(2)}, u32[]{:S(2)}) collective-permute-start(bf16[1088,256]{1,0:T(8,128)(2,1)} %collective-permute-done.18.refs_6_), channel_id=1, source_target_pairs={{8,0},{16,8},{24,16},{28,24},{20,28},{12,20},{4,12},{0,4},{9,1},{1... | collective-permute-start | bytes 1671176 | tf_op jit(solution)/shard_map/ppermute | solution.py:246
  86.0 22.9 %collective-permute-start.19 = (bf16[1088,256]{1,0:T(8,128)(2,1)}, bf16[1088,256]{1,0:T(8,128)(2,1)}, u32[]{:S(2)}, u32[]{:S(2)}) collective-permute-start(bf16[1088,256]{1,0:T(8,128)(2,1)} %collective-permute-done.4.refs_5_), channel_id=1, source_target_pairs={{0,8},{8,16},{16,24},{24,28},{28,20},{20,12},{12,4},{4,0},{1,9},{9... | collective-permute-start | bytes 1671176 | tf_op jit(solution)/shard_map/ppermute | solution.py:244
  97.0 22.4 %collective-permute-start.10 = (bf16[1088,256]{1,0:T(8,128)(2,1)S(1)}, bf16[1088,256]{1,0:T(8,128)(2,1)}, u32[]{:S(2)}, u32[]{:S(2)}) collective-permute-start(bf16[1088,256]{1,0:T(8,128)(2,1)S(1)} %copy-done.6), channel_id=1, source_target_pairs={{0,8},{8,16},{16,24},{24,28},{28,20},{20,12},{12,4},{4,0},{1,9},{9... | collective-permute-start | bytes 1671176 | tf_op jit(solution)/shard_map/ppermute | solution.py:244
  98.6 22.3 %collective-permute-start.11 = (bf16[1088,256]{1,0:T(8,128)(2,1)S(1)}, bf16[1088,256]{1,0:T(8,128)(2,1)}, u32[]{:S(2)}, u32[]{:S(2)}) collective-permute-start(bf16[1088,256]{1,0:T(8,128)(2,1)S(1)} %copy-done.6), channel_id=1, source_target_pairs={{8,0},{16,8},{24,16},{28,24},{20,28},{12,20},{4,12},{0,4},{9,1},{1... | collective-permute-start | bytes 1671176 | tf_op jit(solution)/shard_map/ppermute | solution.py:246
  108.9 22.4 %collective-permute-start.26 = (bf16[1088,256]{1,0:T(8,128)(2,1)}, bf16[1088,256]{1,0:T(8,128)(2,1)}, u32[]{:S(2)}, u32[]{:S(2)}) collective-permute-start(bf16[1088,256]{1,0:T(8,128)(2,1)} %collective-permute-done.8.refs_1_), channel_id=1, source_target_pairs={{0,8},{8,16},{16,24},{24,28},{28,20},{20,12},{12,4},{4,0},{1,9},{9... | collective-permute-start | bytes 1671176 | tf_op jit(solution)/shard_map/ppermute | solution.py:244
  110.5 22.3 %collective-permute-start.27 = (bf16[1088,256]{1,0:T(8,128)(2,1)}, bf16[1088,256]{1,0:T(8,128)(2,1)}, u32[]{:S(2)}, u32[]{:S(2)}) collective-permute-start(bf16[1088,256]{1,0:T(8,128)(2,1)} %collective-permute-done.9.refs_2_), channel_id=1, source_target_pairs={{8,0},{16,8},{24,16},{28,24},{20,28},{12,20},{4,12},{0,4},{9,1},{1... | collective-permute-start | bytes 1671176 | tf_op jit(solution)/shard_map/ppermute | solution.py:246
  120.9 22.3 %collective-permute-start.21 = (bf16[1088,256]{1,0:T(8,128)(2,1)}, bf16[1088,256]{1,0:T(8,128)(2,1)S(1)}, u32[]{:S(2)}, u32[]{:S(2)}) collective-permute-start(bf16[1088,256]{1,0:T(8,128)(2,1)} %collective-permute-done.10.refs_1_), channel_id=1, source_target_pairs={{0,8},{8,16},{16,24},{24,28},{28,20},{20,12},{12,4},{4,0},{1,9},{9... | collective-permute-start | bytes 1671176 | tf_op jit(solution)/shard_map/ppermute | solution.py:244
  122.5 22.2 %collective-permute-start.22 = (bf16[1088,256]{1,0:T(8,128)(2,1)}, bf16[1088,256]{1,0:T(8,128)(2,1)S(1)}, u32[]{:S(2)}, u32[]{:S(2)}) collective-permute-start(bf16[1088,256]{1,0:T(8,128)(2,1)} %collective-permute-done.11.refs_2_), channel_id=1, source_target_pairs={{8,0},{16,8},{24,16},{28,24},{20,28},{12,20},{4,12},{0,4},{9,1},{1... | collective-permute-start | bytes 1671176 | tf_op jit(solution)/shard_map/ppermute | solution.py:246
  132.8 22.3 %collective-permute-start.28 = (bf16[1088,256]{1,0:T(8,128)(2,1)}, bf16[1088,256]{1,0:T(8,128)(2,1)S(1)}, u32[]{:S(2)}, u32[]{:S(2)}) collective-permute-start(bf16[1088,256]{1,0:T(8,128)(2,1)} %collective-permute-done.26.refs_3_), channel_id=1, source_target_pairs={{0,8},{8,16},{16,24},{24,28},{28,20},{20,12},{12,4},{4,0},{1,9},{9... | collective-permute-start | bytes 1671176 | tf_op jit(solution)/shard_map/ppermute | solution.py:244
  134.4 22.2 %collective-permute-start.29 = (bf16[1088,256]{1,0:T(8,128)(2,1)}, bf16[1088,256]{1,0:T(8,128)(2,1)S(1)}, u32[]{:S(2)}, u32[]{:S(2)}) collective-permute-start(bf16[1088,256]{1,0:T(8,128)(2,1)} %collective-permute-done.27.refs_4_), channel_id=1, source_target_pairs={{8,0},{16,8},{24,16},{28,24},{20,28},{12,20},{4,12},{0,4},{9,1},{1... | collective-permute-start | bytes 1671176 | tf_op jit(solution)/shard_map/ppermute | solution.py:246
  144.6 22.4 %collective-permute-start.24 = (bf16[1088,256]{1,0:T(8,128)(2,1)S(1)}, bf16[1088,256]{1,0:T(8,128)(2,1)S(1)}, u32[]{:S(2)}, u32[]{:S(2)}) collective-permute-start(bf16[1088,256]{1,0:T(8,128)(2,1)S(1)} %collective-permute-done.21.refs_3_), channel_id=1, source_target_pairs={{0,8},{8,16},{16,24},{24,28},{28,20},{20,12},{12,4},{4,0},{1,9},{9... | collective-permute-start | bytes 1671176 | tf_op jit(solution)/shard_map/ppermute | solution.py:244
  146.2 22.3 %collective-permute-start.25 = (bf16[1088,256]{1,0:T(8,128)(2,1)S(1)}, bf16[1088,256]{1,0:T(8,128)(2,1)S(1)}, u32[]{:S(2)}, u32[]{:S(2)}) collective-permute-start(bf16[1088,256]{1,0:T(8,128)(2,1)S(1)} %collective-permute-done.22.refs_4_), channel_id=1, source_target_pairs={{8,0},{16,8},{24,16},{28,24},{20,28},{12,20},{4,12},{0,4},{9,1},{1... | collective-permute-start | bytes 1671176 | tf_op jit(solution)/shard_map/ppermute | solution.py:246
  156.6 16.4 %collective-permute-start.31 = (bf16[544,256]{1,0:T(8,128)(2,1)S(1)}, bf16[544,256]{1,0:T(8,128)(2,1)S(1)}, u32[]{:S(2)}, u32[]{:S(2)}) collective-permute-start(bf16[544,256]{1,0:T(8,128)(2,1)S(1)} %slice.12), channel_id=1, source_target_pairs={{0,8},{8,16},{16,24},{24,28},{28,20},{20,12},{12,4},{4,0},{1,9},{9... | collective-permute-start | bytes 835592 | tf_op jit(solution)/shard_map/ppermute | solution.py:244
  (57 other events, 951.0 us)

commit v5 on v4

--- a/solution.py
+++ b/solution.py
@@ -26,7 +26,7 @@
     outs = refs[: len(heads)]
     rows_held, weight, sems = refs[len(heads) :]
     tok_rows = tokens_ref.shape[0]
-    tiles = 4
+    tiles = 1
     tile = tok_rows // tiles
     columns = weight.shape[1]
     copies = []
@@ -86,7 +86,7 @@
         scratch_shapes=[
             pltpu.VMEM((tok_rows, width), jnp.bfloat16),
             pltpu.VMEM((width, 2 * HD * len(heads)), jnp.bfloat16),
-            pltpu.SemaphoreType.DMA((2 * len(heads) + 4,)),
+            pltpu.SemaphoreType.DMA((2 * len(heads) + 1,)),
         ],
         compiler_params=pltpu.CompilerParams(vmem_limit_bytes=60 * MIB),
         cost_estimate=pl.CostEstimate(
@@ -166,7 +166,7 @@
             pltpu.VMEM((devices * share, 2 * HD), jnp.bfloat16),
             pltpu.SemaphoreType.DMA((2 * devices + 1,)),
         ],
-        compiler_params=pltpu.CompilerParams(vmem_limit_bytes=48 * MIB),
+        compiler_params=pltpu.CompilerParams(vmem_limit_bytes=(60 if head < 2 else 24) * MIB),
         cost_estimate=pl.CostEstimate(
             flops=4 * tok_rows * 1152 * HD,
             bytes_accessed=devices * tok_rows * 4 * HD,
@@ -207,7 +207,7 @@
         out_shape=jax.ShapeDtypeStruct(
             (tok_rows, columns), jnp.bfloat16 if final else jnp.float32
         ),
-        compiler_params=pltpu.CompilerParams(vmem_limit_bytes=63 * MIB),
+        compiler_params=pltpu.CompilerParams(vmem_limit_bytes=24 * MIB),
         cost_estimate=pl.CostEstimate(
             flops=2 * tok_rows * len(pieces) * HD * columns,
             bytes_accessed=6 * MIB,

time: 202 us -> 198 us (0.980)
  local copies, waits for them, and re-layouts: 11.4 us -> 8.34 us
  Pallas kernels: 47.1 us -> 44.6 us
    ppermute x15, waiting for transfers between devices: 58.7 us -> 53.6 us  [step(): given.append(lax.ppermute(ahead, 'seq', self.forward))]
    ppermute x15, waiting for transfers between devices: 27.7 us -> 31.6 us  [step(): given.append(lax.ppermute(behind, 'seq', self.backward))]
    pallas_call x2, Pallas kernels: 8.34 us -> 4.76 us  [project_out(): pl.pallas_call(functools.partial(out_kernel, len(pieces), final), grid=(t...]
    unnamed x75 -> x39, local copies, waits for them, and re-layouts: 5.43 us -> 1.97 us
    ppermute x15, waiting for transfers between devices: 7.26 us -> 10.2 us  [to_head(): return lax.ppermute(value, 'head', [(g, g ^ flip) for g in range(groups)])]
    pallas_call x4, Pallas kernels: 19.3 us -> 21.3 us  [attend(): pl.pallas_call(functools.partial(attend_kernel, devices), grid=(1,), in_s...]
  transfers between devices with their start and end apart: 45 -> 45, of which waited for: 29 -> 28; matrix products, arithmetic and copies ran while one was open for 6% -> 7% of each run, Pallas kernels for 19% -> 19%
where the time goes in v5:
time: 198 us
  waiting for transfers between devices  95.4 us (48%)
  Pallas kernels  44.6 us (23%)
  starting transfers between devices  40.9 us (21%)
  local copies, waits for them, and re-layouts  8.34 us (4%)
  matrix products  5.48 us (3%)
  other arithmetic  2.83 us (1%)
    ppermute x15, waiting for transfers between devices, step(): given.append(lax.ppermute(ahead, 'seq', self.forward))  53.6 us
    ppermute x15, waiting for transfers between devices, step(): given.append(lax.ppermute(behind, 'seq', self.backward))  31.6 us
    ppermute x15, starting transfers between devices, step(): given.append(lax.ppermute(ahead, 'seq', self.forward))  26.1 us
    pallas_call x4, Pallas kernels, attend(): pl.pallas_call(functools.partial(attend_kernel, devices), grid=(1,), in_s...  21.3 us
    pallas_call x3, Pallas kernels, project_kv(): pl.pallas_call(functools.partial(kv_kernel, heads), grid=(1,), in_specs=[...  18.5 us
    ppermute x15, waiting for transfers between devices, to_head(): return lax.ppermute(value, 'head', [(g, g ^ flip) for g in range(groups)])  10.2 us
    ppermute x15, starting transfers between devices, to_head(): return lax.ppermute(value, 'head', [(g, g ^ flip) for g in range(groups)])  9 us
    ppermute x15, starting transfers between devices, step(): given.append(lax.ppermute(behind, 'seq', self.backward))  5.77 us
  transfers between devices with their start and end apart: 45, of which 28 were waited for; matrix products, arithmetic and copies ran while one was open for 7% of the time, Pallas kernels for 19%

profile of v5, /device:TPU:0, one launch (start us, length us, event | category | flops | bytes accessed | tf_op | source)
XLA Modules:
  0.0 197.8 jit_solution(15096104967454421514)
XLA Ops:
  1.5 5.7 %project_kv.3.refs_0_ = bf16[1088,256]{1,0:T(8,128)(2,1)} custom-call(bf16[1024,2048]{1,0:T(8,128)(2,1)} %tokens_ref.4, bf16[2048,512]{1,0:T(8,128)(2,1)} %wk_ref.5, bf16[2048,512]{1,0:T(8,128)(2,1)} %wv_ref.5, s32[1,64]{1,0:T(1,128)} %get-tuple-element.92.start_ref, s32[1,64]{1,0:T(1,128)} %get-tuple-element.91.end_ref), custom_call_target="tpu_custom_call" | custom-call | flops 1073741824 | bytes 6291456 | tf_op jit(solution)/shard_map/project_kv/pallas_call | solution.py:80
  7.1 3.1 %collective-permute-start = (bf16[1088,256]{1,0:T(8,128)(2,1)}, bf16[1088,256]{1,0:T(8,128)(2,1)}, u32[]{:S(2)}, u32[]{:S(2)}) collective-permute-start(bf16[1088,256]{1,0:T(8,128)(2,1)} %project_kv.3.refs_0_), channel_id=1, source_target_pairs={{0,8},{8,16},{16,24},{24,28},{28,20},{20,12},{12,4},{4,0},{1,9},{9... | collective-permute-start | bytes 1671176 | tf_op jit(solution)/shard_map/ppermute | solution.py:244
  10.2 5.6 %project_kv.5.refs_0_ = bf16[1088,256]{1,0:T(8,128)(2,1)} custom-call(bf16[1024,2048]{1,0:T(8,128)(2,1)} %tokens_ref.4, bf16[2048,512]{1,0:T(8,128)(2,1)} %wk_ref.5, bf16[2048,512]{1,0:T(8,128)(2,1)} %wv_ref.5, s32[1,64]{1,0:T(1,128)} %get-tuple-element.92.start_ref, s32[1,64]{1,0:T(1,128)} %get-tuple-element.91.end_ref), custom_call_target="tpu_custom_call" | custom-call | flops 1073741824 | bytes 6291456 | tf_op jit(solution)/shard_map/project_kv/pallas_call | solution.py:80
  17.9 6.0 %collective-permute-done.refs_1_ = bf16[1088,256]{1,0:T(8,128)(2,1)} collective-permute-done((bf16[1088,256]{1,0:T(8,128)(2,1)}, bf16[1088,256]{1,0:T(8,128)(2,1)}, u32[]{:S(2)}, u32[]{:S(2)}) %collective-permute-start) | collective-permute-done | bytes 557088 | tf_op jit(solution)/shard_map/ppermute | solution.py:244
  28.1 7.8 %collective-permute-done.12.refs_1_ = bf16[1088,256]{1,0:T(8,128)(2,1)} collective-permute-done((bf16[1088,256]{1,0:T(8,128)(2,1)}, bf16[1088,256]{1,0:T(8,128)(2,1)}, u32[]{:S(2)}, u32[]{:S(2)}) %collective-permute-start.12) | collective-permute-done | bytes 557088 | tf_op jit(solution)/shard_map/ppermute | solution.py:244
  44.3 3.5 %collective-permute-done.2.refs_3_ = bf16[1088,256]{1,0:T(8,128)(2,1)} collective-permute-done((bf16[1088,256]{1,0:T(8,128)(2,1)}, bf16[1088,256]{1,0:T(8,128)(2,1)}, u32[]{:S(2)}, u32[]{:S(2)}) %collective-permute-start.2) | collective-permute-done | bytes 557088 | tf_op jit(solution)/shard_map/ppermute | solution.py:244
  52.0 2.3 %constant_dynamic-slice_fusion.2 = (bf16[512,512]{1,0:T(8,128)(2,1)}, bf16[512,512]{1,0:T(8,128)(2,1)}) fusion(bf16[512,2048]{1,0:T(8,128)(2,1)} %param.17, s32[]{:T(128)S(6)} %select_n.35, s32[]{:T(128)S(6)} %select_n.34), kind=kLoop, calls=%fused_computation.10 | loop fusion | bytes 2097160 | tf_op jit(solution)/shard_map/dynamic_slice | solution.py:334
  54.2 5.5 %collective-permute-done.14.refs_3_ = bf16[1088,256]{1,0:T(8,128)(2,1)} collective-permute-done((bf16[1088,256]{1,0:T(8,128)(2,1)}, bf16[1088,256]{1,0:T(8,128)(2,1)}, u32[]{:S(2)}, u32[]{:S(2)}) %collective-permute-start.14) | collective-permute-done | bytes 557088 | tf_op jit(solution)/shard_map/ppermute | solution.py:244
  59.7 7.2 %project_kv.4 = (bf16[1088,256]{1,0:T(8,128)(2,1)}, bf16[1088,256]{1,0:T(8,128)(2,1)}) custom-call(bf16[1024,2048]{1,0:T(8,128)(2,1)} %tokens_ref.4, bf16[2048,512]{1,0:T(8,128)(2,1)} %wk_ref.5, bf16[2048,512]{1,0:T(8,128)(2,1)} %wv_ref.5, s32[1,64]{1,0:T(1,128)} %get-tuple-element.92.start_ref, s32[1,64]{1,0:T(1,128)} %get-tuple-element.91.end_ref), custom_call_target="tpu_custom_call" | custom-call | flops 2147483648 | bytes 6291456 | tf_op jit(solution)/shard_map/project_kv/pallas_call | solution.py:80
  67.0 2.2 %collective-permute-start.17 = (bf16[1088,256]{1,0:T(8,128)(2,1)}, bf16[1088,256]{1,0:T(8,128)(2,1)S(1)}, u32[]{:S(2)}, u32[]{:S(2)}) collective-permute-start(bf16[1088,256]{1,0:T(8,128)(2,1)} %collective-permute-done.14.refs_3_), channel_id=1, source_target_pairs={{0,8},{8,16},{16,24},{24,28},{28,20},{20,12},{12,4},{4,0},{1,9},{9... | collective-permute-start | bytes 1671176 | tf_op jit(solution)/shard_map/ppermute | solution.py:244
  74.4 5.5 %convolution_convert_fusion.q_ref = bf16[1024,512]{1,0:T(8,128)(2,1)} fusion(bf16[1024,2048]{1,0:T(8,128)(2,1)} %tokens_ref.4, bf16[2048,512]{1,0:T(8,128)(2,1)S(1)} %copy-done), kind=kOutput, calls=%fused_computation.1 | convolution fusion | flops 2148007936 | bytes 7340032 | tf_op jit(solution)/shard_map/dot_general | solution.py:329
  79.9 3.0 %collective-permute-done.17.refs_5_ = bf16[1088,256]{1,0:T(8,128)(2,1)S(1)} collective-permute-done((bf16[1088,256]{1,0:T(8,128)(2,1)}, bf16[1088,256]{1,0:T(8,128)(2,1)S(1)}, u32[]{:S(2)}, u32[]{:S(2)}) %collective-permute-start.17) | collective-permute-done | bytes 557088 | tf_op jit(solution)/shard_map/ppermute | solution.py:244
  87.0 7.9 %collective-permute-done.8.refs_1_ = bf16[1088,256]{1,0:T(8,128)(2,1)} collective-permute-done((bf16[1088,256]{1,0:T(8,128)(2,1)}, bf16[1088,256]{1,0:T(8,128)(2,1)}, u32[]{:S(2)}, u32[]{:S(2)}) %collective-permute-start.8) | collective-permute-done | bytes 557088 | tf_op jit(solution)/shard_map/ppermute | solution.py:244
  100.7 8.2 %collective-permute-done.20.refs_7_ = bf16[1088,256]{1,0:T(8,128)(2,1)} collective-permute-done((bf16[1088,256]{1,0:T(8,128)(2,1)}, bf16[1088,256]{1,0:T(8,128)(2,1)}, u32[]{:S(2)}, u32[]{:S(2)}) %collective-permute-start.20) | collective-permute-done | bytes 557088 | tf_op jit(solution)/shard_map/ppermute | solution.py:246
  112.8 6.2 %attend.4.refs_0_ = bf16[1024,128]{1,0:T(8,128)(2,1)} custom-call(s32[8,9]{1,0:T(8,128)} %pad_add_fusion.table_ref, s32[8]{0:T(128)} %gather_fusion, bf16[1024,512]{1,0:T(8,128)(2,1)} %convolution_convert_fusion.q_ref, bf16[1088,256]{1,0:T(8,128)(2,1)} %project_kv.3.refs_0_, bf16[1088,256]{1,0:T(8,128)(2,1)} %collective-permute-done.refs_1_, ...), custom_call_target="tpu_custom_call" | custom-call | flops 603979776 | bytes 4194304 | tf_op jit(solution)/shard_map/attend/pallas_call | solution.py:157
  124.3 6.2 %attend.5.refs_4_ = bf16[1024,128]{1,0:T(8,128)(2,1)} custom-call(s32[8,9]{1,0:T(8,128)} %pad_add_fusion.table_ref, s32[8]{0:T(128)} %gather_fusion, bf16[1024,512]{1,0:T(8,128)(2,1)} %convolution_convert_fusion.q_ref, bf16[1088,256]{1,0:T(8,128)(2,1)} %project_kv.5.refs_0_, bf16[1088,256]{1,0:T(8,128)(2,1)} %collective-permute-done.12.refs_1_, ...), custom_call_target="tpu_custom_call" | custom-call | flops 603979776 | bytes 4194304 | tf_op jit(solution)/shard_map/attend/pallas_call | solution.py:157
  134.8 7.7 %collective-permute-done.21.refs_3_ = bf16[1088,256]{1,0:T(8,128)(2,1)S(1)} collective-permute-done((bf16[1088,256]{1,0:T(8,128)(2,1)}, bf16[1088,256]{1,0:T(8,128)(2,1)S(1)}, u32[]{:S(2)}, u32[]{:S(2)}) %collective-permute-start.21) | collective-permute-done | bytes 557088 | tf_op jit(solution)/shard_map/ppermute | solution.py:244
  142.5 2.2 %collective-permute-done.22.refs_4_ = bf16[1088,256]{1,0:T(8,128)(2,1)} collective-permute-done((bf16[1088,256]{1,0:T(8,128)(2,1)}, bf16[1088,256]{1,0:T(8,128)(2,1)}, u32[]{:S(2)}, u32[]{:S(2)}) %collective-permute-start.22) | collective-permute-done | bytes 557088 | tf_op jit(solution)/shard_map/ppermute | solution.py:246
  148.2 5.1 %collective-permute-done.30.refs_5_ = bf16[1024,128]{1,0:T(8,128)(2,1)S(1)} collective-permute-done((bf16[1024,128]{1,0:T(8,128)(2,1)}, bf16[1024,128]{1,0:T(8,128)(2,1)S(1)}, u32[]{:S(2)}, u32[]{:S(2)}) %collective-permute-start.30) | collective-permute-done | bytes 262176 | tf_op jit(solution)/shard_map/ppermute | solution.py:288
  158.7 7.7 %collective-permute-done.24.refs_5_ = bf16[1088,256]{1,0:T(8,128)(2,1)S(1)} collective-permute-done((bf16[1088,256]{1,0:T(8,128)(2,1)S(1)}, bf16[1088,256]{1,0:T(8,128)(2,1)S(1)}, u32[]{:S(2)}, u32[]{:S(2)}) %collective-permute-start.24) | collective-permute-done | bytes 557088 | tf_op jit(solution)/shard_map/ppermute | solution.py:244
  174.5 4.6 %attend.6.refs_8_ = bf16[1024,128]{1,0:T(8,128)(2,1)S(1)} custom-call(s32[8,9]{1,0:T(8,128)S(1)} %copy-done.8, s32[8]{0:T(128)S(1)} %copy-done.9, bf16[1024,512]{1,0:T(8,128)(2,1)S(1)} %copy-done.1, bf16[1088,256]{1,0:T(8,128)(2,1)S(1)} %copy-done.7, bf16[1088,256]{1,0:T(8,128)(2,1)} %collective-permute-done.8.refs_1_, ...), custom_call_target="tpu_custom_call" | custom-call | flops 603979776 | bytes 4194304 | tf_op jit(solution)/shard_map/attend/pallas_call | solution.py:157
  181.2 4.4 %attend.7.refs_12_ = bf16[1024,128]{1,0:T(8,128)(2,1)S(1)} custom-call(s32[8,9]{1,0:T(8,128)S(1)} %copy-done.8, s32[8]{0:T(128)S(1)} %copy-done.9, bf16[1024,512]{1,0:T(8,128)(2,1)S(1)} %copy-done.1, bf16[1088,256]{1,0:T(8,128)(2,1)S(1)} %copy-done.6, bf16[1088,256]{1,0:T(8,128)(2,1)} %collective-permute-done.10.refs_1_, ...), custom_call_target="tpu_custom_call" | custom-call | flops 603979776 | bytes 4194304 | tf_op jit(solution)/shard_map/attend/pallas_call | solution.py:157
  188.0 3.4 %project_out.2.refs_4_ = f32[1024,512]{1,0:T(8,128)S(1)} custom-call(bf16[1024,128]{1,0:T(8,128)(2,1)S(1)} %copy-done.4, bf16[1024,128]{1,0:T(8,128)(2,1)S(1)} %collective-permute-done.23.refs_1_, bf16[1024,128]{1,0:T(8,128)(2,1)S(1)} %collective-permute-done.36.refs_2_, bf16[1024,128]{1,0:T(8,128)(2,1)S(1)} %collective-permute-done.37.refs_3_, ...), custom_call_target="tpu_custom_call" | custom-call | flops 1879048192 | bytes 6291456 | tf_op jit(solution)/shard_map/project_out/pallas_call | solution.py:200
  191.4 3.5 %collective-permute-done.35.refs_0_ = bf16[1024,128]{1,0:T(8,128)(2,1)S(1)} collective-permute-done((bf16[1024,128]{1,0:T(8,128)(2,1)S(1)}, bf16[1024,128]{1,0:T(8,128)(2,1)S(1)}, u32[]{:S(2)}, u32[]{:S(2)}) %collective-permute-start.35) | collective-permute-done | bytes 262176 | tf_op jit(solution)/shard_map/ppermute | solution.py:288
  (128 shorter events, 73.3 us)
Async XLA Ops:
  7.1 16.8 %collective-permute-start = (bf16[1088,256]{1,0:T(8,128)(2,1)}, bf16[1088,256]{1,0:T(8,128)(2,1)}, u32[]{:S(2)}, u32[]{:S(2)}) collective-permute-start(bf16[1088,256]{1,0:T(8,128)(2,1)} %project_kv.3.refs_0_), channel_id=1, source_target_pairs={{0,8},{8,16},{16,24},{24,28},{28,20},{20,12},{12,4},{4,0},{1,9},{9... | collective-permute-start | bytes 1671176 | tf_op jit(solution)/shard_map/ppermute | solution.py:244
  15.9 20.0 %collective-permute-start.12 = (bf16[1088,256]{1,0:T(8,128)(2,1)}, bf16[1088,256]{1,0:T(8,128)(2,1)}, u32[]{:S(2)}, u32[]{:S(2)}) collective-permute-start(bf16[1088,256]{1,0:T(8,128)(2,1)} %project_kv.5.refs_0_), channel_id=1, source_target_pairs={{0,8},{8,16},{16,24},{24,28},{28,20},{20,12},{12,4},{4,0},{1,9},{9... | collective-permute-start | bytes 1671176 | tf_op jit(solution)/shard_map/ppermute | solution.py:244
  17.9 20.0 %collective-permute-start.13 = (bf16[1088,256]{1,0:T(8,128)(2,1)}, bf16[1088,256]{1,0:T(8,128)(2,1)S(1)}, u32[]{:S(2)}, u32[]{:S(2)}) collective-permute-start(bf16[1088,256]{1,0:T(8,128)(2,1)} %project_kv.5.refs_0_), channel_id=1, source_target_pairs={{8,0},{16,8},{24,16},{28,24},{20,28},{12,20},{4,12},{0,4},{9,1},{1... | collective-permute-start | bytes 1671176 | tf_op jit(solution)/shard_map/ppermute | solution.py:246
  26.1 21.7 %collective-permute-start.2 = (bf16[1088,256]{1,0:T(8,128)(2,1)}, bf16[1088,256]{1,0:T(8,128)(2,1)}, u32[]{:S(2)}, u32[]{:S(2)}) collective-permute-start(bf16[1088,256]{1,0:T(8,128)(2,1)} %collective-permute-done.refs_1_), channel_id=1, source_target_pairs={{0,8},{8,16},{16,24},{24,28},{28,20},{20,12},{12,4},{4,0},{1,9},{9... | collective-permute-start | bytes 1671176 | tf_op jit(solution)/shard_map/ppermute | solution.py:244
  27.6 22.3 %collective-permute-start.3 = (bf16[1088,256]{1,0:T(8,128)(2,1)}, bf16[1088,256]{1,0:T(8,128)(2,1)}, u32[]{:S(2)}, u32[]{:S(2)}) collective-permute-start(bf16[1088,256]{1,0:T(8,128)(2,1)} %collective-permute-done.1.refs_2_), channel_id=1, source_target_pairs={{8,0},{16,8},{24,16},{28,24},{20,28},{12,20},{4,12},{0,4},{9,1},{1... | collective-permute-start | bytes 1671176 | tf_op jit(solution)/shard_map/ppermute | solution.py:246
  38.7 21.0 %collective-permute-start.14 = (bf16[1088,256]{1,0:T(8,128)(2,1)}, bf16[1088,256]{1,0:T(8,128)(2,1)}, u32[]{:S(2)}, u32[]{:S(2)}) collective-permute-start(bf16[1088,256]{1,0:T(8,128)(2,1)} %collective-permute-done.12.refs_1_), channel_id=1, source_target_pairs={{0,8},{8,16},{16,24},{24,28},{28,20},{20,12},{12,4},{4,0},{1,9},{9... | collective-permute-start | bytes 1671176 | tf_op jit(solution)/shard_map/ppermute | solution.py:244
  43.8 23.1 %collective-permute-start.15 = (bf16[1088,256]{1,0:T(8,128)(2,1)}, bf16[1088,256]{1,0:T(8,128)(2,1)}, u32[]{:S(2)}, u32[]{:S(2)}) collective-permute-start(bf16[1088,256]{1,0:T(8,128)(2,1)} %copy-done.11), channel_id=1, source_target_pairs={{8,0},{16,8},{24,16},{28,24},{20,28},{12,20},{4,12},{0,4},{9,1},{1... | collective-permute-start | bytes 1671176 | tf_op jit(solution)/shard_map/ppermute | solution.py:246
  49.9 20.9 %collective-permute-start.4 = (bf16[1088,256]{1,0:T(8,128)(2,1)}, bf16[1088,256]{1,0:T(8,128)(2,1)}, u32[]{:S(2)}, u32[]{:S(2)}) collective-permute-start(bf16[1088,256]{1,0:T(8,128)(2,1)} %collective-permute-done.2.refs_3_), channel_id=1, source_target_pairs={{0,8},{8,16},{16,24},{24,28},{28,20},{20,12},{12,4},{4,0},{1,9},{9... | collective-permute-start | bytes 1671176 | tf_op jit(solution)/shard_map/ppermute | solution.py:244
  51.5 20.8 %collective-permute-start.5 = (bf16[1088,256]{1,0:T(8,128)(2,1)}, bf16[1088,256]{1,0:T(8,128)(2,1)}, u32[]{:S(2)}, u32[]{:S(2)}) collective-permute-start(bf16[1088,256]{1,0:T(8,128)(2,1)} %collective-permute-done.3.refs_4_), channel_id=1, source_target_pairs={{8,0},{16,8},{24,16},{28,24},{20,28},{12,20},{4,12},{0,4},{9,1},{1... | collective-permute-start | bytes 1671176 | tf_op jit(solution)/shard_map/ppermute | solution.py:246
  72.3 22.5 %collective-permute-start.8 = (bf16[1088,256]{1,0:T(8,128)(2,1)}, bf16[1088,256]{1,0:T(8,128)(2,1)}, u32[]{:S(2)}, u32[]{:S(2)}) collective-permute-start(bf16[1088,256]{1,0:T(8,128)(2,1)} %get-tuple-element.57.refs_0_), channel_id=1, source_target_pairs={{0,8},{8,16},{16,24},{24,28},{28,20},{20,12},{12,4},{4,0},{1,9},{9... | collective-permute-start | bytes 1671176 | tf_op jit(solution)/shard_map/ppermute | solution.py:244
  73.9 23.0 %collective-permute-start.9 = (bf16[1088,256]{1,0:T(8,128)(2,1)}, bf16[1088,256]{1,0:T(8,128)(2,1)}, u32[]{:S(2)}, u32[]{:S(2)}) collective-permute-start(bf16[1088,256]{1,0:T(8,128)(2,1)} %get-tuple-element.57.refs_0_), channel_id=1, source_target_pairs={{8,0},{16,8},{24,16},{28,24},{20,28},{12,20},{4,12},{0,4},{9,1},{1... | collective-permute-start | bytes 1671176 | tf_op jit(solution)/shard_map/ppermute | solution.py:246
  85.0 23.9 %collective-permute-start.20 = (bf16[1088,256]{1,0:T(8,128)(2,1)}, bf16[1088,256]{1,0:T(8,128)(2,1)}, u32[]{:S(2)}, u32[]{:S(2)}) collective-permute-start(bf16[1088,256]{1,0:T(8,128)(2,1)} %collective-permute-done.18.refs_6_), channel_id=1, source_target_pairs={{8,0},{16,8},{24,16},{28,24},{20,28},{12,20},{4,12},{0,4},{9,1},{1... | collective-permute-start | bytes 1671176 | tf_op jit(solution)/shard_map/ppermute | solution.py:246
  85.6 23.3 %collective-permute-start.19 = (bf16[1088,256]{1,0:T(8,128)(2,1)}, bf16[1088,256]{1,0:T(8,128)(2,1)}, u32[]{:S(2)}, u32[]{:S(2)}) collective-permute-start(bf16[1088,256]{1,0:T(8,128)(2,1)} %collective-permute-done.4.refs_5_), channel_id=1, source_target_pairs={{0,8},{8,16},{16,24},{24,28},{28,20},{20,12},{12,4},{4,0},{1,9},{9... | collective-permute-start | bytes 1671176 | tf_op jit(solution)/shard_map/ppermute | solution.py:244
  96.9 22.1 %collective-permute-start.10 = (bf16[1088,256]{1,0:T(8,128)(2,1)}, bf16[1088,256]{1,0:T(8,128)(2,1)}, u32[]{:S(2)}, u32[]{:S(2)}) collective-permute-start(bf16[1088,256]{1,0:T(8,128)(2,1)} %get-tuple-element.59.refs_0_), channel_id=1, source_target_pairs={{0,8},{8,16},{16,24},{24,28},{28,20},{20,12},{12,4},{4,0},{1,9},{9... | collective-permute-start | bytes 1671176 | tf_op jit(solution)/shard_map/ppermute | solution.py:244
  98.5 22.3 %collective-permute-start.11 = (bf16[1088,256]{1,0:T(8,128)(2,1)}, bf16[1088,256]{1,0:T(8,128)(2,1)}, u32[]{:S(2)}, u32[]{:S(2)}) collective-permute-start(bf16[1088,256]{1,0:T(8,128)(2,1)} %get-tuple-element.59.refs_0_), channel_id=1, source_target_pairs={{8,0},{16,8},{24,16},{28,24},{20,28},{12,20},{4,12},{0,4},{9,1},{1... | collective-permute-start | bytes 1671176 | tf_op jit(solution)/shard_map/ppermute | solution.py:246
  108.9 21.8 %collective-permute-start.26 = (bf16[1088,256]{1,0:T(8,128)(2,1)}, bf16[1088,256]{1,0:T(8,128)(2,1)}, u32[]{:S(2)}, u32[]{:S(2)}) collective-permute-start(bf16[1088,256]{1,0:T(8,128)(2,1)} %collective-permute-done.8.refs_1_), channel_id=1, source_target_pairs={{0,8},{8,16},{16,24},{24,28},{28,20},{20,12},{12,4},{4,0},{1,9},{9... | collective-permute-start | bytes 1671176 | tf_op jit(solution)/shard_map/ppermute | solution.py:244
  110.5 22.3 %collective-permute-start.27 = (bf16[1088,256]{1,0:T(8,128)(2,1)}, bf16[1088,256]{1,0:T(8,128)(2,1)}, u32[]{:S(2)}, u32[]{:S(2)}) collective-permute-start(bf16[1088,256]{1,0:T(8,128)(2,1)} %collective-permute-done.9.refs_2_), channel_id=1, source_target_pairs={{8,0},{16,8},{24,16},{28,24},{20,28},{12,20},{4,12},{0,4},{9,1},{1... | collective-permute-start | bytes 1671176 | tf_op jit(solution)/shard_map/ppermute | solution.py:246
  120.8 21.7 %collective-permute-start.21 = (bf16[1088,256]{1,0:T(8,128)(2,1)}, bf16[1088,256]{1,0:T(8,128)(2,1)S(1)}, u32[]{:S(2)}, u32[]{:S(2)}) collective-permute-start(bf16[1088,256]{1,0:T(8,128)(2,1)} %collective-permute-done.10.refs_1_), channel_id=1, source_target_pairs={{0,8},{8,16},{16,24},{24,28},{28,20},{20,12},{12,4},{4,0},{1,9},{9... | collective-permute-start | bytes 1671176 | tf_op jit(solution)/shard_map/ppermute | solution.py:244
  122.4 22.3 %collective-permute-start.22 = (bf16[1088,256]{1,0:T(8,128)(2,1)}, bf16[1088,256]{1,0:T(8,128)(2,1)}, u32[]{:S(2)}, u32[]{:S(2)}) collective-permute-start(bf16[1088,256]{1,0:T(8,128)(2,1)} %collective-permute-done.11.refs_2_), channel_id=1, source_target_pairs={{8,0},{16,8},{24,16},{28,24},{20,28},{12,20},{4,12},{0,4},{9,1},{1... | collective-permute-start | bytes 1671176 | tf_op jit(solution)/shard_map/ppermute | solution.py:246
  132.8 21.7 %collective-permute-start.28 = (bf16[1088,256]{1,0:T(8,128)(2,1)}, bf16[1088,256]{1,0:T(8,128)(2,1)S(1)}, u32[]{:S(2)}, u32[]{:S(2)}) collective-permute-start(bf16[1088,256]{1,0:T(8,128)(2,1)} %collective-permute-done.26.refs_3_), channel_id=1, source_target_pairs={{0,8},{8,16},{16,24},{24,28},{28,20},{20,12},{12,4},{4,0},{1,9},{9... | collective-permute-start | bytes 1671176 | tf_op jit(solution)/shard_map/ppermute | solution.py:244
  134.3 22.2 %collective-permute-start.29 = (bf16[1088,256]{1,0:T(8,128)(2,1)}, bf16[1088,256]{1,0:T(8,128)(2,1)S(1)}, u32[]{:S(2)}, u32[]{:S(2)}) collective-permute-start(bf16[1088,256]{1,0:T(8,128)(2,1)} %collective-permute-done.27.refs_4_), channel_id=1, source_target_pairs={{8,0},{16,8},{24,16},{28,24},{20,28},{12,20},{4,12},{0,4},{9,1},{1... | collective-permute-start | bytes 1671176 | tf_op jit(solution)/shard_map/ppermute | solution.py:246
  144.7 21.7 %collective-permute-start.24 = (bf16[1088,256]{1,0:T(8,128)(2,1)S(1)}, bf16[1088,256]{1,0:T(8,128)(2,1)S(1)}, u32[]{:S(2)}, u32[]{:S(2)}) collective-permute-start(bf16[1088,256]{1,0:T(8,128)(2,1)S(1)} %collective-permute-done.21.refs_3_), channel_id=1, source_target_pairs={{0,8},{8,16},{16,24},{24,28},{28,20},{20,12},{12,4},{4,0},{1,9},{9... | collective-permute-start | bytes 1671176 | tf_op jit(solution)/shard_map/ppermute | solution.py:244
  146.3 22.2 %collective-permute-start.25 = (bf16[1088,256]{1,0:T(8,128)(2,1)}, bf16[1088,256]{1,0:T(8,128)(2,1)S(1)}, u32[]{:S(2)}, u32[]{:S(2)}) collective-permute-start(bf16[1088,256]{1,0:T(8,128)(2,1)} %collective-permute-done.22.refs_4_), channel_id=1, source_target_pairs={{8,0},{16,8},{24,16},{28,24},{20,28},{12,20},{4,12},{0,4},{9,1},{1... | collective-permute-start | bytes 1671176 | tf_op jit(solution)/shard_map/ppermute | solution.py:246
  158.2 16.2 %collective-permute-start.32 = (bf16[544,256]{1,0:T(8,128)(2,1)S(1)}, bf16[544,256]{1,0:T(8,128)(2,1)S(1)}, u32[]{:S(2)}, u32[]{:S(2)}) collective-permute-start(bf16[544,256]{1,0:T(8,128)(2,1)S(1)} %slice.13), channel_id=1, source_target_pairs={{8,0},{16,8},{24,16},{28,24},{20,28},{12,20},{4,12},{0,4},{9,1},{1... | collective-permute-start | bytes 835592 | tf_op jit(solution)/shard_map/ppermute | solution.py:246
  (39 other events, 736.2 us)

commit v6 on v5

--- a/solution.py
+++ b/solution.py
@@ -51,9 +51,8 @@
     share = start_ref.shape[1]
     start = start_ref[...]
     end = end_ref[...]
-    ones = jnp.ones((tile, HD), jnp.bfloat16)
     sums = jnp.zeros((share, columns), jnp.float32)
-    counts = jnp.zeros((share, HD), jnp.float32)
+    counts = jnp.broadcast_to((end - start).astype(jnp.float32), (HD, share)).T
     for at in range(tiles):
         copies[2 * len(heads) + at].wait()
         rows = slice(at * tile, (at + 1) * tile)
@@ -66,7 +65,6 @@
         member = member.astype(jnp.float32).astype(jnp.bfloat16)
         over_rows = (((0,), (0,)), ((), ()))
         sums += lax.dot_general(member, kv, over_rows, preferred_element_type=jnp.float32)
-        counts += lax.dot_general(member, ones, over_rows, preferred_element_type=jnp.float32)
     means = (sums / counts[:, :1]).astype(jnp.bfloat16)
     for to, out in enumerate(outs):
         out[tok_rows:, :] = means[:, 2 * to * HD : 2 * (to + 1) * HD]
@@ -191,7 +189,7 @@
     tok_rows = pieces[0].shape[0]
     columns = weights[0].shape[1]
     final = total is not None
-    tile = tok_rows // 2 if final else 512
+    tile = tok_rows if final else tok_rows
     row_spec = pl.BlockSpec((tile, columns), lambda i: (i, 0))
 
     def weight_spec(head):

time: 198 us -> 198 us (level)
  transfers between devices with their start and end apart: 45 -> 45, of which waited for: 28 -> 29; matrix products, arithmetic and copies ran while one was open for 7% -> 7% of each run, Pallas kernels for 19% -> 19%
where the time goes in v6:
time: 198 us
  waiting for transfers between devices  95.8 us (48%)
  Pallas kernels  43.9 us (22%)
  starting transfers between devices  41 us (21%)
  local copies, waits for them, and re-layouts  8.34 us (4%)
  matrix products  5.48 us (3%)
  other arithmetic  2.83 us (1%)
    ppermute x15, waiting for transfers between devices, step(): given.append(lax.ppermute(ahead, 'seq', self.forward))  53.6 us
    ppermute x15, waiting for transfers between devices, step(): given.append(lax.ppermute(behind, 'seq', self.backward))  31.6 us
    ppermute x15, starting transfers between devices, step(): given.append(lax.ppermute(ahead, 'seq', self.forward))  26 us
    pallas_call x4, Pallas kernels, attend(): pl.pallas_call(functools.partial(attend_kernel, devices), grid=(1,), in_s...  21.3 us
    pallas_call x3, Pallas kernels, project_kv(): pl.pallas_call(functools.partial(kv_kernel, heads), grid=(1,), in_specs=[...  18 us
    ppermute x15, waiting for transfers between devices, to_head(): return lax.ppermute(value, 'head', [(g, g ^ flip) for g in range(groups)])  10.6 us
    ppermute x15, starting transfers between devices, to_head(): return lax.ppermute(value, 'head', [(g, g ^ flip) for g in range(groups)])  9.08 us
    ppermute x15, starting transfers between devices, step(): given.append(lax.ppermute(behind, 'seq', self.backward))  5.84 us
  transfers between devices with their start and end apart: 45, of which 29 were waited for; matrix products, arithmetic and copies ran while one was open for 7% of the time, Pallas kernels for 19%

profile of v6, /device:TPU:0, one launch (start us, length us, event | category | flops | bytes accessed | tf_op | source)
XLA Modules:
  0.0 197.7 jit_solution(6556898189883449996)
XLA Ops:
  1.5 5.5 %project_kv.3.refs_0_ = bf16[1088,256]{1,0:T(8,128)(2,1)} custom-call(bf16[1024,2048]{1,0:T(8,128)(2,1)} %tokens_ref.4, bf16[2048,512]{1,0:T(8,128)(2,1)} %wk_ref.5, bf16[2048,512]{1,0:T(8,128)(2,1)} %wv_ref.5, s32[1,64]{1,0:T(1,128)} %get-tuple-element.92.start_ref, s32[1,64]{1,0:T(1,128)} %get-tuple-element.91.end_ref), custom_call_target="tpu_custom_call" | custom-call | flops 1073741824 | bytes 6291456 | tf_op jit(solution)/shard_map/project_kv/pallas_call | solution.py:78
  6.9 3.1 %collective-permute-start = (bf16[1088,256]{1,0:T(8,128)(2,1)}, bf16[1088,256]{1,0:T(8,128)(2,1)}, u32[]{:S(2)}, u32[]{:S(2)}) collective-permute-start(bf16[1088,256]{1,0:T(8,128)(2,1)} %project_kv.3.refs_0_), channel_id=1, source_target_pairs={{0,8},{8,16},{16,24},{24,28},{28,20},{20,12},{12,4},{4,0},{1,9},{9... | collective-permute-start | bytes 1671176 | tf_op jit(solution)/shard_map/ppermute | solution.py:242
  10.0 5.5 %project_kv.5.refs_0_ = bf16[1088,256]{1,0:T(8,128)(2,1)} custom-call(bf16[1024,2048]{1,0:T(8,128)(2,1)} %tokens_ref.4, bf16[2048,512]{1,0:T(8,128)(2,1)} %wk_ref.5, bf16[2048,512]{1,0:T(8,128)(2,1)} %wv_ref.5, s32[1,64]{1,0:T(1,128)} %get-tuple-element.92.start_ref, s32[1,64]{1,0:T(1,128)} %get-tuple-element.91.end_ref), custom_call_target="tpu_custom_call" | custom-call | flops 1073741824 | bytes 6291456 | tf_op jit(solution)/shard_map/project_kv/pallas_call | solution.py:78
  17.6 6.1 %collective-permute-done.refs_1_ = bf16[1088,256]{1,0:T(8,128)(2,1)} collective-permute-done((bf16[1088,256]{1,0:T(8,128)(2,1)}, bf16[1088,256]{1,0:T(8,128)(2,1)}, u32[]{:S(2)}, u32[]{:S(2)}) %collective-permute-start) | collective-permute-done | bytes 557088 | tf_op jit(solution)/shard_map/ppermute | solution.py:242
  27.9 7.8 %collective-permute-done.12.refs_1_ = bf16[1088,256]{1,0:T(8,128)(2,1)} collective-permute-done((bf16[1088,256]{1,0:T(8,128)(2,1)}, bf16[1088,256]{1,0:T(8,128)(2,1)}, u32[]{:S(2)}, u32[]{:S(2)}) %collective-permute-start.12) | collective-permute-done | bytes 557088 | tf_op jit(solution)/shard_map/ppermute | solution.py:242
  44.1 3.5 %collective-permute-done.2.refs_3_ = bf16[1088,256]{1,0:T(8,128)(2,1)} collective-permute-done((bf16[1088,256]{1,0:T(8,128)(2,1)}, bf16[1088,256]{1,0:T(8,128)(2,1)}, u32[]{:S(2)}, u32[]{:S(2)}) %collective-permute-start.2) | collective-permute-done | bytes 557088 | tf_op jit(solution)/shard_map/ppermute | solution.py:242
  47.6 2.2 %collective-permute-done.3.refs_4_ = bf16[1088,256]{1,0:T(8,128)(2,1)} collective-permute-done((bf16[1088,256]{1,0:T(8,128)(2,1)}, bf16[1088,256]{1,0:T(8,128)(2,1)}, u32[]{:S(2)}, u32[]{:S(2)}) %collective-permute-start.3) | collective-permute-done | bytes 557088 | tf_op jit(solution)/shard_map/ppermute | solution.py:244
  51.8 2.3 %constant_dynamic-slice_fusion.2 = (bf16[512,512]{1,0:T(8,128)(2,1)}, bf16[512,512]{1,0:T(8,128)(2,1)}) fusion(bf16[512,2048]{1,0:T(8,128)(2,1)} %param.17, s32[]{:T(128)S(6)} %select_n.35, s32[]{:T(128)S(6)} %select_n.34), kind=kLoop, calls=%fused_computation.10 | loop fusion | bytes 2097160 | tf_op jit(solution)/shard_map/dynamic_slice | solution.py:332
  54.1 5.5 %collective-permute-done.14.refs_3_ = bf16[1088,256]{1,0:T(8,128)(2,1)} collective-permute-done((bf16[1088,256]{1,0:T(8,128)(2,1)}, bf16[1088,256]{1,0:T(8,128)(2,1)}, u32[]{:S(2)}, u32[]{:S(2)}) %collective-permute-start.14) | collective-permute-done | bytes 557088 | tf_op jit(solution)/shard_map/ppermute | solution.py:242
  59.6 7.1 %project_kv.4 = (bf16[1088,256]{1,0:T(8,128)(2,1)}, bf16[1088,256]{1,0:T(8,128)(2,1)}) custom-call(bf16[1024,2048]{1,0:T(8,128)(2,1)} %tokens_ref.4, bf16[2048,512]{1,0:T(8,128)(2,1)} %wk_ref.5, bf16[2048,512]{1,0:T(8,128)(2,1)} %wv_ref.5, s32[1,64]{1,0:T(1,128)} %get-tuple-element.92.start_ref, s32[1,64]{1,0:T(1,128)} %get-tuple-element.91.end_ref), custom_call_target="tpu_custom_call" | custom-call | flops 2147483648 | bytes 6291456 | tf_op jit(solution)/shard_map/project_kv/pallas_call | solution.py:78
  66.7 2.2 %collective-permute-start.17 = (bf16[1088,256]{1,0:T(8,128)(2,1)}, bf16[1088,256]{1,0:T(8,128)(2,1)S(1)}, u32[]{:S(2)}, u32[]{:S(2)}) collective-permute-start(bf16[1088,256]{1,0:T(8,128)(2,1)} %collective-permute-done.14.refs_3_), channel_id=1, source_target_pairs={{0,8},{8,16},{16,24},{24,28},{28,20},{20,12},{12,4},{4,0},{1,9},{9... | collective-permute-start | bytes 1671176 | tf_op jit(solution)/shard_map/ppermute | solution.py:242
  74.3 5.5 %convolution_convert_fusion.q_ref = bf16[1024,512]{1,0:T(8,128)(2,1)} fusion(bf16[1024,2048]{1,0:T(8,128)(2,1)} %tokens_ref.4, bf16[2048,512]{1,0:T(8,128)(2,1)S(1)} %copy-done), kind=kOutput, calls=%fused_computation.1 | convolution fusion | flops 2148007936 | bytes 7340032 | tf_op jit(solution)/shard_map/dot_general | solution.py:327
  79.7 2.8 %collective-permute-done.17.refs_5_ = bf16[1088,256]{1,0:T(8,128)(2,1)S(1)} collective-permute-done((bf16[1088,256]{1,0:T(8,128)(2,1)}, bf16[1088,256]{1,0:T(8,128)(2,1)S(1)}, u32[]{:S(2)}, u32[]{:S(2)}) %collective-permute-start.17) | collective-permute-done | bytes 557088 | tf_op jit(solution)/shard_map/ppermute | solution.py:242
  86.7 7.9 %collective-permute-done.8.refs_1_ = bf16[1088,256]{1,0:T(8,128)(2,1)} collective-permute-done((bf16[1088,256]{1,0:T(8,128)(2,1)}, bf16[1088,256]{1,0:T(8,128)(2,1)}, u32[]{:S(2)}, u32[]{:S(2)}) %collective-permute-start.8) | collective-permute-done | bytes 557088 | tf_op jit(solution)/shard_map/ppermute | solution.py:242
  100.4 8.2 %collective-permute-done.20.refs_7_ = bf16[1088,256]{1,0:T(8,128)(2,1)} collective-permute-done((bf16[1088,256]{1,0:T(8,128)(2,1)}, bf16[1088,256]{1,0:T(8,128)(2,1)}, u32[]{:S(2)}, u32[]{:S(2)}) %collective-permute-start.20) | collective-permute-done | bytes 557088 | tf_op jit(solution)/shard_map/ppermute | solution.py:244
  112.5 6.2 %attend.4.refs_0_ = bf16[1024,128]{1,0:T(8,128)(2,1)} custom-call(s32[8,9]{1,0:T(8,128)} %pad_add_fusion.table_ref, s32[8]{0:T(128)} %gather_fusion, bf16[1024,512]{1,0:T(8,128)(2,1)} %convolution_convert_fusion.q_ref, bf16[1088,256]{1,0:T(8,128)(2,1)} %project_kv.3.refs_0_, bf16[1088,256]{1,0:T(8,128)(2,1)} %collective-permute-done.refs_1_, ...), custom_call_target="tpu_custom_call" | custom-call | flops 603979776 | bytes 4194304 | tf_op jit(solution)/shard_map/attend/pallas_call | solution.py:155
  124.0 6.2 %attend.5.refs_4_ = bf16[1024,128]{1,0:T(8,128)(2,1)} custom-call(s32[8,9]{1,0:T(8,128)} %pad_add_fusion.table_ref, s32[8]{0:T(128)} %gather_fusion, bf16[1024,512]{1,0:T(8,128)(2,1)} %convolution_convert_fusion.q_ref, bf16[1088,256]{1,0:T(8,128)(2,1)} %project_kv.5.refs_0_, bf16[1088,256]{1,0:T(8,128)(2,1)} %collective-permute-done.12.refs_1_, ...), custom_call_target="tpu_custom_call" | custom-call | flops 603979776 | bytes 4194304 | tf_op jit(solution)/shard_map/attend/pallas_call | solution.py:155
  134.5 7.8 %collective-permute-done.21.refs_3_ = bf16[1088,256]{1,0:T(8,128)(2,1)S(1)} collective-permute-done((bf16[1088,256]{1,0:T(8,128)(2,1)}, bf16[1088,256]{1,0:T(8,128)(2,1)S(1)}, u32[]{:S(2)}, u32[]{:S(2)}) %collective-permute-start.21) | collective-permute-done | bytes 557088 | tf_op jit(solution)/shard_map/ppermute | solution.py:242
  147.9 5.3 %collective-permute-done.30.refs_5_ = bf16[1024,128]{1,0:T(8,128)(2,1)S(1)} collective-permute-done((bf16[1024,128]{1,0:T(8,128)(2,1)}, bf16[1024,128]{1,0:T(8,128)(2,1)S(1)}, u32[]{:S(2)}, u32[]{:S(2)}) %collective-permute-start.30) | collective-permute-done | bytes 262176 | tf_op jit(solution)/shard_map/ppermute | solution.py:286
  158.4 7.7 %collective-permute-done.24.refs_5_ = bf16[1088,256]{1,0:T(8,128)(2,1)S(1)} collective-permute-done((bf16[1088,256]{1,0:T(8,128)(2,1)S(1)}, bf16[1088,256]{1,0:T(8,128)(2,1)S(1)}, u32[]{:S(2)}, u32[]{:S(2)}) %collective-permute-start.24) | collective-permute-done | bytes 557088 | tf_op jit(solution)/shard_map/ppermute | solution.py:242
  174.2 4.6 %attend.6.refs_8_ = bf16[1024,128]{1,0:T(8,128)(2,1)S(1)} custom-call(s32[8,9]{1,0:T(8,128)S(1)} %copy-done.8, s32[8]{0:T(128)S(1)} %copy-done.9, bf16[1024,512]{1,0:T(8,128)(2,1)S(1)} %copy-done.1, bf16[1088,256]{1,0:T(8,128)(2,1)S(1)} %copy-done.7, bf16[1088,256]{1,0:T(8,128)(2,1)} %collective-permute-done.8.refs_1_, ...), custom_call_target="tpu_custom_call" | custom-call | flops 603979776 | bytes 4194304 | tf_op jit(solution)/shard_map/attend/pallas_call | solution.py:155
  180.9 4.4 %attend.7.refs_12_ = bf16[1024,128]{1,0:T(8,128)(2,1)S(1)} custom-call(s32[8,9]{1,0:T(8,128)S(1)} %copy-done.8, s32[8]{0:T(128)S(1)} %copy-done.9, bf16[1024,512]{1,0:T(8,128)(2,1)S(1)} %copy-done.1, bf16[1088,256]{1,0:T(8,128)(2,1)S(1)} %copy-done.6, bf16[1088,256]{1,0:T(8,128)(2,1)} %collective-permute-done.10.refs_1_, ...), custom_call_target="tpu_custom_call" | custom-call | flops 603979776 | bytes 4194304 | tf_op jit(solution)/shard_map/attend/pallas_call | solution.py:155
  188.0 3.2 %project_out.2.refs_4_ = f32[1024,512]{1,0:T(8,128)S(1)} custom-call(bf16[1024,128]{1,0:T(8,128)(2,1)S(1)} %copy-done.4, bf16[1024,128]{1,0:T(8,128)(2,1)S(1)} %collective-permute-done.23.refs_1_, bf16[1024,128]{1,0:T(8,128)(2,1)S(1)} %collective-permute-done.36.refs_2_, bf16[1024,128]{1,0:T(8,128)(2,1)S(1)} %collective-permute-done.37.refs_3_, ...), custom_call_target="tpu_custom_call" | custom-call | flops 1879048192 | bytes 6291456 | tf_op jit(solution)/shard_map/project_out/pallas_call | solution.py:198
  191.2 3.6 %collective-permute-done.35.refs_0_ = bf16[1024,128]{1,0:T(8,128)(2,1)S(1)} collective-permute-done((bf16[1024,128]{1,0:T(8,128)(2,1)S(1)}, bf16[1024,128]{1,0:T(8,128)(2,1)S(1)}, u32[]{:S(2)}, u32[]{:S(2)}) %collective-permute-start.35) | collective-permute-done | bytes 262176 | tf_op jit(solution)/shard_map/ppermute | solution.py:286
  (128 shorter events, 73.5 us)
Async XLA Ops:
  6.9 16.8 %collective-permute-start = (bf16[1088,256]{1,0:T(8,128)(2,1)}, bf16[1088,256]{1,0:T(8,128)(2,1)}, u32[]{:S(2)}, u32[]{:S(2)}) collective-permute-start(bf16[1088,256]{1,0:T(8,128)(2,1)} %project_kv.3.refs_0_), channel_id=1, source_target_pairs={{0,8},{8,16},{16,24},{24,28},{28,20},{20,12},{12,4},{4,0},{1,9},{9... | collective-permute-start | bytes 1671176 | tf_op jit(solution)/shard_map/ppermute | solution.py:242
  15.5 20.2 %collective-permute-start.12 = (bf16[1088,256]{1,0:T(8,128)(2,1)}, bf16[1088,256]{1,0:T(8,128)(2,1)}, u32[]{:S(2)}, u32[]{:S(2)}) collective-permute-start(bf16[1088,256]{1,0:T(8,128)(2,1)} %project_kv.5.refs_0_), channel_id=1, source_target_pairs={{0,8},{8,16},{16,24},{24,28},{28,20},{20,12},{12,4},{4,0},{1,9},{9... | collective-permute-start | bytes 1671176 | tf_op jit(solution)/shard_map/ppermute | solution.py:242
  17.6 20.1 %collective-permute-start.13 = (bf16[1088,256]{1,0:T(8,128)(2,1)}, bf16[1088,256]{1,0:T(8,128)(2,1)S(1)}, u32[]{:S(2)}, u32[]{:S(2)}) collective-permute-start(bf16[1088,256]{1,0:T(8,128)(2,1)} %project_kv.5.refs_0_), channel_id=1, source_target_pairs={{8,0},{16,8},{24,16},{28,24},{20,28},{12,20},{4,12},{0,4},{9,1},{1... | collective-permute-start | bytes 1671176 | tf_op jit(solution)/shard_map/ppermute | solution.py:244
  25.9 21.7 %collective-permute-start.2 = (bf16[1088,256]{1,0:T(8,128)(2,1)}, bf16[1088,256]{1,0:T(8,128)(2,1)}, u32[]{:S(2)}, u32[]{:S(2)}) collective-permute-start(bf16[1088,256]{1,0:T(8,128)(2,1)} %collective-permute-done.refs_1_), channel_id=1, source_target_pairs={{0,8},{8,16},{16,24},{24,28},{28,20},{20,12},{12,4},{4,0},{1,9},{9... | collective-permute-start | bytes 1671176 | tf_op jit(solution)/shard_map/ppermute | solution.py:242
  27.5 22.3 %collective-permute-start.3 = (bf16[1088,256]{1,0:T(8,128)(2,1)}, bf16[1088,256]{1,0:T(8,128)(2,1)}, u32[]{:S(2)}, u32[]{:S(2)}) collective-permute-start(bf16[1088,256]{1,0:T(8,128)(2,1)} %collective-permute-done.1.refs_2_), channel_id=1, source_target_pairs={{8,0},{16,8},{24,16},{28,24},{20,28},{12,20},{4,12},{0,4},{9,1},{1... | collective-permute-start | bytes 1671176 | tf_op jit(solution)/shard_map/ppermute | solution.py:244
  38.5 21.0 %collective-permute-start.14 = (bf16[1088,256]{1,0:T(8,128)(2,1)}, bf16[1088,256]{1,0:T(8,128)(2,1)}, u32[]{:S(2)}, u32[]{:S(2)}) collective-permute-start(bf16[1088,256]{1,0:T(8,128)(2,1)} %collective-permute-done.12.refs_1_), channel_id=1, source_target_pairs={{0,8},{8,16},{16,24},{24,28},{28,20},{20,12},{12,4},{4,0},{1,9},{9... | collective-permute-start | bytes 1671176 | tf_op jit(solution)/shard_map/ppermute | solution.py:242
  43.7 23.0 %collective-permute-start.15 = (bf16[1088,256]{1,0:T(8,128)(2,1)}, bf16[1088,256]{1,0:T(8,128)(2,1)}, u32[]{:S(2)}, u32[]{:S(2)}) collective-permute-start(bf16[1088,256]{1,0:T(8,128)(2,1)} %copy-done.11), channel_id=1, source_target_pairs={{8,0},{16,8},{24,16},{28,24},{20,28},{12,20},{4,12},{0,4},{9,1},{1... | collective-permute-start | bytes 1671176 | tf_op jit(solution)/shard_map/ppermute | solution.py:244
  49.8 20.9 %collective-permute-start.4 = (bf16[1088,256]{1,0:T(8,128)(2,1)}, bf16[1088,256]{1,0:T(8,128)(2,1)}, u32[]{:S(2)}, u32[]{:S(2)}) collective-permute-start(bf16[1088,256]{1,0:T(8,128)(2,1)} %collective-permute-done.2.refs_3_), channel_id=1, source_target_pairs={{0,8},{8,16},{16,24},{24,28},{28,20},{20,12},{12,4},{4,0},{1,9},{9... | collective-permute-start | bytes 1671176 | tf_op jit(solution)/shard_map/ppermute | solution.py:242
  51.3 20.9 %collective-permute-start.5 = (bf16[1088,256]{1,0:T(8,128)(2,1)}, bf16[1088,256]{1,0:T(8,128)(2,1)}, u32[]{:S(2)}, u32[]{:S(2)}) collective-permute-start(bf16[1088,256]{1,0:T(8,128)(2,1)} %collective-permute-done.3.refs_4_), channel_id=1, source_target_pairs={{8,0},{16,8},{24,16},{28,24},{20,28},{12,20},{4,12},{0,4},{9,1},{1... | collective-permute-start | bytes 1671176 | tf_op jit(solution)/shard_map/ppermute | solution.py:244
  72.2 22.4 %collective-permute-start.8 = (bf16[1088,256]{1,0:T(8,128)(2,1)}, bf16[1088,256]{1,0:T(8,128)(2,1)}, u32[]{:S(2)}, u32[]{:S(2)}) collective-permute-start(bf16[1088,256]{1,0:T(8,128)(2,1)} %get-tuple-element.57.refs_0_), channel_id=1, source_target_pairs={{0,8},{8,16},{16,24},{24,28},{28,20},{20,12},{12,4},{4,0},{1,9},{9... | collective-permute-start | bytes 1671176 | tf_op jit(solution)/shard_map/ppermute | solution.py:242
  73.8 22.8 %collective-permute-start.9 = (bf16[1088,256]{1,0:T(8,128)(2,1)}, bf16[1088,256]{1,0:T(8,128)(2,1)}, u32[]{:S(2)}, u32[]{:S(2)}) collective-permute-start(bf16[1088,256]{1,0:T(8,128)(2,1)} %get-tuple-element.57.refs_0_), channel_id=1, source_target_pairs={{8,0},{16,8},{24,16},{28,24},{20,28},{12,20},{4,12},{0,4},{9,1},{1... | collective-permute-start | bytes 1671176 | tf_op jit(solution)/shard_map/ppermute | solution.py:244
  84.7 23.9 %collective-permute-start.20 = (bf16[1088,256]{1,0:T(8,128)(2,1)}, bf16[1088,256]{1,0:T(8,128)(2,1)}, u32[]{:S(2)}, u32[]{:S(2)}) collective-permute-start(bf16[1088,256]{1,0:T(8,128)(2,1)} %collective-permute-done.18.refs_6_), channel_id=1, source_target_pairs={{8,0},{16,8},{24,16},{28,24},{20,28},{12,20},{4,12},{0,4},{9,1},{1... | collective-permute-start | bytes 1671176 | tf_op jit(solution)/shard_map/ppermute | solution.py:244
  85.4 23.2 %collective-permute-start.19 = (bf16[1088,256]{1,0:T(8,128)(2,1)}, bf16[1088,256]{1,0:T(8,128)(2,1)}, u32[]{:S(2)}, u32[]{:S(2)}) collective-permute-start(bf16[1088,256]{1,0:T(8,128)(2,1)} %collective-permute-done.4.refs_5_), channel_id=1, source_target_pairs={{0,8},{8,16},{16,24},{24,28},{28,20},{20,12},{12,4},{4,0},{1,9},{9... | collective-permute-start | bytes 1671176 | tf_op jit(solution)/shard_map/ppermute | solution.py:242
  96.6 22.1 %collective-permute-start.10 = (bf16[1088,256]{1,0:T(8,128)(2,1)}, bf16[1088,256]{1,0:T(8,128)(2,1)}, u32[]{:S(2)}, u32[]{:S(2)}) collective-permute-start(bf16[1088,256]{1,0:T(8,128)(2,1)} %get-tuple-element.59.refs_0_), channel_id=1, source_target_pairs={{0,8},{8,16},{16,24},{24,28},{28,20},{20,12},{12,4},{4,0},{1,9},{9... | collective-permute-start | bytes 1671176 | tf_op jit(solution)/shard_map/ppermute | solution.py:242
  98.2 22.3 %collective-permute-start.11 = (bf16[1088,256]{1,0:T(8,128)(2,1)}, bf16[1088,256]{1,0:T(8,128)(2,1)}, u32[]{:S(2)}, u32[]{:S(2)}) collective-permute-start(bf16[1088,256]{1,0:T(8,128)(2,1)} %get-tuple-element.59.refs_0_), channel_id=1, source_target_pairs={{8,0},{16,8},{24,16},{28,24},{20,28},{12,20},{4,12},{0,4},{9,1},{1... | collective-permute-start | bytes 1671176 | tf_op jit(solution)/shard_map/ppermute | solution.py:244
  108.6 21.8 %collective-permute-start.26 = (bf16[1088,256]{1,0:T(8,128)(2,1)}, bf16[1088,256]{1,0:T(8,128)(2,1)}, u32[]{:S(2)}, u32[]{:S(2)}) collective-permute-start(bf16[1088,256]{1,0:T(8,128)(2,1)} %collective-permute-done.8.refs_1_), channel_id=1, source_target_pairs={{0,8},{8,16},{16,24},{24,28},{28,20},{20,12},{12,4},{4,0},{1,9},{9... | collective-permute-start | bytes 1671176 | tf_op jit(solution)/shard_map/ppermute | solution.py:242
  110.1 22.3 %collective-permute-start.27 = (bf16[1088,256]{1,0:T(8,128)(2,1)}, bf16[1088,256]{1,0:T(8,128)(2,1)}, u32[]{:S(2)}, u32[]{:S(2)}) collective-permute-start(bf16[1088,256]{1,0:T(8,128)(2,1)} %collective-permute-done.9.refs_2_), channel_id=1, source_target_pairs={{8,0},{16,8},{24,16},{28,24},{20,28},{12,20},{4,12},{0,4},{9,1},{1... | collective-permute-start | bytes 1671176 | tf_op jit(solution)/shard_map/ppermute | solution.py:244
  120.5 21.7 %collective-permute-start.21 = (bf16[1088,256]{1,0:T(8,128)(2,1)}, bf16[1088,256]{1,0:T(8,128)(2,1)S(1)}, u32[]{:S(2)}, u32[]{:S(2)}) collective-permute-start(bf16[1088,256]{1,0:T(8,128)(2,1)} %collective-permute-done.10.refs_1_), channel_id=1, source_target_pairs={{0,8},{8,16},{16,24},{24,28},{28,20},{20,12},{12,4},{4,0},{1,9},{9... | collective-permute-start | bytes 1671176 | tf_op jit(solution)/shard_map/ppermute | solution.py:242
  122.1 22.3 %collective-permute-start.22 = (bf16[1088,256]{1,0:T(8,128)(2,1)}, bf16[1088,256]{1,0:T(8,128)(2,1)}, u32[]{:S(2)}, u32[]{:S(2)}) collective-permute-start(bf16[1088,256]{1,0:T(8,128)(2,1)} %collective-permute-done.11.refs_2_), channel_id=1, source_target_pairs={{8,0},{16,8},{24,16},{28,24},{20,28},{12,20},{4,12},{0,4},{9,1},{1... | collective-permute-start | bytes 1671176 | tf_op jit(solution)/shard_map/ppermute | solution.py:244
  132.5 21.7 %collective-permute-start.28 = (bf16[1088,256]{1,0:T(8,128)(2,1)}, bf16[1088,256]{1,0:T(8,128)(2,1)S(1)}, u32[]{:S(2)}, u32[]{:S(2)}) collective-permute-start(bf16[1088,256]{1,0:T(8,128)(2,1)} %collective-permute-done.26.refs_3_), channel_id=1, source_target_pairs={{0,8},{8,16},{16,24},{24,28},{28,20},{20,12},{12,4},{4,0},{1,9},{9... | collective-permute-start | bytes 1671176 | tf_op jit(solution)/shard_map/ppermute | solution.py:242
  134.0 22.2 %collective-permute-start.29 = (bf16[1088,256]{1,0:T(8,128)(2,1)}, bf16[1088,256]{1,0:T(8,128)(2,1)S(1)}, u32[]{:S(2)}, u32[]{:S(2)}) collective-permute-start(bf16[1088,256]{1,0:T(8,128)(2,1)} %collective-permute-done.27.refs_4_), channel_id=1, source_target_pairs={{8,0},{16,8},{24,16},{28,24},{20,28},{12,20},{4,12},{0,4},{9,1},{1... | collective-permute-start | bytes 1671176 | tf_op jit(solution)/shard_map/ppermute | solution.py:244
  144.4 21.7 %collective-permute-start.24 = (bf16[1088,256]{1,0:T(8,128)(2,1)S(1)}, bf16[1088,256]{1,0:T(8,128)(2,1)S(1)}, u32[]{:S(2)}, u32[]{:S(2)}) collective-permute-start(bf16[1088,256]{1,0:T(8,128)(2,1)S(1)} %collective-permute-done.21.refs_3_), channel_id=1, source_target_pairs={{0,8},{8,16},{16,24},{24,28},{28,20},{20,12},{12,4},{4,0},{1,9},{9... | collective-permute-start | bytes 1671176 | tf_op jit(solution)/shard_map/ppermute | solution.py:242
  146.0 22.2 %collective-permute-start.25 = (bf16[1088,256]{1,0:T(8,128)(2,1)}, bf16[1088,256]{1,0:T(8,128)(2,1)S(1)}, u32[]{:S(2)}, u32[]{:S(2)}) collective-permute-start(bf16[1088,256]{1,0:T(8,128)(2,1)} %collective-permute-done.22.refs_4_), channel_id=1, source_target_pairs={{8,0},{16,8},{24,16},{28,24},{20,28},{12,20},{4,12},{0,4},{9,1},{1... | collective-permute-start | bytes 1671176 | tf_op jit(solution)/shard_map/ppermute | solution.py:244
  157.9 16.2 %collective-permute-start.32 = (bf16[544,256]{1,0:T(8,128)(2,1)S(1)}, bf16[544,256]{1,0:T(8,128)(2,1)S(1)}, u32[]{:S(2)}, u32[]{:S(2)}) collective-permute-start(bf16[544,256]{1,0:T(8,128)(2,1)S(1)} %slice.13), channel_id=1, source_target_pairs={{8,0},{16,8},{24,16},{28,24},{20,28},{12,20},{4,12},{0,4},{9,1},{1... | collective-permute-start | bytes 835592 | tf_op jit(solution)/shard_map/ppermute | solution.py:244
  (39 other events, 737.7 us)
